TPU v7x, 32 devices: a whole 2x2x4 slice. The times are simulated.
32 devices in a mesh: probe: 4 (over y, core), ex: 8 (over z, x).
Axes of the slice: x: 2, y: 2, z: 4, core: 2. Of those that a mesh axis runs over, the one named last changes fastest.
Arguments:
- tokens: bfloat16 [2048, 768], P('ex'), may hold values from -6 to 6
- segment_ids: int32 [2048], replicated, may hold values from 0 to 6, as said below
- qkv_weight: bfloat16 [768, 2304], replicated, may hold values from -0.21875 to 0.21875
- qkv_bias: bfloat16 [2304], replicated, may hold values from -4 to 4
- out_weight: bfloat16 [768, 768], replicated, may hold values from -1.75 to 1.75
- out_bias: bfloat16 [768], replicated, may hold values from -6 to 6
- up_weight: bfloat16 [768, 3072], replicated, may hold values from -0.21875 to 0.21875
- up_bias: bfloat16 [3072], replicated, may hold values from -4 to 4
- down_weight: bfloat16 [3072, 768], replicated, may hold values from -0.109375 to 0.109375
- down_bias: bfloat16 [768], replicated, may hold values from -6 to 6
- norm1_gain: float32 [768], replicated, may hold values from 0.1 to 1.9
- norm1_bias: float32 [768], replicated, may hold values from -4 to 4
- norm2_gain: float32 [768], replicated, may hold values from 0.1 to 1.9
- norm2_bias: float32 [768], replicated, may hold values from -4 to 4
- probe_dirs: bfloat16 [16, 768, 3072], P('probe', 'ex'), may hold values from -0.21875 to 0.21875
- out_grad: bfloat16 [2048, 768], P('ex'), may hold values from -6 to 6
Outputs:
- layer_out: bfloat16 [2048, 768], P('ex')
- input_grad: bfloat16 [2048, 768], P('ex')
- grad_qkv_weight: float32 [768, 2304], P('ex')
- grad_qkv_bias: float32 [2304], replicated
- grad_out_weight: float32 [768, 768], P('ex')
- grad_out_bias: float32 [768], replicated
- grad_up_weight: float32 [768, 3072], P('ex')
- grad_up_bias: float32 [3072], replicated
- grad_down_weight: float32 [3072, 768], P('ex')
- grad_down_bias: float32 [768], replicated
- grad_norm1_gain: float32 [768], replicated
- grad_norm1_bias: float32 [768], replicated
- grad_norm2_gain: float32 [768], replicated
- grad_norm2_bias: float32 [768], replicated
- curvature: float32 [16, 768, 3072], P('probe', 'ex')
- probe_scores: float32 [16, 1], P('probe')
Inputs may be any that keep to these rules, and one draw needn't show every extreme that they name: `segment_ids`: along each row of 2048 tokens the ids never fall; no id occurs in two rows.
All inputs are finite; a program needn't handle non-finite values.
Results may differ from a plain program's by a relative error of at most 0.012.
Values may be sent and summed in bfloat16 or wider, within the bound.
No kernel may reach another device: no remote copies, remote signals or barrier semaphores. Data moves between devices by JAX's collectives and lax.ppermute only.
A program may use at most 256 MiB of HBM per device.

v0:
```python
import functools

import jax
import jax.numpy as jnp
import numpy as np
from jax import lax
from jax.experimental import pallas as pl
from jax.experimental.pallas import tpu as pltpu
from jax.sharding import PartitionSpec as P

HEADS = 12
HEAD_DIM = 64
ROT = 16
SEQ = 2048

BF = jnp.bfloat16
F32 = jnp.float32
eps_norm = 1e-05
masked_score = -1e30
half_root = 0.7071067811865476
gauss_peak = 0.3989422804014327
MB = 1024 * 1024
LANES = 128
LIGHT = pl.CostEstimate(flops=1000, bytes_accessed=1000, transcendentals=0)
BIG = 58


def dot(a, b):
    return jnp.dot(a, b, preferred_element_type=F32)


def dot_nt(a, b):
    return lax.dot_general(a, b, (((1,), (1,)), ((), ())), preferred_element_type=F32)


def dot_tn(a, b):
    return lax.dot_general(a, b, (((0,), (0,)), ((), ())), preferred_element_type=F32)


def spread_of(features):
    center = jnp.mean(features, axis=-1, keepdims=True)
    centred = features - center
    spread = jnp.mean(centred * centred, axis=-1, keepdims=True)
    return centred, lax.rsqrt(spread + eps_norm)


def standardize(features):
    centred, factor = spread_of(features)
    return centred * factor


def norm_input_term(grad, gain_row, unit, factor):
    unit_grad = grad * gain_row
    inner = unit_grad - jnp.mean(unit_grad, -1, keepdims=True)
    return (inner - unit * jnp.mean(unit_grad * unit, -1, keepdims=True)) * factor


def gelu_parts(pre_act):
    below = 0.5 + 0.5 * lax.erf(pre_act * half_root)
    density = gauss_peak * jnp.exp(-0.5 * pre_act * pre_act)
    return below, density


def rotary_tables(count):
    steps = np.arange(ROT // 2, dtype=np.float32) * np.float32(2.0 / ROT)
    inverse = np.power(np.float32(10000.0), -steps).astype(np.float32)
    angles = np.arange(count, dtype=np.float32)[:, None] * inverse[None, :]
    angles = np.concatenate([angles, angles], axis=1)
    cosine = np.ones((count, HEAD_DIM), np.float32)
    sine = np.zeros((count, HEAD_DIM), np.float32)
    cosine[:, :ROT], sine[:, :ROT] = np.cos(angles), np.sin(angles)
    return np.concatenate([cosine, cosine], axis=1), np.concatenate([sine, sine], axis=1)


def params(limit_mb, **more):
    return pltpu.CompilerParams(vmem_limit_bytes=limit_mb * MB, **more)


def shaped(shape, dtype):
    return jax.ShapeDtypeStruct(shape, dtype)


def whole(*shape):
    return pl.BlockSpec(shape, lambda i: (0,) * len(shape))


VMEM = pl.BlockSpec(memory_space=pltpu.VMEM)
SMEM = pl.BlockSpec(memory_space=pltpu.SMEM)
ANY = pl.BlockSpec(memory_space=pl.ANY)


def far(array):
    return pltpu.with_memory_space_constraint(array, pltpu.HBM)


def call(kernel, *, inputs, in_specs, after=(), aliases=None, **more):
    spare = len(after)

    def body(*refs):
        kernel(*refs[: len(inputs)], *refs[len(inputs) + spare :])

    return pl.pallas_call(
        body, in_specs=list(in_specs) + [ANY] * spare, input_output_aliases=aliases or {},
        cost_estimate=LIGHT, **more,
    )(*inputs, *after)


def tie(value, after):
    return call(
        lambda value_ref, out_ref: None,
        inputs=[value],
        after=after,
        aliases={0: 0},
        in_specs=[ANY],
        out_specs=ANY,
        out_shape=shaped(value.shape, value.dtype),
        name="tie",
    )


def pack_kernel(dirs_ref, packed_ref, sems):
    probes = dirs_ref.shape[0]
    blocks, _, width = packed_ref.shape
    part_width = width // probes
    copies = []
    for block in range(blocks):
        for k in range(probes):
            source = dirs_ref.at[k, :, block * part_width : (block + 1) * part_width]
            target = packed_ref.at[block, :, k * part_width : (k + 1) * part_width]
            copies.append(pltpu.make_async_copy(source, target, sems.at[len(copies)]))
    for copy in copies:
        copy.start()
    for copy in copies:
        copy.wait()


def pack(dirs, blocks, rows, after):
    probes, local_rows, hidden_width = dirs.shape
    part_width = hidden_width // blocks
    if rows > 1:
        split = dirs.reshape(probes, local_rows, rows, blocks, part_width // rows)
        return split.transpose(3, 1, 0, 2, 4).reshape(blocks, local_rows, probes * part_width)
    return call(
        pack_kernel,
        inputs=[dirs],
        after=after,
        in_specs=[VMEM],
        out_specs=ANY,
        out_shape=pltpu.HBM((blocks, local_rows, probes * part_width), dirs.dtype),
        scratch_shapes=[pltpu.SemaphoreType.DMA((blocks * probes,))],
        compiler_params=params(8),
        name="pack",
    )


def slices_kernel(place_ref, tokens_ref, grads_ref, both_ref, first_ref, sems):
    count = both_ref.shape[2]
    copies = []
    for part, source in enumerate((tokens_ref, grads_ref)):
        for target, slot, side in ((both_ref, 0, 0), (both_ref, 1, 2), (first_ref, 0, 0)):
            first = jnp.bitwise_xor(place_ref[0], side) * count
            rows = pl.ds(pl.multiple_of(first, count), count)
            copies.append(pltpu.make_async_copy(source.at[rows, :], target.at[slot, part], sems.at[len(copies)]))
    for copy in copies:
        copy.start()
    for copy in copies:
        copy.wait()


def slices_of(probe_place, probe_groups, tokens, grads):
    tok_count, feature_width = tokens.shape
    size = tok_count // probe_groups
    return call(
        slices_kernel,
        inputs=[probe_place[None].astype(jnp.int32), far(tokens), far(grads)],
        in_specs=[SMEM, ANY, ANY],
        out_specs=[VMEM] * 2,
        out_shape=[shaped((count, 2, size, feature_width), BF) for count in (2, 1)],
        scratch_shapes=[pltpu.SemaphoreType.DMA((6,))],
        compiler_params=params(8),
        name="slices",
    )


def stack_kernel(plan, *refs):
    sources, targets = refs[: -len(plan)], refs[-len(plan) :]
    for parts, target in zip(plan, targets):
        number = 0
        for part in parts:
            count = sources[part].shape[0]
            target[number : number + count] = sources[part][...]
            number += count


def stack(sources, plan, after):
    heights = [sum(sources[part].shape[0] for part in parts) for parts in plan]
    return call(
        functools.partial(stack_kernel, plan),
        inputs=sources,
        after=after,
        in_specs=[VMEM] * len(sources),
        out_specs=[VMEM] * len(plan),
        out_shape=[shaped((n,) + sources[parts[0]].shape[1:], BF) for n, parts in zip(heights, plan)],
        compiler_params=params(8),
        name="stack",
    )


def vectors_kernel(groups, blocks, count, *refs):
    sources, vectors_ref, held, sems = refs[:count], refs[count], refs[count + 1 : -1], refs[-1]
    copies = [pltpu.make_async_copy(source, target, sems.at[k]) for k, (source, target) in enumerate(zip(sources, held))]
    for copy in copies:
        copy.start()
    vectors_ref[...] = jnp.zeros_like(vectors_ref)
    for copy in copies:
        copy.wait()
    *plain, first_bias, second_bias, qkv_bias, segments = held
    for number, source in enumerate(plain):
        vectors_ref[number : number + 1, :] = source[...].reshape(1, -1)
    total = first_bias[...].astype(F32) + second_bias[...].astype(F32)
    vectors_ref[len(plain) : len(plain) + 1, :] = total.reshape(1, -1)
    width = qkv_bias.shape[0] // groups
    bias = qkv_bias[...].astype(F32).reshape(1, -1)
    for number in range(groups):
        vectors_ref[8 + number : 9 + number, :width] = bias[:, number * width : (number + 1) * width]
    block = segments.shape[0] // blocks
    for number in range(blocks):
        row = segments[number * block : (number + 1) * block].astype(F32).reshape(1, -1)
        vectors_ref[16 + number : 17 + number, :block] = row


def vectors_of(groups, blocks, *sources):
    return call(
        functools.partial(vectors_kernel, groups, blocks, len(sources)),
        inputs=[far(source) for source in sources],
        in_specs=[ANY] * len(sources),
        out_specs=VMEM,
        out_shape=shaped((16 + blocks, sources[0].shape[0]), F32),
        scratch_shapes=[pltpu.VMEM(source.shape, source.dtype) for source in sources]
        + [pltpu.SemaphoreType.DMA((len(sources),))],
        compiler_params=params(4),
        name="vectors",
    )


def local_kernel(
    tokens_ref, grads_ref, up_ref, up_bias_ref, down_ref, vectors_ref,
    base_ref, rest_ref, small_ref, normed_s, branch_s, back_s,
):
    step = pl.program_id(0)
    gain, shift, out_bias = vectors_ref[2:3, :], vectors_ref[3:4, :], vectors_ref[4:5, :]

    @pl.when(step == 0)
    def _():
        unit = standardize(tokens_ref[...].astype(F32))
        normed_s[...] = (unit * gain + shift).astype(BF)
        branch_s[...] = jnp.zeros_like(branch_s)
        back_s[...] = jnp.zeros_like(back_s)

    bias = up_bias_ref[pl.ds(pl.multiple_of(step * up_ref.shape[1], LANES), up_ref.shape[1])]
    hidden = dot(normed_s[...], up_ref[...]) + bias.astype(F32).reshape(1, -1)
    upstream = dot_nt(grads_ref[...], down_ref[...])
    below, density = gelu_parts(hidden)
    branch_s[...] += dot((hidden * below).astype(BF), down_ref[...])
    hidden_grad = (upstream * (below + hidden * density)).astype(BF)
    back_s[...] += dot_nt(hidden_grad, up_ref[...])

    @pl.when(step == pl.num_programs(0) - 1)
    def _():
        inputs = tokens_ref[...].astype(F32)
        cot = grads_ref[...].astype(F32)
        centred, factor = spread_of(inputs)
        unit = centred * factor
        back = back_s[...]
        base_ref[...] = inputs + branch_s[...] + out_bias
        rest_ref[...] = cot + norm_input_term(back, gain, unit, factor)
        small_ref[...] = jnp.zeros_like(small_ref)
        small_ref[0:1, :] = jnp.sum(cot, axis=0, keepdims=True)
        small_ref[1:2, :] = jnp.sum(back * unit, axis=0, keepdims=True)
        small_ref[2:3, :] = jnp.sum(back, axis=0, keepdims=True)


def local_part(tokens, grads, up_weight, up_bias, down_weight, vectors):
    tok_count, feature_width = tokens.shape
    hidden_width = up_weight.shape[1]
    step = 512
    own = whole(tok_count, feature_width)
    return call(
        local_kernel,
        inputs=[tokens, grads, far(up_weight), up_bias, far(down_weight), vectors],
        grid=(hidden_width // step,),
        in_specs=[
            own, own,
            pl.BlockSpec((feature_width, step), lambda i: (0, i)),
            whole(hidden_width),
            pl.BlockSpec((step, feature_width), lambda i: (i, 0)),
            whole(8, feature_width),
        ],
        out_specs=[own, own, whole(8, feature_width)],
        out_shape=[
            shaped((tok_count, feature_width), F32),
            shaped((tok_count, feature_width), F32),
            shaped((8, feature_width), F32),
        ],
        scratch_shapes=[
            pltpu.VMEM((tok_count, feature_width), BF),
            pltpu.VMEM((tok_count, feature_width), F32),
            pltpu.VMEM((tok_count, feature_width), F32),
        ],
        compiler_params=params(24),
        name="local",
    )


def lanes(rows):
    return lax.broadcasted_iota(jnp.int32, (rows, 2 * HEAD_DIM), 1)


def flipped(tile):
    return pltpu.roll(tile, HEAD_DIM, 1)


def joined(left, right):
    return jnp.where(lanes(left.shape[0]) < HEAD_DIM, left, flipped(right))


def half_turned(tile):
    place_in = lanes(tile.shape[0]) % HEAD_DIM
    low = pltpu.roll(tile, 2 * HEAD_DIM - ROT // 2, 1)
    high = pltpu.roll(tile, ROT // 2, 1)
    return jnp.where(place_in < ROT // 2, -low, jnp.where(place_in < ROT, high, 0.0))


def with_column(tile, lane, column):
    first = column.astype(BF).astype(F32)
    number = lanes(tile.shape[0])
    return jnp.where(number == lane, first, jnp.where(number == lane + 1, column - first, tile))


def heads_joined(values):
    heads = len(values)
    values = [joined(values[k], values[k + 1]) if k + 1 < heads else values[k] for k in range(0, heads, 2)]
    if heads % 2:
        values[-1] = jnp.where(lanes(values[-1].shape[0]) < HEAD_DIM, values[-1], 0.0)
    return jnp.concatenate(values, axis=1)


def attention_kernel(heads, blocks, block, count, plan, *refs):
    sources, refs = refs[:count], refs[count:]
    (
        place_ref, weight_ref, vectors_ref, out_weight_ref, cos_in, sin_in,
        query_out, key_out, value_out, back_out, unit_out, cot_out, attended_out,
        cos_ref, sin_ref, query_s, key_s, value_s, back_s, unit_s, cot_s,
        window_s, weight_s, bias_s, out_weight_s, attended_s, query_code_s, key_code_s, sems,
        *array_refs,
    ) = refs
    place, probe_place = place_ref[0], place_ref[1]
    feature_width = unit_s.shape[1]
    pair = 2 * HEAD_DIM
    scale = HEAD_DIM ** (-0.5)
    gain, shift = vectors_ref[0:1, :], vectors_ref[1:2, :]
    own_rows = pl.ds(pl.multiple_of(place * block, block), block)
    head_width = heads * HEAD_DIM
    mixed_width = 3 * head_width

    first = probe_place * mixed_width // LANES * LANES
    columns = pl.ds(pl.multiple_of(first, LANES), window_s.shape[1])
    rows = pl.ds(pl.multiple_of(probe_place * head_width, HEAD_DIM), head_width)
    moves = [(weight_ref.at[:, columns], window_s), (out_weight_ref.at[rows, :], out_weight_s.at[:head_width, :])]
    moves += [(cos_in, cos_ref), (sin_in, sin_ref)] + list(zip(sources, array_refs))
    copies = [pltpu.make_async_copy(source, target, sems.at[k]) for k, (source, target) in enumerate(moves)]
    for copy in copies:
        copy.start()
    done = len(copies)

    def leave(number, source, target):
        return pltpu.make_async_copy(source, target, sems.at[done + number])

    def rows_of(number):
        return pl.ds(pl.multiple_of(number * block, block), block)

    def side_rows(distance, side, count):
        own = place_ref[1] % (block // count)
        first = jnp.bitwise_xor(place, distance) * block + jnp.bitwise_xor(own, side) * count
        return pl.ds(pl.multiple_of(first, count), count)

    def together(refs, slot, part):
        return jnp.concatenate([array_refs[ref][base + slot, part] for ref, base in refs], axis=0)

    def arrange(source, target):
        for head in range(heads):
            start = head * 3 * HEAD_DIM
            tile = source[:, start : start + pair]
            target[:, head * pair : (head + 1) * pair] = tile.astype(target.dtype)
        values = [source[:, (3 * head + 2) * HEAD_DIM : (3 * head + 3) * HEAD_DIM] for head in range(heads)]
        values.append(jnp.zeros((source.shape[0], -heads * HEAD_DIM % pair), source.dtype))
        target[:, heads * pair :] = jnp.concatenate(values, axis=1).astype(target.dtype)

    number = lanes(block)
    ones = (number >= HEAD_DIM + 16) & (number < HEAD_DIM + 18)
    coded = (number >= HEAD_DIM) & (number < HEAD_DIM + 16)
    for index in range(blocks):
        segment = jnp.broadcast_to(vectors_ref[16 + index : 17 + index, :block], (pair, block)).T
        segment = segment.astype(jnp.int32)
        match = (number == HEAD_DIM + segment // 8) | (number == HEAD_DIM + 8 + segment % 8)
        here = slice(index * block, (index + 1) * block)
        query_code_s[here, :] = jnp.where(coded & ~match, masked_score, 0.0)
        key_code_s[here, :] = jnp.where(match | ones, 1.0, 0.0)

    out_weight_s[head_width:, :] = jnp.zeros((out_weight_s.shape[0] - head_width, feature_width), BF)
    copies[0].wait()
    odd = probe_place * mixed_width % LANES != 0
    window = window_s[...]
    weight = jnp.where(odd, window[:, HEAD_DIM : HEAD_DIM + mixed_width], window[:, :mixed_width])
    arrange(weight, weight_s)
    bias = vectors_ref[pl.ds(8 + probe_place, 1), :mixed_width]
    arrange(jnp.broadcast_to(bias, (8, mixed_width)), bias_s)
    for copy in copies[1:4]:
        copy.wait()

    def project(sides, refs, slot, distance):
        unit = standardize(together(refs, slot, 0).astype(F32))
        normed = (unit * gain + shift).astype(BF)
        low = unit.astype(BF)
        whole_part = dot(normed, weight_s[...]) + bias_s[:1, :]
        cot = together(refs, slot, 1)
        whole_back = dot_nt(cot, out_weight_s[...])
        count = block // len(sides)
        for number, side in enumerate(sides):
            here = slice(number * count, (number + 1) * count)
            rows = side_rows(distance, side, count)
            unit_s[rows, :] = low[here]
            cot_s[rows, :] = cot[here]
            place_heads(rows, whole_part[here], whole_back[here])

    def place_heads(rows, part, back_part):
        cosine, sine = cos_ref[rows, :], sin_ref[rows, :]
        number = lanes(part.shape[0])
        query_code, key_code = query_code_s[rows, :], key_code_s[rows, :]
        value_code = jnp.where((number >= HEAD_DIM) & (number < HEAD_DIM + 2), 1.0, 0.0)
        first = number < HEAD_DIM
        for head in range(heads):
            plain = part[:, head * pair : (head + 1) * pair]
            both = plain * cosine + half_turned(plain) * sine
            query_s[head, rows, :] = jnp.where(first, both * scale, query_code).astype(BF)
            key_s[head, rows, :] = jnp.where(first, flipped(both), key_code).astype(BF)
            start = heads * pair + head // 2 * pair
            tile = part[:, start : start + pair]
            back_tile = back_part[:, head // 2 * pair : head // 2 * pair + pair]
            if head % 2:
                tile, back_tile = flipped(tile), flipped(back_tile)
            value_s[head, rows, :] = jnp.where(first, tile, value_code).astype(BF)
            back_s[head, rows, :] = jnp.where(first, back_tile, 0.0).astype(BF)

    here = set()
    for sides, distances, refs in plan:
        for number in sorted({ref for ref, _ in refs} - here):
            copies[4 + number].wait()
            here.add(number)
        for slot, distance in enumerate(distances):
            project(sides, refs, slot, distance)
    leaving = [leave(0, key_s, key_out), leave(1, value_s, value_out), leave(2, unit_s, unit_out)]
    leaving.append(leave(3, cot_s, cot_out))
    for copy in leaving:
        copy.start()

    square = (block, block)
    lower = lax.broadcasted_iota(jnp.int32, square, 1) <= lax.broadcasted_iota(jnp.int32, square, 0)

    def head_leaving(head):
        pairs = ((query_s, query_out), (back_s, back_out), (attended_s, attended_out))
        return [leave(4 + 3 * head + k, source.at[head], target.at[head]) for k, (source, target) in enumerate(pairs)]

    def attend(head, carry):
        def scores_of(number):
            start, stop = number * block, (number + 1) * block
            query = query_s[head, start:stop, :]
            near = jnp.where(lower, dot_nt(query, key_s[head, start:stop, :]), masked_score)
            return near, dot_nt(query, key_s[head, :start, :]) if number else None

        ahead = scores_of(0)
        for number in range(blocks):
            start, stop = number * block, (number + 1) * block
            near, far = ahead
            if number + 1 < blocks:
                ahead = scores_of(number + 1)
            top = jnp.max(near, axis=-1, keepdims=True)
            if number:
                top = jnp.maximum(top, jnp.max(far, axis=-1, keepdims=True))
            got = dot(jnp.exp(near - top).astype(BF), value_s[head, start:stop, :])
            if number:
                got = got + dot(jnp.exp(far - top).astype(BF), value_s[head, :start, :])
            total = got[:, HEAD_DIM : HEAD_DIM + 1]
            attended = got / total
            attended_s[head, start:stop, :] = attended.astype(BF)
            back = back_s[head, start:stop, :].astype(F32)
            delta = jnp.sum(attended * back, axis=-1, keepdims=True)
            log_total = top + jnp.log(total)
            query = query_s[head, start:stop, :].astype(F32)
            query_s[head, start:stop, :] = with_column(query, HEAD_DIM + 16, -log_total).astype(BF)
            back_s[head, start:stop, :] = with_column(back, HEAD_DIM, -delta).astype(BF)
        for copy in head_leaving(head):
            copy.start()
        return carry

    lax.fori_loop(0, heads, attend, 0)

    for copy in leaving:
        copy.wait()
    for head in range(heads):
        for copy in head_leaving(head):
            copy.wait()


def attention_back_kernel(
    heads, blocks, place_ref, query_in, key_in, value_in, back_in, unit_in, attended_ref, grad_out_ref, weight_ref,
    vectors_ref, cos_in, sin_in,
    keep_ref, send_ref,
    query_s, key_s, value_s, back_s, unit_ref, cos_ref, sin_ref,
    query_grad_s, key_grad_s, both_s, value_grad_s, mixed_s, total_s, small_s, window_s, sems,
):
    place, probe_place = place_ref[0], place_ref[1]
    block, head_width = attended_ref.shape
    feature_width = unit_ref.shape[1]
    mixed_width = 3 * head_width
    scale = HEAD_DIM ** (-0.5)
    first = probe_place * mixed_width // LANES * LANES
    columns = pl.ds(pl.multiple_of(first, LANES), window_s.shape[1])
    others = [(cos_in, cos_ref), (sin_in, sin_ref), (unit_in, unit_ref), (weight_ref.at[:, columns], window_s)]
    others = [pltpu.make_async_copy(source, target, sems.at[k]) for k, (source, target) in enumerate(others)]

    def arriving(head):
        pairs = ((key_in, key_s), (query_in, query_s), (value_in, value_s), (back_in, back_s))
        return [
            pltpu.make_async_copy(source.at[head], target.at[head], sems.at[4 + len(pairs) * head + k])
            for k, (source, target) in enumerate(pairs)
        ]

    for copy in arriving(0) + others[:2]:
        copy.start()
    for head in range(1, heads):
        for copy in arriving(head):
            copy.start()
    for copy in others[2:]:
        copy.start()
    for copy in others[:2]:
        copy.wait()
    square = (block, block)
    upper = lax.broadcasted_iota(jnp.int32, square, 0) <= lax.broadcasted_iota(jnp.int32, square, 1)

    def through(head, carry):
        for copy in arriving(head):
            copy.wait()
        query_grad_s[...] = jnp.zeros_like(query_grad_s)
        for number in range(blocks):
            start, stop = number * block, (number + 1) * block
            key, value = key_s[head, start:stop, :], value_s[head, start:stop, :]
            key_t = key.T
            key_grad = value_grad = None
            for rows, mask in ((slice(start, stop), upper), (slice(stop, blocks * block), None)):
                if rows.start == rows.stop:
                    continue
                query, back = query_s[head, rows, :], back_s[head, rows, :]
                scores = dot_nt(key, query)
                if mask is not None:
                    scores = jnp.where(mask, scores, masked_score)
                probs = jnp.exp(scores)
                score_grad = (probs * dot_nt(value, back)).astype(BF)
                value_term, key_term = dot(probs.astype(BF), back), dot(score_grad, query)
                value_grad = value_term if value_grad is None else value_grad + value_term
                key_grad = key_term if key_grad is None else key_grad + key_term
                query_grad_s[:, rows] += dot(key_t, score_grad)
            key_grad_s[start:stop, :] = key_grad
            value_grad_s[head, start:stop, :] = value_grad.astype(BF)
        for number in range(blocks):
            rows = slice(number * block, (number + 1) * block)
            both = joined(query_grad_s[:, rows].T * scale, key_grad_s[rows, :])
            both = both * cos_ref[rows, :] - half_turned(both * sin_ref[rows, :])
            both_s[head, rows, :] = both.astype(BF)
        return carry

    lax.fori_loop(0, heads, through, 0)

    for number in range(blocks):
        rows = slice(number * block, (number + 1) * block)
        tiles = []
        for head in range(heads):
            both, value = both_s[head, rows, :].astype(F32), value_grad_s[head, rows, :].astype(F32)
            if head % 2 == 0:
                tiles += [both, value]
            else:
                tiles[-1] = joined(tiles[-1], both)
                tiles.append(joined(flipped(both), value))
        if heads % 2:
            tiles[-1] = jnp.where(lanes(block) < HEAD_DIM, tiles[-1], 0.0)
        mixed_s[rows, :] = jnp.concatenate(tiles, axis=1).astype(BF)

    others[2].wait()
    total_s[...] = dot_tn(unit_ref[...], mixed_s[...])
    sums = jnp.sum(mixed_s[...].astype(F32), axis=0, keepdims=True)
    others[3].wait()
    odd = probe_place * mixed_width % LANES != 0
    window = window_s[...]
    weight = jnp.where(odd, window[:, HEAD_DIM : HEAD_DIM + mixed_width], window[:, :mixed_width])

    own_rows = pl.ds(pl.multiple_of(place * block, block), block)
    mixed_own = mixed_s[own_rows, :][:, :mixed_width]
    normed_back = dot_nt(mixed_own, weight).astype(BF)

    local_rows = grad_out_ref.shape[0]
    first = pl.multiple_of(place * local_rows, local_rows)
    pick = lax.broadcasted_iota(jnp.int32, (local_rows, feature_width), 1) == first + lax.broadcasted_iota(
        jnp.int32, (local_rows, feature_width), 0
    )
    gain, shift = [
        jnp.sum(jnp.where(pick, vectors_ref[k : k + 1, :], 0.0), axis=1, keepdims=True) for k in range(2)
    ]
    grad_qkv = (total_s[pl.ds(first, local_rows), :] * gain + sums * shift).astype(BF)

    wide = weight.astype(F32)
    columns = [
        jnp.sum(wide * total_s[:, :mixed_width], axis=1, keepdims=True),
        jnp.sum(wide * sums[:, :mixed_width], axis=1, keepdims=True),
    ]
    number = lax.broadcasted_iota(jnp.int32, (feature_width, LANES), 1)
    columns = jnp.where(number == 0, columns[0], jnp.where(number == 1, columns[1], 0.0)).T
    piece = feature_width // 2
    small_s[...] = jnp.zeros_like(small_s)
    for k in range(2):
        for part in range(2):
            here = slice(part * piece, (part + 1) * piece)
            small_s[2 * k + part : 2 * k + part + 1, :piece] = columns[k : k + 1, here]
    small_s[pl.ds(4 + 2 * probe_place, 1), :piece] = sums[:, :piece]
    small_s[pl.ds(5 + 2 * probe_place, 1), : mixed_width - piece] = sums[:, piece:mixed_width]
    half, few = block // 2, local_rows // 2
    third = head_width
    odd = probe_place % 2 == 1

    def halves(value):
        low, high = value[: value.shape[0] // 2], value[value.shape[0] // 2 :]
        return jnp.where(odd, high, low), jnp.where(odd, low, high)

    attended, grad_out = attended_ref[...], grad_out_ref[...]
    for number, target in enumerate((keep_ref, send_ref)):
        target[...] = jnp.zeros_like(target)
        target[:half, :feature_width] = halves(normed_back)[number]
        target[:half, feature_width:] = halves(attended)[number]
        target[half : half + few, :feature_width] = halves(grad_out)[number]
        part = halves(grad_qkv)[number]
        target[half : half + few, feature_width:] = part[:, :third]
        target[half + few : half + 2 * few, : 2 * third] = part[:, third : 3 * third]
        put_small(target, half + 2 * few, small_s[...])


def put_small(target, first, small):
    width = small.shape[1]
    high = small.astype(BF)
    target[first:, :width] = high
    target[first:, width : 2 * width] = (small - high.astype(F32)).astype(BF)


def get_small(source, first, width):
    return source[first:, :width].astype(F32) + source[first:, width : 2 * width].astype(F32)


def attention(heads, blocks, numbers, pieces, tokens, qkv_weight, vectors, out_weight, after):
    tok_count, feature_width = tokens.shape
    pair = 2 * HEAD_DIM
    head_width = heads * HEAD_DIM
    value_tiles = -(-heads // 2) * pair
    arrays, plan = [], []
    for refs, (sides, distances) in pieces:
        numbered = []
        for array, base in refs:
            if not any(array is other for other in arrays):
                arrays.append(array)
            numbered.append(([array is other for other in arrays].index(True), base))
        plan.append((sides, distances, numbered))
    cos_table, sin_table = rotary_tables(SEQ)
    per_head = shaped((heads, SEQ, pair), BF)
    window = -(-(3 * head_width) // LANES) * LANES
    return call(
        functools.partial(attention_kernel, heads, blocks, tok_count, len(arrays), plan),
        inputs=arrays + [numbers, far(qkv_weight), vectors, far(out_weight), far(jnp.asarray(cos_table)), far(jnp.asarray(sin_table))],
        after=after,
        in_specs=[ANY] * len(arrays) + [SMEM, ANY, VMEM, ANY, ANY, ANY],
        out_specs=[ANY] * 7,
        out_shape=[pltpu.HBM(per_head.shape, BF)] * 4
        + [pltpu.HBM((SEQ, feature_width), BF)] * 2
        + [pltpu.HBM(per_head.shape, BF)],
        scratch_shapes=[pltpu.VMEM((SEQ, pair), F32)] * 2
        + [pltpu.VMEM((heads, SEQ, pair), BF)] * 4
        + [pltpu.VMEM((SEQ, feature_width), BF)] * 2
        + [
            pltpu.VMEM((feature_width, window), BF),
            pltpu.VMEM((feature_width, heads * pair + value_tiles), BF),
            pltpu.VMEM((8, heads * pair + value_tiles), F32),
            pltpu.VMEM((value_tiles, feature_width), BF),
            pltpu.VMEM((heads, SEQ, pair), BF),
            pltpu.VMEM((SEQ, pair), F32),
            pltpu.VMEM((SEQ, pair), F32),
            pltpu.SemaphoreType.DMA((4 + len(arrays) + 4 + 3 * heads,)),
        ]
        + [pltpu.VMEM(array.shape, array.dtype) for array in arrays],
        compiler_params=params(44),
        name="attention",
    )


def attention_back(heads, blocks, numbers, parts, qkv_weight, vectors, after):
    *_, unit, attended, grad_out = parts
    (tok_count, head_width), (local_rows, feature_width) = attended.shape, grad_out.shape
    pair = 2 * HEAD_DIM
    width = -(-(3 * head_width) // LANES) * LANES
    small_rows = -(-(4 + 2 * HEADS // heads) // 16) * 16
    cos_table, sin_table = rotary_tables(SEQ)
    return call(
        functools.partial(attention_back_kernel, heads, blocks),
        inputs=[numbers, *[far(part) for part in parts[:5]], *parts[5:], far(qkv_weight), vectors, far(jnp.asarray(cos_table)), far(jnp.asarray(sin_table))],
        after=after,
        in_specs=[SMEM] + [ANY] * 5 + [VMEM] * 2 + [ANY, VMEM, ANY, ANY],
        out_specs=[VMEM] * 2,
        out_shape=[
            shaped((tok_count // 2 + local_rows + small_rows, feature_width + head_width), BF),
        ] * 2,
        scratch_shapes=[pltpu.VMEM((heads, SEQ, pair), BF)] * 4
        + [pltpu.VMEM((SEQ, feature_width), BF)]
        + [pltpu.VMEM((SEQ, pair), F32)] * 2
        + [
            pltpu.VMEM((pair, SEQ), F32),
            pltpu.VMEM((SEQ, pair), F32),
            pltpu.VMEM((heads, SEQ, pair), BF),
            pltpu.VMEM((heads, SEQ, pair), BF),
            pltpu.VMEM((SEQ, width), BF),
            pltpu.VMEM((feature_width, width), F32),
            pltpu.VMEM((small_rows, feature_width // 2), F32),
            pltpu.VMEM((feature_width, width), BF),
            pltpu.SemaphoreType.DMA((4 + 4 * heads,)),
        ],
        compiler_params=params(42),
        name="attention_back",
    )


def hidden_kernel(sides, first_call, *refs):
    place_ref, count = refs[0], len(sides)
    piece_refs, (up_ref, up_bias_ref, down_ref, vectors_ref) = refs[1 : count + 1], refs[count + 1 : count + 5]
    before_refs = [None, None] if first_call else refs[count + 5 : count + 7]
    normed_ref, turned_ref, curve_ref, grad_ref, active_ref, bias_grad_ref, cot_sum_ref = refs[-7:]
    cot = jnp.concatenate([ref[0, 1] for ref in piece_refs], axis=0)
    unit = standardize(jnp.concatenate([ref[0, 0] for ref in piece_refs], axis=0).astype(F32))
    normed = (unit * vectors_ref[2:3, :] + vectors_ref[3:4, :]).astype(BF)
    normed_ref[...] = normed
    turned_ref[...] = normed.T
    hidden = dot(normed, up_ref[...]) + up_bias_ref[...]
    upstream = dot_nt(cot, down_ref[...])
    below, density = gelu_parts(hidden)
    active = (hidden * below).astype(BF)
    hidden_grad = (upstream * (below + hidden * density)).astype(BF)
    grad_ref[...] = hidden_grad
    curve_ref[...] = upstream * density * (2.0 - hidden * hidden)
    size = active.shape[0] // count
    for number, side in enumerate(sides):
        rows = pl.ds(pl.multiple_of(jnp.bitwise_xor(place_ref[2], side) * size, size), size)
        active_ref[rows, :] = active[number * size : (number + 1) * size]

    @pl.when(pl.program_id(0) == 0)
    def _():
        for before, target in zip(before_refs, (bias_grad_ref, cot_sum_ref)):
            target[...] = jnp.zeros_like(target) if first_call else before[...]

    bias_grad_ref[...] += jnp.sum(hidden_grad.astype(F32), axis=0, keepdims=True)
    cot_sum_ref[...] += jnp.sum(cot.astype(F32), axis=0, keepdims=True)


def hidden_units(places, pieces, sides, first, distances, count, up_part, up_bias_part, down_part, vectors, before):
    arrays = [array for array, _ in pieces]
    feature_width, part_width = arrays[0].shape[3], up_bias_part.shape[1]
    tok_count = sum(array.shape[2] for array in arrays)

    def fixed(*shape):
        return pl.BlockSpec(shape, lambda i, place_ref: (0,) * len(shape))

    def piece(array, slot_of):
        return pl.BlockSpec((1,) + array.shape[1:], lambda i, place_ref: (slot_of(i), 0, 0, 0))

    def block_of(i, place_ref):
        distance = distances[0]
        for number in range(1, len(distances)):
            distance = jnp.where(i == number, distances[number], distance)
        return (jnp.bitwise_xor(place_ref[1], distance), 0)

    units = pl.BlockSpec((tok_count, part_width), lambda i, place_ref: (first + i, 0))
    sums = [fixed(1, part_width), fixed(1, feature_width)]
    inputs = [places, *arrays, far(up_part), up_bias_part, far(down_part), vectors]
    aliases = {}
    if before:
        aliases = {len(inputs) + 2 + k: k for k in range(5)}
        inputs += list(before[5:]) + [far(array) for array in before[:5]]

    def body(*refs):
        spare = 5 if before else 0
        kept = len(refs) - 7 - spare
        hidden_kernel(sides, before is None, *refs[:kept], *refs[kept + spare :])

    return pl.pallas_call(
        body,
        grid_spec=pltpu.PrefetchScalarGridSpec(
            num_scalar_prefetch=1,
            grid=(len(distances),),
            in_specs=[piece(array, slot_of) for array, slot_of in pieces] + [
                pl.BlockSpec((feature_width, part_width), lambda i, place_ref: (0, place_ref[0])),
                fixed(1, part_width),
                pl.BlockSpec((part_width, feature_width), lambda i, place_ref: (place_ref[0], 0)),
                fixed(8, feature_width),
            ] + (sums + [ANY] * 5 if before else []),
            out_specs=[
                pl.BlockSpec((tok_count, feature_width), lambda i, place_ref: (first + i, 0)),
                pl.BlockSpec((feature_width, tok_count), lambda i, place_ref: (0, first + i)),
                units, units, pl.BlockSpec((tok_count, part_width), block_of),
            ] + sums,
        ),
        out_shape=[
            pltpu.HBM((count, feature_width), BF),
            pltpu.HBM((feature_width, count), BF),
            pltpu.HBM((count, part_width), F32),
            pltpu.HBM((count, part_width), BF),
            pltpu.HBM((count, part_width), BF),
            shaped((1, part_width), F32),
            shaped((1, feature_width), F32),
        ],
        input_output_aliases=aliases,
        compiler_params=params(30),
        name="hidden_units",
        cost_estimate=LIGHT,
    )(*inputs)


def curvature_kernel(
    probes, steps, place_ref, dirs_in, local_ref, up_bias_ref, normed_in, turned_in, curve_in, grad_in,
    curvature_out, score_ref,
    curvature_ref, dirs_ref, normed_ref, turned_ref, curve_ref, score_s, spare_s, weighted_s, sems,
):
    feature_width, width = dirs_ref.shape
    part_width = width // probes
    half = part_width // 2
    size = normed_ref.shape[0] // steps

    def moves(step):
        rows = slice(step * size, (step + 1) * size)
        return [
            pltpu.make_async_copy(source.at[rows, :], target, sems.at[3 * step + k])
            for k, (source, target) in enumerate((
                (normed_in, normed_ref.at[rows, :]),
                (curve_in, curve_ref.at[rows, :]),
                (grad_in, weighted_s.at[rows, width:]),
            ))
        ]

    begin = pltpu.make_async_copy(dirs_in, dirs_ref, sems.at[3 * steps])
    last = pltpu.make_async_copy(turned_in, turned_ref, sems.at[3 * steps + 1])
    begin.start()
    for step in range(steps):
        for copy in moves(step):
            copy.start()
    last.start()
    score_s[...] = jnp.zeros_like(score_s)
    begin.wait()
    for step in range(steps):
        for copy in moves(step):
            copy.wait()
        rows = slice(step * size, (step + 1) * size)
        along = dot(normed_ref[rows, :], dirs_ref[...])
        curve, wide = curve_ref[rows, :], weighted_s[rows, width:].astype(F32)
        for k in range(probes):
            columns = slice(k * part_width, (k + 1) * part_width)
            part = along[:, columns]
            weighted_s[rows, columns] = (part * curve).astype(BF)
            score_s[k : k + 1, :] += jnp.sum(part * wide, axis=0, keepdims=True)
    last.wait()
    shape = curvature_ref.shape[:2]
    leaving = []
    for k in range(0, probes, 2):
        columns = slice(k * part_width, (k + 2) * part_width)
        total = dot(turned_ref[...], weighted_s[:, columns])
        curvature_ref[:, :, columns] = total.astype(BF).reshape(shape + (2 * part_width,))
        leaving.append((curvature_ref.at[:, :, columns], curvature_out.at[:, :, columns]))
        pltpu.make_async_copy(*leaving[-1], sems.at[3 * steps + 1 + len(leaving)]).start()
    final = dot(turned_ref[...], weighted_s[:, width:]).astype(BF)
    own = jnp.where(place_ref[0] == 1, final[:, half:], final[:, :half])
    scores = jnp.sum(score_s[...], axis=1, keepdims=True)
    score_ref[...] = jnp.broadcast_to(scores, score_ref.shape)

    spare_s[...] = jnp.zeros_like(spare_s)
    row = 0
    for values in (local_ref[1:2, :], local_ref[2:3, :], up_bias_ref[...]):
        high = values.astype(BF).astype(F32)
        for part in (high, values - high):
            for start in range(0, values.shape[1], HEAD_DIM):
                spare_s[row : row + 1, HEAD_DIM:] = part[:, start : start + HEAD_DIM]
                row += 1
    high = scores.astype(BF).astype(F32)
    for part in (high, scores - high):
        for k in range(probes):
            spare_s[row : row + 1, HEAD_DIM + k : HEAD_DIM + k + 1] = part[k : k + 1, :]
        row += 1
    tail = jnp.concatenate([own[:, LANES:], jnp.zeros((feature_width, HEAD_DIM), BF)], axis=1)
    tail = tail.reshape(shape + (LANES,)) + spare_s[...].astype(BF)[None]
    curvature_ref[:, :, width : width + LANES] = own[:, :LANES].reshape(shape + (LANES,))
    curvature_ref[:, :, width + LANES :] = tail
    leaving.append((curvature_ref.at[:, :, width:], curvature_out.at[:, :, width:]))
    pltpu.make_async_copy(*leaving[-1], sems.at[3 * steps + 1 + len(leaving)]).start()
    for number, move in enumerate(leaving):
        pltpu.make_async_copy(*move, sems.at[3 * steps + 2 + number]).wait()


def curvature_of(blocks, core, probes, units, dirs, local_small, up_bias_grad, after):
    (count, feature_width), part_width = units[0].shape, units[2].shape[1]
    width = probes * part_width
    steps = 4
    local_rows = feature_width // blocks
    out = (blocks, local_rows, width + 2 * LANES)
    return call(
        functools.partial(curvature_kernel, probes, steps),
        inputs=[core[None].astype(jnp.int32), far(dirs), local_small, up_bias_grad] + [far(array) for array in units],
        after=after,
        in_specs=[SMEM, ANY, VMEM, VMEM] + [ANY] * 4,
        out_specs=[ANY, VMEM],
        out_shape=[pltpu.HBM(out, BF), shaped((8, LANES), F32)],
        scratch_shapes=[
            pltpu.VMEM(out, BF),
            pltpu.VMEM((feature_width, width), BF),
            pltpu.VMEM((count, feature_width), BF),
            pltpu.VMEM((feature_width, count), BF),
            pltpu.VMEM((count, part_width), F32),
            pltpu.VMEM((8, part_width), F32),
            pltpu.VMEM((local_rows, LANES), F32),
            pltpu.VMEM((count, width + part_width), BF),
            pltpu.SemaphoreType.DMA((3 * steps + 3 + probes // 2,)),
        ],
        compiler_params=params(52),
        name="curvature",
    )


def weights_kernel(heads, place_ref, active_in, cot_in, attended_in, down_ref, attended_ref, out_ref, *scratch):
    active_s, cot_s, attended_s, joined_s, total_s, sems = scratch
    moves = [(cot_in, cot_s), (active_in, active_s), (attended_in, attended_s)]
    copies = [pltpu.make_async_copy(source, target, sems.at[k]) for k, (source, target) in enumerate(moves)]
    for copy in copies:
        copy.start()
    for copy in copies[:2]:
        copy.wait()
    down_ref[...] = dot_tn(active_s[...], cot_s[...])
    copies[2].wait()
    block = attended_ref.shape[0]
    for number in range(cot_s.shape[0] // block):
        rows = slice(number * block, (number + 1) * block)
        values = [attended_s[head, rows, :].astype(F32) for head in range(heads)]
        joined_s[rows, :] = heads_joined(values).astype(BF)
    own = pl.ds(pl.multiple_of(place_ref[0] * block, block), block)
    attended_ref[...] = joined_s[own, :][:, : attended_ref.shape[1]]
    total_s[...] = dot_tn(joined_s[...], cot_s[...])
    local_rows = out_ref.shape[0]
    rows = pl.ds(pl.multiple_of(place_ref[3], local_rows), local_rows)
    out_ref[...] = jnp.where(place_ref[2] == 1, total_s[rows, :], 0.0).astype(BF)


def weights_back(heads, blocks, numbers, active, cot, attended, after):
    (count, feature_width), part_width, pair = cot.shape, active.shape[1], 2 * HEAD_DIM
    value_tiles = -(-heads // 2) * pair
    return call(
        functools.partial(weights_kernel, heads),
        inputs=[numbers, far(active), far(cot), far(attended)],
        after=after,
        in_specs=[SMEM, ANY, ANY, ANY],
        out_specs=[VMEM] * 3,
        out_shape=[
            shaped((part_width, feature_width), F32),
            shaped((count // blocks, heads * HEAD_DIM), BF),
            shaped((feature_width // blocks, feature_width), BF),
        ],
        scratch_shapes=[
            pltpu.VMEM(active.shape, BF),
            pltpu.VMEM(cot.shape, BF),
            pltpu.VMEM(attended.shape, BF),
            pltpu.VMEM((count, value_tiles), BF),
            pltpu.VMEM((value_tiles, feature_width), F32),
            pltpu.SemaphoreType.DMA((3,)),
        ],
        compiler_params=params(32),
        name="weights_back",
    )


def unpack_kernel(got_in, curvature_out, got_s, curvature_s, sems):
    blocks, _, width = got_s.shape
    probes = curvature_s.shape[0]
    part_width = width // probes

    def arrive(k):
        columns = slice(k * part_width, (k + 1) * part_width)
        return pltpu.make_async_copy(got_in.at[:, :, columns], got_s.at[:, :, columns], sems.at[k])

    def leave(k):
        return pltpu.make_async_copy(curvature_s.at[k], curvature_out.at[k], sems.at[probes + k])

    for k in range(probes):
        arrive(k).start()
    for k in range(probes):
        arrive(k).wait()
        for block in range(blocks):
            part = got_s[block, :, k * part_width : (k + 1) * part_width]
            curvature_s[k, :, block * part_width : (block + 1) * part_width] = part.astype(F32)
        leave(k).start()
    for k in range(probes):
        leave(k).wait()


def unpack(got, probes, part_width, after):
    blocks, local_rows, _ = got.shape
    out = (probes, local_rows, blocks * part_width)
    return call(
        unpack_kernel,
        inputs=[far(got)],
        after=after,
        in_specs=[ANY],
        out_specs=ANY,
        out_shape=pltpu.HBM(out, F32),
        scratch_shapes=[
            pltpu.VMEM((blocks, local_rows, probes * part_width), BF),
            pltpu.VMEM(out, F32),
            pltpu.SemaphoreType.DMA((2 * probes,)),
        ],
        compiler_params=params(24),
        name="unpack",
    )


def peel_kernel(probes, got_ref, up_ref, gain_ref, shift_ref, up_bias_ref, score_ref):
    blocks, _, share = got_ref.shape
    part_width = up_bias_ref.shape[0] // blocks
    tails = []
    for block in range(blocks):
        up_ref[:, block * share : (block + 1) * share] = got_ref[block]
        tails.append(got_ref[block, :, share - LANES :].astype(F32))
    total = tails[0]
    for tail in tails[1:]:
        total = total + tail

    def vector(rows, first, length):
        count = length // HEAD_DIM
        parts = [
            rows[first + k : first + k + 1, HEAD_DIM:] + rows[first + count + k : first + count + k + 1, HEAD_DIM:]
            for k in range(count)
        ]
        return jnp.concatenate(parts, axis=1)

    length = gain_ref.shape[0]
    step = 2 * length // HEAD_DIM
    gain_ref[...] = vector(total, 0, length).reshape(gain_ref.shape)
    shift_ref[...] = vector(total, step, length).reshape(shift_ref.shape)
    biases = [vector(tail, 2 * step, part_width) for tail in tails]
    up_bias_ref[...] = jnp.concatenate(biases, axis=1).reshape(up_bias_ref.shape)
    row = 2 * step + 2 * part_width // HEAD_DIM
    scores = total[row : row + 1, HEAD_DIM : HEAD_DIM + probes] + total[row + 1 : row + 2, HEAD_DIM : HEAD_DIM + probes]
    score_ref[...] = scores.reshape(score_ref.shape)


def peel(got, probes, part_width, after):
    blocks, local_rows, width = got.shape
    share = width - probes * part_width
    feature_width = blocks * local_rows
    vector = shaped((feature_width,), F32)
    return call(
        functools.partial(peel_kernel, probes),
        inputs=[got],
        after=after,
        grid=(1,),
        in_specs=[pl.BlockSpec((blocks, local_rows, share), lambda i: (0, 0, width // share - 1))],
        out_specs=[
            whole(local_rows, blocks * share), whole(feature_width), whole(feature_width),
            whole(blocks * part_width), whole(probes),
        ],
        out_shape=[
            shaped((local_rows, blocks * share), BF),
            vector, vector, shaped((blocks * part_width,), F32), shaped((probes,), F32),
        ],
        compiler_params=params(BIG),
        name="peel",
    )


def spread_kernel(blocks, half, place_ref, mine_ref, got_ref, out_ref):
    odd = place_ref[0] == 1
    stride = mine_ref.shape[1] // blocks
    for block in range(blocks):
        here = slice(block * stride, block * stride + half)
        mine, got = mine_ref[:, here], got_ref[:, here]
        both = jnp.concatenate([jnp.where(odd, got, mine), jnp.where(odd, mine, got)], axis=1)
        out_ref[:, block * 2 * half : (block + 1) * 2 * half] = both.astype(F32)


def spread(core, mine, got, blocks, half, after):
    return call(
        functools.partial(spread_kernel, blocks, half),
        inputs=[core[None].astype(jnp.int32), mine, got],
        after=after,
        in_specs=[SMEM, VMEM, VMEM],
        out_specs=VMEM,
        out_shape=shaped((mine.shape[0], blocks * 2 * half), F32),
        compiler_params=params(12),
        name="spread",
    )


def merge_kernel(feature_width, half, few, place_ref, mine_ref, got_ref, merged_ref):
    odd = place_ref[0] == 1
    third = mine_ref.shape[1] - feature_width

    def ordered(rows, columns):
        mine, got = mine_ref[rows, columns], got_ref[rows, columns]
        return jnp.concatenate([jnp.where(odd, got, mine), jnp.where(odd, mine, got)], axis=1)

    main = slice(0, half + few)
    total = mine_ref[main, :feature_width].astype(F32) + got_ref[main, :feature_width].astype(F32)
    merged_ref[...] = jnp.zeros_like(merged_ref)
    merged_ref[main, :feature_width] = total.astype(BF)
    merged_ref[main, feature_width:] = ordered(main, slice(feature_width, feature_width + third))
    rows = slice(half + few, half + 2 * few)
    merged_ref[rows, : 4 * third] = ordered(rows, slice(0, 2 * third))
    first, width = half + 2 * few, feature_width // 2
    put_small(merged_ref, first, get_small(mine_ref, first, width) + get_small(got_ref, first, width))


def merge(core, mine, got, feature_width, half, few):
    count, width = mine.shape
    return call(
        functools.partial(merge_kernel, feature_width, half, few),
        inputs=[core[None].astype(jnp.int32), mine, got],
        in_specs=[SMEM, VMEM, VMEM],
        out_specs=VMEM,
        out_shape=shaped((count, 2 * width - feature_width), BF),
        compiler_params=params(12),
        name="merge",
    )


def finish_kernel(
    few, place_ref, mine_ref, got_ref, tokens_ref, base_ref, rest_ref, vectors_ref, out_weight_ref,
    final_ref, small_ref,
):
    tok_count, feature_width = tokens_ref.shape
    half = tok_count // 2
    third = (mine_ref.shape[1] - feature_width) // 2
    upper = place_ref[1] == 1
    own = pl.ds(pl.multiple_of(place_ref[0] * half, half), half)

    def ordered(rows, columns):
        mine, got = mine_ref[rows, columns], got_ref[rows, columns]
        return jnp.where(upper, got, mine), jnp.where(upper, mine, got)

    attended = jnp.concatenate(ordered(slice(0, half), slice(feature_width, None)), axis=1)
    layer_out = base_ref[own, :] + dot(attended, out_weight_ref[...])
    main = slice(0, half + few)
    total = mine_ref[main, :feature_width].astype(F32) + got_ref[main, :feature_width].astype(F32)
    centred, factor = spread_of(tokens_ref[own, :].astype(F32))
    term = norm_input_term(total[:half], vectors_ref[0:1, :], centred * factor, factor)
    final_ref[:half, :feature_width] = layer_out.astype(BF)
    final_ref[:half, feature_width:] = (rest_ref[own, :] + term).astype(BF)
    parts = []
    firsts = ordered(slice(half, half + few), slice(feature_width, None))
    others = ordered(slice(half + few, half + 2 * few), slice(0, 4 * third))
    for first, other in zip(firsts, others):
        for core in range(2):
            parts += [first[:, core * third : (core + 1) * third], other[:, 2 * core * third : 2 * (core + 1) * third]]
    grad_qkv = jnp.concatenate(parts, axis=1)
    final_ref[half : half + few, :feature_width] = total[half:].astype(BF)
    final_ref[half : half + few, feature_width:] = grad_qkv[:, :feature_width]
    final_ref[half + few :, :] = grad_qkv[:, feature_width:]
    first, width = half + 2 * few, feature_width // 2
    small_ref[...] = get_small(mine_ref, first, width) + get_small(got_ref, first, width)


def finish(places, mine, got, tokens, base, rest, vectors, out_weight, few):
    tok_count, feature_width = tokens.shape
    half = tok_count // 2
    return call(
        functools.partial(finish_kernel, few),
        inputs=[places, mine, got, tokens, far(base), far(rest), vectors, far(out_weight)],
        in_specs=[SMEM] + [VMEM] * 7,
        out_specs=[VMEM] * 2,
        out_shape=[
            shaped((half + 2 * few, 2 * feature_width), BF),
            shaped((mine.shape[0] - half - 2 * few, feature_width // 2), F32),
        ],
        compiler_params=params(20),
        name="finish",
    )


def join_kernel(
    few, mixed_width, place_ref, mine_ref, got_ref, small_ref, cot_ref,
    layer_out_ref, input_grad_ref, out_ref, qkv_ref, gain_ref, shift_ref, qkv_bias_ref, out_bias_ref, down_bias_ref,
):
    half = layer_out_ref.shape[0] // 2
    feature_width = layer_out_ref.shape[1]
    odd = place_ref[0] == 1
    mine, got = mine_ref[...], got_ref[...]
    for core, side in enumerate((jnp.where(odd, got, mine), jnp.where(odd, mine, got))):
        rows = slice(core * half, (core + 1) * half)
        layer_out_ref[rows, :] = side[:half, :feature_width]
        input_grad_ref[rows, :] = side[:half, feature_width:]
        rows = slice(core * few, (core + 1) * few)
        out_ref[rows, :] = side[half : half + few, :feature_width].astype(F32)
        qkv_ref[rows, :feature_width] = side[half : half + few, feature_width:].astype(F32)
        qkv_ref[rows, feature_width:] = side[half + few :, :].astype(F32)
    small = small_ref[...]

    def rows_of(first, total):
        return jnp.concatenate([small[first : first + 1, :], small[first + 1 : first + 2, :]], axis=1)[:, :total]

    gain_ref[...] = rows_of(0, feature_width).reshape(gain_ref.shape)
    shift_ref[...] = rows_of(2, feature_width).reshape(shift_ref.shape)
    groups = qkv_bias_ref.shape[0] // mixed_width
    bias = [rows_of(4 + 2 * number, mixed_width) for number in range(groups)]
    qkv_bias_ref[...] = jnp.concatenate(bias, axis=1).reshape(qkv_bias_ref.shape)
    for ref in (out_bias_ref, down_bias_ref):
        ref[...] = cot_ref[...].reshape(ref.shape)


def join(core, mine, got, small, cot, tok_count, few, mixed_width):
    feature_width = cot.shape[1]
    vector = shaped((feature_width,), F32)
    return call(
        functools.partial(join_kernel, few, mixed_width),
        inputs=[core[None].astype(jnp.int32), mine, got, small, cot],
        in_specs=[SMEM] + [VMEM] * 4,
        out_specs=[VMEM] * 9,
        out_shape=[shaped((tok_count, feature_width), BF)] * 2
        + [shaped((2 * few, feature_width), F32), shaped((2 * few, 3 * feature_width), F32), vector, vector]
        + [shaped((4 * mixed_width,), F32), vector, vector],
        compiler_params=params(16),
        name="join",
    )


def on_device(
    tokens,
    segment_ids,
    qkv_weight,
    qkv_bias,
    out_weight,
    out_bias,
    up_weight,
    up_bias,
    down_weight,
    down_bias,
    norm1_gain,
    norm1_bias,
    norm2_gain,
    norm2_bias,
    probe_dirs,
    out_grad,
):
    tok_count, feature_width = tokens.shape
    hidden_width = up_weight.shape[1]
    probe_count, local_rows = probe_dirs.shape[:2]
    groups = lax.axis_size("ex")
    probe_groups = lax.axis_size("probe")
    blocks = SEQ // tok_count
    rows = groups // blocks
    ex_place = lax.axis_index("ex")
    place = ex_place % blocks
    row_place = ex_place // blocks
    probe_place = lax.axis_index("probe")
    core, upper = probe_place % 2, probe_place // 2
    heads = HEADS // probe_groups
    head_width = heads * HEAD_DIM
    part_width = hidden_width // blocks
    fine = part_width // rows
    row_groups = None
    if rows > 1:
        row_groups = [[r * blocks + b for b in range(blocks)] for r in range(rows)]
    across = [[r * blocks + b for r in range(rows)] for b in range(blocks)]

    def swap(value, distance):
        return lax.ppermute(value, "ex", [(i, i ^ distance) for i in range(groups)])

    def swap_probe(value, distance):
        return lax.ppermute(value, "probe", [(i, i ^ distance) for i in range(probe_groups)])

    def over_rows(value):
        if rows > 1:
            return lax.psum_scatter(value, "ex", axis_index_groups=across, scatter_dimension=0, tiled=True)
        return value

    def my_part(value, axis):
        shape = value.shape
        split = shape[:axis] + (rows, blocks, fine) + shape[axis + 1 :]
        part = lax.dynamic_index_in_dim(value.reshape(split), place, axis + 1, keepdims=False)
        return part.reshape(shape[:axis] + (part_width,) + shape[axis + 1 :])

    mine, share = slices_of(probe_place, probe_groups, tokens, out_grad)
    aside = swap(mine, 1)
    near, diagonal, distant, farthest = [swap(share, distance) for distance in (2, 3, 4, 6)]

    segments = segment_ids
    if rows > 1:
        segments = lax.dynamic_slice_in_dim(segment_ids, row_place * SEQ, SEQ)
    vectors = vectors_of(
        probe_groups, blocks, norm1_gain, norm1_bias, norm2_gain, norm2_bias, out_bias, down_bias, qkv_bias, segments
    )
    base, rest, local_small = local_part(tokens, out_grad, up_weight, up_bias, down_weight, vectors)

    second, third = stack([near, diagonal, distant, farthest], [(0, 1), (2, 3)], [local_small])
    third_aside, third_over = swap(third, 1), swap_probe(third, 2)
    (quarters,) = stack([mine, aside, third, third_over], [(0, 1, 2, 3)], [])
    swapped = swap_probe(quarters, 1)
    up_bias_part = my_part(up_bias, 0).astype(F32)[None]
    up_part, down_part = up_weight, down_weight
    if rows > 1:
        up_part, down_part = my_part(up_weight, 1), my_part(down_weight, 0)

    def pieces_of(array, other, slots, distances):
        return [
            ([(side, slot) for side in (array, other) for slot in pair], ((0, 2, 1, 3), (distance,)))
            for pair, distance in zip(slots, distances)
        ]

    pieces = pieces_of(quarters, swapped, ((0, 1), (2, 3), (4, 6), (5, 7)), (0, 1, 4, 6))
    slots = [lambda i: jnp.where(i < 2, 2 * i, i + 2), lambda i: jnp.where(i < 2, 2 * i + 1, i + 4)]
    refs = [(array, slot_of) for array in (quarters, swapped) for slot_of in slots]
    unit_place = place if rows == 1 else place * 0
    places = jnp.stack([unit_place, place, probe_place]).astype(jnp.int32)
    fixed = (SEQ, up_part, up_bias_part, down_part, vectors)
    units = hidden_units(places, refs, (0, 2, 1, 3), 0, (0, 1, 4, 6), *fixed, None)
    second_over, third_across = swap_probe(second, 2), swap_probe(third_aside, 2)

    dirs = tie(pack(probe_dirs, blocks, rows, [local_small]), [third_aside, third_over, aside])
    dirs = lax.all_to_all(dirs, "ex", 0, 0, axis_index_groups=row_groups, tiled=True)
    dirs = dirs.reshape(blocks * local_rows, probe_count * part_width)
    if rows > 1:
        dirs = lax.all_gather(dirs, "ex", axis_index_groups=across, tiled=True)

    last = ((second, second_over, (2, 3)), (third_aside, third_across, (5, 7)))
    for number, (array, over, distances) in enumerate(last):
        (quarters,) = stack([array, over], [(0, 1)], [units[5]])
        swapped = swap_probe(quarters, 1)
        pieces += pieces_of(quarters, swapped, ((0, 2), (1, 3)), distances)
        refs = [(side, lambda i, k=k: i + 2 * k) for side in (quarters, swapped) for k in range(2)]
        units = hidden_units(places, refs, (0, 2, 1, 3), 4 + 2 * number, distances, *fixed, units)
    *units, active, grad_up_bias, cot_sum = units

    block_rows = feature_width // blocks
    offset = place * block_rows - probe_place * head_width
    holds = (offset >= 0) & (offset < head_width)
    numbers = jnp.stack([place, probe_place, holds, jnp.where(holds, offset, 0)]).astype(jnp.int32)
    *parts, cot, attended = attention(heads, blocks, numbers, pieces, tokens, qkv_weight, vectors, out_weight, [cot_sum])

    part, scores = curvature_of(
        blocks, core, probe_count, units, dirs, local_small, grad_up_bias, [far(attended)]
    )
    part = over_rows(part.reshape(feature_width, -1)).reshape(blocks, local_rows, -1)
    got = lax.all_to_all(part, "ex", 0, 0, axis_index_groups=row_groups, tiled=True)

    grad_down, attended, grad_out = weights_back(heads, blocks, numbers, active, cot, attended, [scores])
    parts += [attended, grad_out]
    keep, send = attention_back(heads, blocks, numbers, parts, qkv_weight, vectors, [scores])
    half, few = tok_count // 2, block_rows // 2
    merged = merge(core, keep, swap_probe(send, 1), feature_width, half, few)
    final, small = finish(
        jnp.stack([core, upper]).astype(jnp.int32), merged, swap_probe(merged, 2), tokens, base, rest, vectors,
        out_weight, few,
    )
    (
        layer_out, input_grad, grad_out_weight, grad_qkv_weight,
        grad_gain_one, grad_shift_one, grad_qkv_bias, grad_out_bias, grad_down_bias,
    ) = join(core, final, swap_probe(final, 1), small, cot_sum, tok_count, few, 3 * head_width)

    if rows == 1:
        up_half, grad_gain_two, grad_shift_two, grad_up_bias, scores = peel(
            got, probe_count, part_width, [layer_out]
        )
        other_half = swap_probe(up_half, 1)
        curvature = unpack(got, probe_count, part_width, [far(up_half)])
        scores = scores[:, None]
        grad_up_weight = spread(core, up_half, other_half, blocks, part_width // 2, [])
    else:
        start = probe_count * part_width
        units = got[:, :, :start].reshape(blocks, local_rows, probe_count, rows, fine)
        curvature = units.transpose(2, 1, 3, 0, 4).reshape(probe_count, local_rows, hidden_width)
        curvature = curvature.astype(F32)
        up_half = got[:, :, start : start + part_width // 2]
        both = lax.all_gather(up_half, "probe", axis_index_groups=[[0, 1], [2, 3]])
        both = both.transpose(2, 1, 0, 3).reshape(local_rows, blocks, rows, fine)
        grad_up_weight = both.transpose(0, 2, 1, 3).reshape(local_rows, hidden_width).astype(F32)
        grad_down = over_rows(grad_down)

        def over_groups(value):
            value = lax.all_gather(value, "ex", axis_index_groups=row_groups, tiled=True)
            return lax.dynamic_slice_in_dim(over_rows(value), place * local_rows, local_rows, 0)

        grad_qkv_weight, grad_out_weight = over_groups(grad_qkv_weight), over_groups(grad_out_weight)
        grad_gain_one, grad_shift_one, grad_qkv_bias, grad_out_bias, grad_up_bias = lax.psum(
            (grad_gain_one, grad_shift_one, grad_qkv_bias, grad_out_bias, grad_up_bias[0]),
            "ex",
            axis_index_groups=across,
        )
        grad_down_bias = grad_out_bias
        grad_up_bias = lax.all_gather(grad_up_bias, "ex", axis_index_groups=row_groups)
        grad_up_bias = grad_up_bias.reshape(blocks, rows, fine).transpose(1, 0, 2).reshape(-1)
        grad_gain_two, grad_shift_two = lax.psum((local_small[1], local_small[2]), "ex")
        scores = lax.psum(scores[:probe_count, :1], "ex", axis_index_groups=row_groups)
        scores = lax.all_gather(scores, "ex", axis_index_groups=across, axis=1, tiled=True)
    return (
        layer_out,
        input_grad,
        grad_qkv_weight,
        grad_qkv_bias,
        grad_out_weight,
        grad_out_bias,
        grad_up_weight,
        grad_up_bias,
        grad_down,
        grad_down_bias,
        grad_gain_one,
        grad_shift_one,
        grad_gain_two,
        grad_shift_two,
        curvature,
        scores,
    )


def solution(mesh):
    in_specs = (
        P("ex", None),
        P(),
        P(),
        P(),
        P(),
        P(),
        P(),
        P(),
        P(),
        P(),
        P(),
        P(),
        P(),
        P(),
        P("probe", "ex", None),
        P("ex", None),
    )
    out_specs = (
        P("ex", None),
        P("ex", None),
        P("ex", None),
        P(),
        P("ex", None),
        P(),
        P("ex", None),
        P(),
        P("ex", None),
        P(),
        P(),
        P(),
        P(),
        P(),
        P("probe", "ex", None),
        P("probe", None),
    )
    return jax.shard_map(
        on_device, mesh=mesh, in_specs=in_specs, out_specs=out_specs, check_vma=False
    )
```

profile of v0, /device:TPU:1, one launch (start us, length us, event | category | flops | bytes accessed | tf_op | source)
XLA Modules:
  0.0 189.3 jit_solution(14328208232979468532)
XLA Ops:
  0.7 1.2 slices.1
  1.8 2.2 %collective-permute-start.1 = (bf16[1,2,64,768]{3,2,1,0:T(8,128)(2,1)S(1)}, bf16[1,2,64,768]{3,2,1,0:T(8,128)(2,1)S(1)}, u32[]{:S(2)}, u32[]{:S(2)}) collective-permute-start(bf16[1,2,64,768]{3,2,1,0:T(8,128)(2,1)S(1)} %get-tuple-element.75), channel_id=1, source_target_pairs={{0,2},{1,3},{2,0},{3,1},{4,6},{5,7},{6,4},{7,5},{8,10},{9,11},{10,... | collective-permute-start | bytes 589832 | tf_op jit(solution)/shard_map/ppermute | solution.py:1288
  4.0 1.1 collective-permute-start.2
  5.1 2.3 %collective-permute-start.3 = (bf16[1,2,64,768]{3,2,1,0:T(8,128)(2,1)S(1)}, bf16[1,2,64,768]{3,2,1,0:T(8,128)(2,1)S(1)}, u32[]{:S(2)}, u32[]{:S(2)}) collective-permute-start(bf16[1,2,64,768]{3,2,1,0:T(8,128)(2,1)S(1)} %get-tuple-element.75), channel_id=1, source_target_pairs={{0,4},{1,5},{2,6},{3,7},{4,0},{5,1},{6,2},{7,3},{8,12},{9,13},{10,... | collective-permute-start | bytes 589832 | tf_op jit(solution)/shard_map/ppermute | solution.py:1288
  7.4 1.1 collective-permute-start.4
  8.8 1.0 vectors.1.refs_5_.refs_8_.refs_9_.refs_6_
  9.8 1.0 copy-done.4
  10.7 1.0 copy-done.7
  12.4 9.6 %local.1 = (f32[256,768]{1,0:T(8,128)S(1)}, f32[256,768]{1,0:T(8,128)S(1)}, f32[8,768]{1,0:T(8,128)S(1)}) custom-call(bf16[256,768]{1,0:T(8,128)(2,1)S(1)} %copy-done.4, bf16[256,768]{1,0:T(8,128)(2,1)S(1)} %copy-done.7, bf16[768,3072]{1,0:T(8,128)(2,1)} %refs_5_.7, bf16[3072]{0:T(1024)(128)(2,1)S(1)} %copy-done.19, bf16[3072,768]{1,0:T(8,128)(2,1)} %refs_7_.9, ...), custom_call_target="tpu_custom_call" | custom-call | flops 1000 | bytes 1000 | tf_op jit(solution)/shard_map/local/pallas_call | solution.py:102
  22.1 1.2 collective-permute-done.4.refs_3_
  23.3 0.8 stack.45
  24.1 1.2 collective-permute-start.5
  25.3 1.2 collective-permute-start.9
  26.5 1.7 pack.1.refs_0_
  28.3 4.8 %collective-permute-done.5.refs_3_.refs_2_ = bf16[2,2,64,768]{3,2,1,0:T(8,128)(2,1)S(1)} collective-permute-done((bf16[2,2,64,768]{3,2,1,0:T(8,128)(2,1)S(1)}, bf16[2,2,64,768]{3,2,1,0:T(8,128)(2,1)S(1)}, u32[]{:S(2)}, u32[]{:S(2)}) %collective-permute-start.5) | collective-permute-done | bytes 393248 | tf_op jit(solution)/shard_map/ppermute | solution.py:1291
  33.1 1.0 collective-permute-done.9.refs_0_.refs_1_
  34.8 4.7 %all-to-all-start = ((bf16[8,96,1536]{2,1,0:T(8,128)(2,1)}), bf16[8,96,1536]{2,1,0:T(8,128)(2,1)}, u32[]{:S(2)}, u32[]{:S(2)}) async-start(bf16[8,96,1536]{2,1,0:T(8,128)(2,1)} %tie.1), calls=%async_computation | async-start | bytes 4718592 | tf_op jit(solution)/shard_map/all_to_all | solution.py:1341
  39.6 3.2 %collective-permute-start.6 = (bf16[8,2,64,768]{3,2,1,0:T(8,128)(2,1)S(1)}, bf16[8,2,64,768]{3,2,1,0:T(8,128)(2,1)S(1)}, u32[]{:S(2)}, u32[]{:S(2)}) collective-permute-start(bf16[8,2,64,768]{3,2,1,0:T(8,128)(2,1)S(1)} %stack.46.refs_1_.refs_2_.refs_0_), channel_id=1, source_target_pairs={{0,8},{8,0},{16,24},{24,16},{1,9},{9,1},{17,25},{25,17},{2,10},{10... | collective-permute-start | bytes 4718600 | tf_op jit(solution)/shard_map/ppermute | solution.py:1291
  42.8 0.8 collective-permute-start.7
  43.7 2.2 %collective-permute-done.6.refs_3_.refs_4_.refs_1_ = bf16[8,2,64,768]{3,2,1,0:T(8,128)(2,1)S(1)} collective-permute-done((bf16[8,2,64,768]{3,2,1,0:T(8,128)(2,1)S(1)}, bf16[8,2,64,768]{3,2,1,0:T(8,128)(2,1)S(1)}, u32[]{:S(2)}, u32[]{:S(2)}) %collective-permute-start.6) | collective-permute-done | bytes 1572896 | tf_op jit(solution)/shard_map/ppermute | solution.py:1291
  45.9 6.9 %hidden_units.3 = (bf16[2048,768]{1,0:T(8,128)(2,1)}, bf16[768,2048]{1,0:T(8,128)(2,1)}, f32[2048,384]{1,0:T(8,128)}, bf16[2048,384]{1,0:T(8,128)(2,1)}, bf16[20...) custom-call(s32[3]{0:T(128)S(1)} %pad_add_fusion.2.refs_0_, ...), custom_call_target="tpu_custom_call" | custom-call | flops 1000 | bytes 1000 | tf_op jit(solution)/shard_map/hidden_units/pallas_call | solution.py:806
  52.7 1.1 collective-permute-done.7.refs_1_
  53.8 1.2 stack.47.refs_1_.refs_2_
  55.0 0.9 collective-permute-start.8
  56.7 1.2 collective-permute-done.8.refs_3_.refs_4_
  57.8 4.9 %hidden_units.4 = (bf16[2048,768]{1,0:T(8,128)(2,1)}, bf16[768,2048]{1,0:T(8,128)(2,1)}, f32[2048,384]{1,0:T(8,128)}, bf16[2048,384]{1,0:T(8,128)(2,1)}, bf16[20...) custom-call(s32[3]{0:T(128)S(1)} %pad_add_fusion.2.refs_0_, ...), custom_call_target="tpu_custom_call", output_to_operand_aliasing={{0}: (11, {}), {1}: (12, {}), {2}: (13, {}), {3}: (14, {}),... | custom-call | flops 1000 | bytes 1000 | tf_op jit(solution)/shard_map/hidden_units/pallas_call | solution.py:806
  62.7 4.0 %collective-permute-done.10.refs_1_ = bf16[2,2,64,768]{3,2,1,0:T(8,128)(2,1)S(1)} collective-permute-done((bf16[2,2,64,768]{3,2,1,0:T(8,128)(2,1)S(1)}, bf16[2,2,64,768]{3,2,1,0:T(8,128)(2,1)S(1)}, u32[]{:S(2)}, u32[]{:S(2)}) %collective-permute-start.10) | collective-permute-done | bytes 393248 | tf_op jit(solution)/shard_map/ppermute | solution.py:1291
  66.7 0.9 stack.48.refs_1_.refs_2_.refs_4_
  67.6 0.8 collective-permute-start.11
  68.5 2.2 %collective-permute-done.11.refs_3_.refs_4_.refs_5_ = bf16[4,2,64,768]{3,2,1,0:T(8,128)(2,1)} collective-permute-done((bf16[4,2,64,768]{3,2,1,0:T(8,128)(2,1)}, bf16[4,2,64,768]{3,2,1,0:T(8,128)(2,1)}, u32[]{:S(2)}, u32[]{:S(2)}) %collective-permute-start.11) | collective-permute-done | bytes 786464 | tf_op jit(solution)/shard_map/ppermute | solution.py:1291
  70.7 5.3 %hidden_units.5 = (bf16[2048,768]{1,0:T(8,128)(2,1)}, bf16[768,2048]{1,0:T(8,128)(2,1)}, f32[2048,384]{1,0:T(8,128)}, bf16[2048,384]{1,0:T(8,128)(2,1)}, bf16[20...) custom-call(s32[3]{0:T(128)S(1)} %pad_add_fusion.2.refs_0_, ...), custom_call_target="tpu_custom_call", output_to_operand_aliasing={{0}: (11, {}), {1}: (12, {}), {2}: (13, {}), {3}: (14, {}),... | custom-call | flops 1000 | bytes 1000 | tf_op jit(solution)/shard_map/hidden_units/pallas_call | solution.py:806
  76.0 21.5 %attention.1 = (bf16[3,2048,128]{2,1,0:T(8,128)(2,1)}, bf16[3,2048,128]{2,1,0:T(8,128)(2,1)}, bf16[3,2048,128]{2,1,0:T(8,128)(2,1)}, bf16[3,2048,128]{2,1,0:T(8,...) custom-call(bf16[8,2,64,768]{3,2,1,0:T(8,128)(2,1)S(1)} %stack.46.refs_1_.refs_2_.ref, ...), custom_call_target="tpu_custom_call" | custom-call | flops 1000 | bytes 1000 | tf_op jit(solution)/shard_map/attention/pallas_call | solution.py:102
  97.5 15.7 %curvature.1 = (bf16[8,96,1792]{2,1,0:T(8,128)(2,1)}, f32[8,128]{1,0:T(8,128)S(1)}) custom-call(s32[1]{0:T(128)} %bitcast.refs_0_, bf16[768,1536]{1,0:T(8,128)(2,1)} %bitcast.8.refs_1_, f32[8,768]{1,0:T(8,128)S(1)} %get-tuple-element.76.refs_4_.refs_1_.refs_2_, f32[1,384]{1,0:T(1,128)S(1)} %get-tuple-element.102.refs_3_, ...), custom_call_target="tpu_custom_call" | custom-call | flops 1000 | bytes 1000 | tf_op jit(solution)/shard_map/curvature/pallas_call | solution.py:102
  113.3 6.2 %all-to-all-start.1 = ((bf16[8,96,1792]{2,1,0:T(8,128)(2,1)}), bf16[8,96,1792]{2,1,0:T(8,128)(2,1)}, u32[]{:S(2)}, u32[]{:S(2)}) async-start(bf16[8,96,1792]{2,1,0:T(8,128)(2,1)} %get-tuple-element.122), calls=%async_computation.1 | async-start | bytes 5505024 | tf_op jit(solution)/shard_map/all_to_all | solution.py:1365
  119.5 6.2 %weights_back.1 = (f32[384,768]{1,0:T(8,128)}, bf16[256,192]{1,0:T(8,128)(2,1)S(1)}, bf16[96,768]{1,0:T(8,128)(2,1)S(1)}) custom-call(s32[4]{0:T(128)S(1)} %pad_add_fusion.1.refs_6_.refs_0_, bf16[2048,384]{1,0:T(8,128)(2,1)} %get-tuple-element.99.refs_1_, bf16[2048,768]{1,0:T(8,128)(2,1)} %get-tuple-element.100.refs_2_, ...), custom_call_target="tpu_custom_call" | custom-call | flops 1000 | bytes 1000 | tf_op jit(solution)/shard_map/weights_back/pallas_call | solution.py:102
  125.7 30.5 %attention_back.1 = (bf16[240,960]{1,0:T(8,128)(2,1)S(1)}, bf16[240,960]{1,0:T(8,128)(2,1)S(1)}) custom-call(s32[4]{0:T(128)S(1)} %pad_add_fusion.1.refs_6_.refs_0_, bf16[3,2048,128]{2,1,0:T(8,128)(2,1)} %get-tuple-element.94.refs_1_, bf16[3,2048,128]{2,1,0:T(8,128)(2,1)} %get-tuple-element.95.refs_2_, bf16[3,2048,128]{2,1,0:T(8,128)(2,1)} %get-tuple-element.96.refs_3_, ...), custom_call_target="tpu_custom_call" | custom-call | flops 1000 | bytes 1000 | tf_op jit(solution)/shard_map/attention_back/pallas_call | solution.py:102
  156.9 1.5 collective-permute-done.12.refs_2_
  158.7 0.8 collective-permute-start.13
  159.5 12.9 %collective-permute-done.13.refs_2_ = bf16[240,1152]{1,0:T(8,128)(2,1)S(1)} collective-permute-done((bf16[240,1152]{1,0:T(8,128)(2,1)S(1)}, bf16[240,1152]{1,0:T(8,128)(2,1)S(1)}, u32[]{:S(2)}, u32[]{:S(2)}) %collective-permute-start.13) | collective-permute-done | bytes 552992 | tf_op jit(solution)/shard_map/ppermute | solution.py:1291
  172.5 2.2 %finish.1 = (bf16[224,1536]{1,0:T(8,128)(2,1)S(1)}, f32[16,384]{1,0:T(8,128)S(1)}) custom-call(s32[2]{0:T(128)S(1)} %pad_add_fusion.refs_0_, bf16[240,1152]{1,0:T(8,128)(2,1)S(1)} %merge.1.refs_1_, bf16[240,1152]{1,0:T(8,128)(2,1)S(1)} %collective-permute-done.13.refs_2_, bf16[256,768]{1,0:T(8,128)(2,1)S(1)} %copy-done.5, f32[256,768]{1,0:T(8,128)} %copy-done.15, ...), custom_call_target="tpu_custom_call" | custom-call | flops 1000 | bytes 1000 | tf_op jit(solution)/shard_map/finish/pallas_call | solution.py:102
  174.7 1.3 collective-permute-start.14
  176.0 1.8 collective-permute-done.14.refs_2_
  177.8 1.3 join.1
  179.1 2.2 %all-to-all-done.1.refs_0_ = bf16[8,96,1792]{2,1,0:T(8,128)(2,1)} async-done(((bf16[8,96,1792]{2,1,0:T(8,128)(2,1)}), bf16[8,96,1792]{2,1,0:T(8,128)(2,1)}, u32[]{:S(2)}, u32[]{:S(2)}) %all-to-all-start.1) | async-done | bytes 2752544 | tf_op jit(solution)/shard_map/all_to_all | solution.py:1365
  181.2 1.8 peel.1
  183.0 1.5 collective-permute-start.15
  184.5 3.4 %unpack.1 = f32[4,96,3072]{2,1,0:T(8,128)} custom-call(bf16[8,96,1792]{2,1,0:T(8,128)(2,1)} %all-to-all-done.1.refs_0_, bf16[96,2048]{1,0:T(8,128)(2,1)} %get-tuple-element.123.refs_1_), custom_call_target="tpu_custom_call" | custom-call | flops 1000 | bytes 1000 | tf_op jit(solution)/shard_map/unpack/pallas_call | solution.py:102
  187.9 1.2 spread.1
  (57 shorter events, 3.8 us)
Async XLA Ops:
  1.8 20.2 %collective-permute-start.1 = (bf16[1,2,64,768]{3,2,1,0:T(8,128)(2,1)S(1)}, bf16[1,2,64,768]{3,2,1,0:T(8,128)(2,1)S(1)}, u32[]{:S(2)}, u32[]{:S(2)}) collective-permute-start(bf16[1,2,64,768]{3,2,1,0:T(8,128)(2,1)S(1)} %get-tuple-element.75), channel_id=1, source_target_pairs={{0,2},{1,3},{2,0},{3,1},{4,6},{5,7},{6,4},{7,5},{8,10},{9,11},{10,... | collective-permute-start | bytes 589832 | tf_op jit(solution)/shard_map/ppermute | solution.py:1288
  4.0 18.0 %collective-permute-start.2 = (bf16[1,2,64,768]{3,2,1,0:T(8,128)(2,1)S(1)}, bf16[1,2,64,768]{3,2,1,0:T(8,128)(2,1)S(1)}, u32[]{:S(2)}, u32[]{:S(2)}) collective-permute-start(bf16[1,2,64,768]{3,2,1,0:T(8,128)(2,1)S(1)} %get-tuple-element.75), channel_id=1, source_target_pairs={{0,3},{1,2},{2,1},{3,0},{4,7},{5,6},{6,5},{7,4},{8,11},{9,10},{10,... | collective-permute-start | bytes 589832 | tf_op jit(solution)/shard_map/ppermute | solution.py:1288
  5.1 16.9 %collective-permute-start.3 = (bf16[1,2,64,768]{3,2,1,0:T(8,128)(2,1)S(1)}, bf16[1,2,64,768]{3,2,1,0:T(8,128)(2,1)S(1)}, u32[]{:S(2)}, u32[]{:S(2)}) collective-permute-start(bf16[1,2,64,768]{3,2,1,0:T(8,128)(2,1)S(1)} %get-tuple-element.75), channel_id=1, source_target_pairs={{0,4},{1,5},{2,6},{3,7},{4,0},{5,1},{6,2},{7,3},{8,12},{9,13},{10,... | collective-permute-start | bytes 589832 | tf_op jit(solution)/shard_map/ppermute | solution.py:1288
  7.4 15.8 %collective-permute-start.4 = (bf16[1,2,64,768]{3,2,1,0:T(8,128)(2,1)S(1)}, bf16[1,2,64,768]{3,2,1,0:T(8,128)(2,1)S(1)}, u32[]{:S(2)}, u32[]{:S(2)}) collective-permute-start(bf16[1,2,64,768]{3,2,1,0:T(8,128)(2,1)S(1)} %get-tuple-element.75), channel_id=1, source_target_pairs={{0,6},{1,7},{2,4},{3,5},{4,2},{5,3},{6,0},{7,1},{8,14},{9,15},{10,... | collective-permute-start | bytes 589832 | tf_op jit(solution)/shard_map/ppermute | solution.py:1288
  8.5 19.7 %collective-permute-start = (bf16[2,2,64,768]{3,2,1,0:T(8,128)(2,1)S(1)}, bf16[2,2,64,768]{3,2,1,0:T(8,128)(2,1)S(1)}, u32[]{:S(2)}, u32[]{:S(2)}) collective-permute-start(bf16[2,2,64,768]{3,2,1,0:T(8,128)(2,1)S(1)} %get-tuple-element.74.refs_0_), channel_id=1, source_target_pairs={{0,1},{1,0},{2,3},{3,2},{4,5},{5,4},{6,7},{7,6},{8,9},{9,8},{10,11... | collective-permute-start | bytes 1179656 | tf_op jit(solution)/shard_map/ppermute | solution.py:1288
  9.7 1.0 copy-start.4
  10.7 1.0 copy-start.7
  11.7 0.7 copy-start.19
  12.4 14.1 %copy-start.6 = (bf16[4,96,3072]{2,1,0:T(8,128)(2,1)S(1)}, bf16[4,96,3072]{2,1,0:T(8,128)(2,1)}, u32[]{:S(2)}) copy-start(bf16[4,96,3072]{2,1,0:T(8,128)(2,1)} %refs_0_.5) | copy-start | bytes 7077892
  22.0 6.2 %copy-start.15 = (f32[256,768]{1,0:T(8,128)}, f32[256,768]{1,0:T(8,128)S(1)}, u32[]{:S(2)}) copy-start(f32[256,768]{1,0:T(8,128)S(1)} %get-tuple-element.112.refs_4_) | copy-start | bytes 2359300
  22.0 6.2 %copy-start.16 = (f32[256,768]{1,0:T(8,128)}, f32[256,768]{1,0:T(8,128)S(1)}, u32[]{:S(2)}) copy-start(f32[256,768]{1,0:T(8,128)S(1)} %get-tuple-element.113.refs_5_) | copy-start | bytes 2359300
  24.1 4.2 %copy-start.17 = (bf16[2,2,64,768]{3,2,1,0:T(8,128)(2,1)}, bf16[2,2,64,768]{3,2,1,0:T(8,128)(2,1)S(1)}, u32[]{:S(2)}) copy-start(bf16[2,2,64,768]{3,2,1,0:T(8,128)(2,1)S(1)} %get-tuple-element.77.refs_2_) | copy-start | bytes 1179652
  24.1 9.0 %collective-permute-start.5 = (bf16[2,2,64,768]{3,2,1,0:T(8,128)(2,1)S(1)}, bf16[2,2,64,768]{3,2,1,0:T(8,128)(2,1)S(1)}, u32[]{:S(2)}, u32[]{:S(2)}) collective-permute-start(bf16[2,2,64,768]{3,2,1,0:T(8,128)(2,1)S(1)} %get-tuple-element.77.refs_2_), channel_id=1, source_target_pairs={{0,16},{8,24},{16,0},{24,8},{1,17},{9,25},{17,1},{25,9},{2,18},{10... | collective-permute-start | bytes 1179656 | tf_op jit(solution)/shard_map/ppermute | solution.py:1291
  25.3 8.7 %collective-permute-start.9 = (bf16[2,2,64,768]{3,2,1,0:T(8,128)(2,1)S(1)}, bf16[2,2,64,768]{3,2,1,0:T(8,128)(2,1)S(1)}, u32[]{:S(2)}, u32[]{:S(2)}) collective-permute-start(bf16[2,2,64,768]{3,2,1,0:T(8,128)(2,1)S(1)} %get-tuple-element.77.refs_2_), channel_id=1, source_target_pairs={{0,1},{1,0},{2,3},{3,2},{4,5},{5,4},{6,7},{7,6},{8,9},{9,8},{10,11... | collective-permute-start | bytes 1179656 | tf_op jit(solution)/shard_map/ppermute | solution.py:1288
  28.3 5.8 %copy-start.8 = (bf16[2,2,64,768]{3,2,1,0:T(8,128)(2,1)}, bf16[2,2,64,768]{3,2,1,0:T(8,128)(2,1)S(1)}, u32[]{:S(2)}) copy-start(bf16[2,2,64,768]{3,2,1,0:T(8,128)(2,1)S(1)} %collective-permute-done.refs_1_.refs_3_) | copy-start | bytes 1179652
  33.1 1.0 copy-start.10
  34.0 0.7 copy-start.12
  34.8 4.7 %copy-start.9 = (bf16[2,2,64,768]{3,2,1,0:T(8,128)(2,1)S(1)}, bf16[2,2,64,768]{3,2,1,0:T(8,128)(2,1)}, u32[]{:S(2)}) copy-start(bf16[2,2,64,768]{3,2,1,0:T(8,128)(2,1)} %copy-done.8) | copy-start | bytes 1179652
  34.8 4.7 %copy-start.11 = (bf16[2,2,64,768]{3,2,1,0:T(8,128)(2,1)S(1)}, bf16[2,2,64,768]{3,2,1,0:T(8,128)(2,1)}, u32[]{:S(2)}) copy-start(bf16[2,2,64,768]{3,2,1,0:T(8,128)(2,1)} %copy-done.10) | copy-start | bytes 1179652
  34.8 4.7 %copy-start.18 = (bf16[2,2,64,768]{3,2,1,0:T(8,128)(2,1)S(1)}, bf16[2,2,64,768]{3,2,1,0:T(8,128)(2,1)}, u32[]{:S(2)}) copy-start(bf16[2,2,64,768]{3,2,1,0:T(8,128)(2,1)} %copy-done.17) | copy-start | bytes 1179652
  34.8 62.8 %all-to-all-start = ((bf16[8,96,1536]{2,1,0:T(8,128)(2,1)}), bf16[8,96,1536]{2,1,0:T(8,128)(2,1)}, u32[]{:S(2)}, u32[]{:S(2)}) async-start(bf16[8,96,1536]{2,1,0:T(8,128)(2,1)} %tie.1), calls=%async_computation | async-start | bytes 4718592 | tf_op jit(solution)/shard_map/all_to_all | solution.py:1341
  39.5 4.1 %copy-start.20 = (bf16[3072]{0:T(1024)(128)(2,1)S(1)}, bf16[3072]{0:T(1024)(128)(2,1)}, u32[]{:S(2)}) copy-start(bf16[3072]{0:T(1024)(128)(2,1)} %refs_3_.4) | copy-start | bytes 18436
  39.6 6.2 %collective-permute-start.6 = (bf16[8,2,64,768]{3,2,1,0:T(8,128)(2,1)S(1)}, bf16[8,2,64,768]{3,2,1,0:T(8,128)(2,1)S(1)}, u32[]{:S(2)}, u32[]{:S(2)}) collective-permute-start(bf16[8,2,64,768]{3,2,1,0:T(8,128)(2,1)S(1)} %stack.46.refs_1_.refs_2_.refs_0_), channel_id=1, source_target_pairs={{0,8},{8,0},{16,24},{24,16},{1,9},{9,1},{17,25},{25,17},{2,10},{10... | collective-permute-start | bytes 4718600 | tf_op jit(solution)/shard_map/ppermute | solution.py:1291
  42.8 11.0 %collective-permute-start.7 = (bf16[2,2,64,768]{3,2,1,0:T(8,128)(2,1)}, bf16[2,2,64,768]{3,2,1,0:T(8,128)(2,1)}, u32[]{:S(2)}, u32[]{:S(2)}) collective-permute-start(bf16[2,2,64,768]{3,2,1,0:T(8,128)(2,1)} %get-tuple-element.78.refs_0_), channel_id=1, source_target_pairs={{0,16},{8,24},{16,0},{24,8},{1,17},{9,25},{17,1},{25,9},{2,18},{10... | collective-permute-start | bytes 1179656 | tf_op jit(solution)/shard_map/ppermute | solution.py:1291
  43.7 12.2 %copy-start.13 = (bf16[2,2,64,768]{3,2,1,0:T(8,128)(2,1)S(1)}, bf16[2,2,64,768]{3,2,1,0:T(8,128)(2,1)}, u32[]{:S(2)}) copy-start(bf16[2,2,64,768]{3,2,1,0:T(8,128)(2,1)} %copy-done.12) | copy-start | bytes 1179652
  55.0 7.7 %copy-start = (bf16[4,2,64,768]{3,2,1,0:T(8,128)(2,1)}, bf16[4,2,64,768]{3,2,1,0:T(8,128)(2,1)S(1)}, u32[]{:S(2)}) copy-start(bf16[4,2,64,768]{3,2,1,0:T(8,128)(2,1)S(1)} %stack.47.refs_1_.refs_2_) | copy-start | bytes 2359300
  55.0 2.8 %collective-permute-start.8 = (bf16[4,2,64,768]{3,2,1,0:T(8,128)(2,1)S(1)}, bf16[4,2,64,768]{3,2,1,0:T(8,128)(2,1)S(1)}, u32[]{:S(2)}, u32[]{:S(2)}) collective-permute-start(bf16[4,2,64,768]{3,2,1,0:T(8,128)(2,1)S(1)} %stack.47.refs_1_.refs_2_), channel_id=1, source_target_pairs={{0,8},{8,0},{16,24},{24,16},{1,9},{9,1},{17,25},{25,17},{2,10},{10... | collective-permute-start | bytes 2359304 | tf_op jit(solution)/shard_map/ppermute | solution.py:1291
  55.9 10.8 %collective-permute-start.10 = (bf16[2,2,64,768]{3,2,1,0:T(8,128)(2,1)S(1)}, bf16[2,2,64,768]{3,2,1,0:T(8,128)(2,1)S(1)}, u32[]{:S(2)}, u32[]{:S(2)}) collective-permute-start(bf16[2,2,64,768]{3,2,1,0:T(8,128)(2,1)S(1)} %copy-done.13), channel_id=1, source_target_pairs={{0,16},{8,24},{16,0},{24,8},{1,17},{9,25},{17,1},{25,9},{2,18},{10... | collective-permute-start | bytes 1179656 | tf_op jit(solution)/shard_map/ppermute | solution.py:1291
  57.8 4.9 %copy-start.2 = (bf16[4,2,64,768]{3,2,1,0:T(8,128)(2,1)}, bf16[4,2,64,768]{3,2,1,0:T(8,128)(2,1)S(1)}, u32[]{:S(2)}) copy-start(bf16[4,2,64,768]{3,2,1,0:T(8,128)(2,1)S(1)} %collective-permute-done.8.refs_3_.refs_4_) | copy-start | bytes 2359300
  67.6 3.0 %collective-permute-start.11 = (bf16[4,2,64,768]{3,2,1,0:T(8,128)(2,1)}, bf16[4,2,64,768]{3,2,1,0:T(8,128)(2,1)}, u32[]{:S(2)}, u32[]{:S(2)}) collective-permute-start(bf16[4,2,64,768]{3,2,1,0:T(8,128)(2,1)} %stack.48.refs_1_.refs_2_.refs_4_), channel_id=1, source_target_pairs={{0,8},{8,0},{16,24},{24,16},{1,9},{9,1},{17,25},{25,17},{2,10},{10... | collective-permute-start | bytes 2359304 | tf_op jit(solution)/shard_map/ppermute | solution.py:1291
  70.7 5.3 %copy-start.1 = (bf16[4,2,64,768]{3,2,1,0:T(8,128)(2,1)S(1)}, bf16[4,2,64,768]{3,2,1,0:T(8,128)(2,1)}, u32[]{:S(2)}) copy-start(bf16[4,2,64,768]{3,2,1,0:T(8,128)(2,1)} %copy-done) | copy-start | bytes 2359300
  70.7 5.3 %copy-start.3 = (bf16[4,2,64,768]{3,2,1,0:T(8,128)(2,1)S(1)}, bf16[4,2,64,768]{3,2,1,0:T(8,128)(2,1)}, u32[]{:S(2)}) copy-start(bf16[4,2,64,768]{3,2,1,0:T(8,128)(2,1)} %copy-done.2) | copy-start | bytes 2359300
  113.3 68.0 %all-to-all-start.1 = ((bf16[8,96,1792]{2,1,0:T(8,128)(2,1)}), bf16[8,96,1792]{2,1,0:T(8,128)(2,1)}, u32[]{:S(2)}, u32[]{:S(2)}) async-start(bf16[8,96,1792]{2,1,0:T(8,128)(2,1)} %get-tuple-element.122), calls=%async_computation.1 | async-start | bytes 5505024 | tf_op jit(solution)/shard_map/all_to_all | solution.py:1365
  125.7 46.8 %copy-start.5 = (bf16[256,768]{1,0:T(8,128)(2,1)S(1)}, bf16[256,768]{1,0:T(8,128)(2,1)}, u32[]{:S(2)}) copy-start(bf16[256,768]{1,0:T(8,128)(2,1)} %refs_3_.5) | copy-start | bytes 1179652
  156.2 2.2 %collective-permute-start.12 = (bf16[240,960]{1,0:T(8,128)(2,1)S(1)}, bf16[240,960]{1,0:T(8,128)(2,1)S(1)}, u32[]{:S(2)}, u32[]{:S(2)}) collective-permute-start(bf16[240,960]{1,0:T(8,128)(2,1)S(1)} %get-tuple-element.111), channel_id=1, source_target_pairs={{0,8},{8,0},{16,24},{24,16},{1,9},{9,1},{17,25},{25,17},{2,10},{10... | collective-permute-start | bytes 1382408 | tf_op jit(solution)/shard_map/ppermute | solution.py:1291
  158.7 13.8 %collective-permute-start.13 = (bf16[240,1152]{1,0:T(8,128)(2,1)S(1)}, bf16[240,1152]{1,0:T(8,128)(2,1)S(1)}, u32[]{:S(2)}, u32[]{:S(2)}) collective-permute-start(bf16[240,1152]{1,0:T(8,128)(2,1)S(1)} %merge.1.refs_1_), channel_id=1, source_target_pairs={{0,16},{8,24},{16,0},{24,8},{1,17},{9,25},{17,1},{25,9},{2,18},{10... | collective-permute-start | bytes 1658888 | tf_op jit(solution)/shard_map/ppermute | solution.py:1291
  174.7 3.0 %collective-permute-start.14 = (bf16[224,1536]{1,0:T(8,128)(2,1)S(1)}, bf16[224,1536]{1,0:T(8,128)(2,1)S(1)}, u32[]{:S(2)}, u32[]{:S(2)}) collective-permute-start(bf16[224,1536]{1,0:T(8,128)(2,1)S(1)} %get-tuple-element.114.refs_1_), channel_id=1, source_target_pairs={{0,8},{8,0},{16,24},{24,16},{1,9},{9,1},{17,25},{25,17},{2,10},{10... | collective-permute-start | bytes 2064392 | tf_op jit(solution)/shard_map/ppermute | solution.py:1291
  183.0 4.9 %copy-start.14 = (bf16[96,2048]{1,0:T(8,128)(2,1)S(1)}, bf16[96,2048]{1,0:T(8,128)(2,1)}, u32[]{:S(2)}) copy-start(bf16[96,2048]{1,0:T(8,128)(2,1)} %get-tuple-element.123.refs_1_) | copy-start | bytes 1179652
  183.0 4.9 %collective-permute-start.15 = (bf16[96,2048]{1,0:T(8,128)(2,1)}, bf16[96,2048]{1,0:T(8,128)(2,1)S(1)}, u32[]{:S(2)}, u32[]{:S(2)}) collective-permute-start(bf16[96,2048]{1,0:T(8,128)(2,1)} %get-tuple-element.123.refs_1_), channel_id=1, source_target_pairs={{0,8},{8,0},{16,24},{24,16},{1,9},{9,1},{17,25},{25,17},{2,10},{10... | collective-permute-start | bytes 1179656 | tf_op jit(solution)/shard_map/ppermute | solution.py:1291
where the time goes:
time: 193 us; the launch traced here: 189 us
  Pallas kernels  118 us (61%)
  waiting for transfers between devices  35.9 us (19%)
  starting transfers between devices  30.9 us (16%)
  local copies, waits for them, and re-layouts  3.51 us (2%)
    pallas_call x19, Pallas kernels, call(): pl.pallas_call(body, in_specs=list(in_specs) + [ANY] * spare, input_outpu...  101 us
    ppermute x10, waiting for transfers between devices, swap_probe(): lax.ppermute(value, 'probe', [(i, i ^ distance) for i in range(probe_grou...  31.6 us
    pallas_call x3, Pallas kernels, hidden_units(): pl.pallas_call(body, grid_spec=pltpu.PrefetchScalarGridSpec(num_scalar_pr...  17 us
    ppermute x10, starting transfers between devices, swap_probe(): lax.ppermute(value, 'probe', [(i, i ^ distance) for i in range(probe_grou...  11.9 us
    ppermute x6, starting transfers between devices, swap(): return lax.ppermute(value, 'ex', [(i, i ^ distance) for i in range(groups)])  8.13 us
    all_to_all x1, starting transfers between devices, on_device(): lax.all_to_all(part, 'ex', 0, 0, axis_index_groups=row_groups, tiled=True)  6.16 us
    all_to_all x1, starting transfers between devices, on_device(): lax.all_to_all(dirs, 'ex', 0, 0, axis_index_groups=row_groups, tiled=True)  4.68 us
  transfers between devices with their start and end apart: 18, of which 12 were waited for; matrix products, arithmetic and copies ran while one was open for 0% of the time, Pallas kernels for 52%

commit v1 on v0

--- a/solution.py
+++ b/solution.py
@@ -1343,12 +1343,13 @@
     if rows > 1:
         dirs = lax.all_gather(dirs, "ex", axis_index_groups=across, tiled=True)
 
-    last = ((second, second_over, (2, 3)), (third_aside, third_across, (5, 7)))
-    for number, (array, over, distances) in enumerate(last):
-        (quarters,) = stack([array, over], [(0, 1)], [units[5]])
-        swapped = swap_probe(quarters, 1)
-        pieces += pieces_of(quarters, swapped, ((0, 2), (1, 3)), distances)
-        refs = [(side, lambda i, k=k: i + 2 * k) for side in (quarters, swapped) for k in range(2)]
+    (near_quarters,) = stack([second, second_over], [(0, 1)], [units[5]])
+    (far_quarters,) = stack([third_aside, third_across], [(0, 1)], [near_quarters])
+    near_swapped = tie(swap_probe(near_quarters, 1), [far_quarters])
+    last = ((near_quarters, near_swapped, (2, 3)), (far_quarters, swap_probe(far_quarters, 1), (5, 7)))
+    for number, (array, swapped, distances) in enumerate(last):
+        pieces += pieces_of(array, swapped, ((0, 2), (1, 3)), distances)
+        refs = [(side, lambda i, k=k: i + 2 * k) for side in (array, swapped) for k in range(2)]
         units = hidden_units(places, refs, (0, 2, 1, 3), 4 + 2 * number, distances, *fixed, units)
     *units, active, grad_up_bias, cot_sum = units
 

time: 193 us -> 191 us (0.990)
  waiting for transfers between devices: 35.9 us -> 33.3 us
    ppermute x10, waiting for transfers between devices: 31.6 us -> 29.7 us  [swap_probe(): lax.ppermute(value, 'probe', [(i, i ^ distance) for i in range(probe_grou...]
    pallas_call x19 -> x20, Pallas kernels: 101 us -> 101 us  [call(): pl.pallas_call(body, in_specs=list(in_specs) + [ANY] * spare, input_outpu...]
  transfers between devices with their start and end apart: 18 -> 18, of which waited for: 12 -> 10; matrix products, arithmetic and copies ran while one was open for 0% -> 0% of each run, Pallas kernels for 52% -> 52%
where the time goes in v1:
time: 191 us; the launch traced here: 187 us
  Pallas kernels  118 us (62%)
  waiting for transfers between devices  33.3 us (17%)
  starting transfers between devices  32 us (17%)
  local copies, waits for them, and re-layouts  2.76 us (1%)
    pallas_call x20, Pallas kernels, call(): pl.pallas_call(body, in_specs=list(in_specs) + [ANY] * spare, input_outpu...  101 us
    ppermute x10, waiting for transfers between devices, swap_probe(): lax.ppermute(value, 'probe', [(i, i ^ distance) for i in range(probe_grou...  29.7 us
    pallas_call x3, Pallas kernels, hidden_units(): pl.pallas_call(body, grid_spec=pltpu.PrefetchScalarGridSpec(num_scalar_pr...  17.1 us
    ppermute x10, starting transfers between devices, swap_probe(): lax.ppermute(value, 'probe', [(i, i ^ distance) for i in range(probe_grou...  13 us
    ppermute x6, starting transfers between devices, swap(): return lax.ppermute(value, 'ex', [(i, i ^ distance) for i in range(groups)])  8.13 us
    all_to_all x1, starting transfers between devices, on_device(): lax.all_to_all(part, 'ex', 0, 0, axis_index_groups=row_groups, tiled=True)  6.18 us
    all_to_all x1, starting transfers between devices, on_device(): lax.all_to_all(dirs, 'ex', 0, 0, axis_index_groups=row_groups, tiled=True)  4.71 us
  transfers between devices with their start and end apart: 18, of which 10 were waited for; matrix products, arithmetic and copies ran while one was open for 0% of the time, Pallas kernels for 52%

profile of v1, /device:TPU:1, one launch (start us, length us, event | category | flops | bytes accessed | tf_op | source)
XLA Modules:
  0.0 187.4 jit_solution(3547653548304312766)
XLA Ops:
  0.7 1.2 slices.1
  1.8 2.2 %collective-permute-start.1 = (bf16[1,2,64,768]{3,2,1,0:T(8,128)(2,1)S(1)}, bf16[1,2,64,768]{3,2,1,0:T(8,128)(2,1)S(1)}, u32[]{:S(2)}, u32[]{:S(2)}) collective-permute-start(bf16[1,2,64,768]{3,2,1,0:T(8,128)(2,1)S(1)} %get-tuple-element.75), channel_id=1, source_target_pairs={{0,2},{1,3},{2,0},{3,1},{4,6},{5,7},{6,4},{7,5},{8,10},{9,11},{10,... | collective-permute-start | bytes 589832 | tf_op jit(solution)/shard_map/ppermute | solution.py:1288
  4.0 1.1 collective-permute-start.2
  5.1 2.3 %collective-permute-start.3 = (bf16[1,2,64,768]{3,2,1,0:T(8,128)(2,1)S(1)}, bf16[1,2,64,768]{3,2,1,0:T(8,128)(2,1)S(1)}, u32[]{:S(2)}, u32[]{:S(2)}) collective-permute-start(bf16[1,2,64,768]{3,2,1,0:T(8,128)(2,1)S(1)} %get-tuple-element.75), channel_id=1, source_target_pairs={{0,4},{1,5},{2,6},{3,7},{4,0},{5,1},{6,2},{7,3},{8,12},{9,13},{10,... | collective-permute-start | bytes 589832 | tf_op jit(solution)/shard_map/ppermute | solution.py:1288
  7.4 1.1 collective-permute-start.4
  8.8 1.0 vectors.1.refs_5_.refs_8_.refs_9_.refs_6_
  9.8 1.0 copy-done.4
  10.7 1.0 copy-done.7
  11.7 0.7 copy-done.15
  12.4 9.6 %local.1 = (f32[256,768]{1,0:T(8,128)S(1)}, f32[256,768]{1,0:T(8,128)S(1)}, f32[8,768]{1,0:T(8,128)S(1)}) custom-call(bf16[256,768]{1,0:T(8,128)(2,1)S(1)} %copy-done.4, bf16[256,768]{1,0:T(8,128)(2,1)S(1)} %copy-done.7, bf16[768,3072]{1,0:T(8,128)(2,1)} %refs_5_.7, bf16[3072]{0:T(1024)(128)(2,1)S(1)} %copy-done.15, bf16[3072,768]{1,0:T(8,128)(2,1)} %refs_7_.9, ...), custom_call_target="tpu_custom_call" | custom-call | flops 1000 | bytes 1000 | tf_op jit(solution)/shard_map/local/pallas_call | solution.py:102
  22.1 1.2 collective-permute-done.4.refs_3_
  23.3 0.8 stack.45
  24.1 1.2 collective-permute-start.5
  25.3 1.2 collective-permute-start.9
  26.5 1.7 pack.1.refs_0_
  28.2 4.9 %collective-permute-done.5.refs_3_.refs_2_ = bf16[2,2,64,768]{3,2,1,0:T(8,128)(2,1)S(1)} collective-permute-done((bf16[2,2,64,768]{3,2,1,0:T(8,128)(2,1)S(1)}, bf16[2,2,64,768]{3,2,1,0:T(8,128)(2,1)S(1)}, u32[]{:S(2)}, u32[]{:S(2)}) %collective-permute-start.5) | collective-permute-done | bytes 393248 | tf_op jit(solution)/shard_map/ppermute | solution.py:1291
  33.2 1.0 collective-permute-done.9.refs_0_.refs_1_
  34.2 4.7 %all-to-all-start = ((bf16[8,96,1536]{2,1,0:T(8,128)(2,1)}), bf16[8,96,1536]{2,1,0:T(8,128)(2,1)}, u32[]{:S(2)}, u32[]{:S(2)}) async-start(bf16[8,96,1536]{2,1,0:T(8,128)(2,1)} %tie.3), calls=%async_computation | async-start | bytes 4718592 | tf_op jit(solution)/shard_map/all_to_all | solution.py:1341
  39.0 3.2 %collective-permute-start.6 = (bf16[8,2,64,768]{3,2,1,0:T(8,128)(2,1)S(1)}, bf16[8,2,64,768]{3,2,1,0:T(8,128)(2,1)S(1)}, u32[]{:S(2)}, u32[]{:S(2)}) collective-permute-start(bf16[8,2,64,768]{3,2,1,0:T(8,128)(2,1)S(1)} %stack.46.refs_1_.refs_2_.refs_0_), channel_id=1, source_target_pairs={{0,8},{8,0},{16,24},{24,16},{1,9},{9,1},{17,25},{25,17},{2,10},{10... | collective-permute-start | bytes 4718600 | tf_op jit(solution)/shard_map/ppermute | solution.py:1291
  42.8 0.9 collective-permute-start.10
  43.8 1.4 collective-permute-done.6.refs_3_.refs_4_.refs_1_
  45.2 6.9 %hidden_units.3 = (bf16[2048,768]{1,0:T(8,128)(2,1)}, bf16[768,2048]{1,0:T(8,128)(2,1)}, f32[2048,384]{1,0:T(8,128)}, bf16[2048,384]{1,0:T(8,128)(2,1)}, bf16[20...) custom-call(s32[3]{0:T(128)S(1)} %pad_add_fusion.2.refs_0_, ...), custom_call_target="tpu_custom_call" | custom-call | flops 1000 | bytes 1000 | tf_op jit(solution)/shard_map/hidden_units/pallas_call | solution.py:806
  52.1 1.1 collective-permute-done.7.refs_1_
  53.2 1.2 stack.47.refs_2_.refs_1_
  54.4 1.4 collective-permute-start.8
  55.7 5.9 %collective-permute-done.10.refs_1_ = bf16[2,2,64,768]{3,2,1,0:T(8,128)(2,1)} collective-permute-done((bf16[2,2,64,768]{3,2,1,0:T(8,128)(2,1)}, bf16[2,2,64,768]{3,2,1,0:T(8,128)(2,1)}, u32[]{:S(2)}, u32[]{:S(2)}) %collective-permute-start.10) | collective-permute-done | bytes 393248 | tf_op jit(solution)/shard_map/ppermute | solution.py:1291
  61.6 1.2 stack.48.refs_1_.refs_2_.refs_4_
  62.8 0.9 collective-permute-start.11
  63.8 5.1 %hidden_units.4 = (bf16[2048,768]{1,0:T(8,128)(2,1)}, bf16[768,2048]{1,0:T(8,128)(2,1)}, f32[2048,384]{1,0:T(8,128)}, bf16[2048,384]{1,0:T(8,128)(2,1)}, bf16[20...) custom-call(s32[3]{0:T(128)S(1)} %pad_add_fusion.2.refs_0_, ...), custom_call_target="tpu_custom_call", output_to_operand_aliasing={{0}: (11, {}), {1}: (12, {}), {2}: (13, {}), {3}: (14, {}),... | custom-call | flops 1000 | bytes 1000 | tf_op jit(solution)/shard_map/hidden_units/pallas_call | solution.py:806
  69.0 5.1 %hidden_units.5 = (bf16[2048,768]{1,0:T(8,128)(2,1)}, bf16[768,2048]{1,0:T(8,128)(2,1)}, f32[2048,384]{1,0:T(8,128)}, bf16[2048,384]{1,0:T(8,128)(2,1)}, bf16[20...) custom-call(s32[3]{0:T(128)S(1)} %pad_add_fusion.2.refs_0_, ...), custom_call_target="tpu_custom_call", output_to_operand_aliasing={{0}: (11, {}), {1}: (12, {}), {2}: (13, {}), {3}: (14, {}),... | custom-call | flops 1000 | bytes 1000 | tf_op jit(solution)/shard_map/hidden_units/pallas_call | solution.py:806
  74.1 21.5 %attention.1 = (bf16[3,2048,128]{2,1,0:T(8,128)(2,1)}, bf16[3,2048,128]{2,1,0:T(8,128)(2,1)}, bf16[3,2048,128]{2,1,0:T(8,128)(2,1)}, bf16[3,2048,128]{2,1,0:T(8,...) custom-call(bf16[8,2,64,768]{3,2,1,0:T(8,128)(2,1)S(1)} %stack.46.refs_1_.refs_2_.ref, ...), custom_call_target="tpu_custom_call" | custom-call | flops 1000 | bytes 1000 | tf_op jit(solution)/shard_map/attention/pallas_call | solution.py:102
  95.6 15.7 %curvature.1 = (bf16[8,96,1792]{2,1,0:T(8,128)(2,1)}, f32[8,128]{1,0:T(8,128)S(1)}) custom-call(s32[1]{0:T(128)} %bitcast.refs_0_, bf16[768,1536]{1,0:T(8,128)(2,1)} %bitcast.8.refs_1_, f32[8,768]{1,0:T(8,128)S(1)} %get-tuple-element.76.refs_4_.refs_1_.refs_2_, f32[1,384]{1,0:T(1,128)S(1)} %get-tuple-element.102.refs_3_, ...), custom_call_target="tpu_custom_call" | custom-call | flops 1000 | bytes 1000 | tf_op jit(solution)/shard_map/curvature/pallas_call | solution.py:102
  111.3 6.2 %all-to-all-start.1 = ((bf16[8,96,1792]{2,1,0:T(8,128)(2,1)}), bf16[8,96,1792]{2,1,0:T(8,128)(2,1)}, u32[]{:S(2)}, u32[]{:S(2)}) async-start(bf16[8,96,1792]{2,1,0:T(8,128)(2,1)} %get-tuple-element.122), calls=%async_computation.1 | async-start | bytes 5505024 | tf_op jit(solution)/shard_map/all_to_all | solution.py:1366
  117.5 6.2 %weights_back.1 = (f32[384,768]{1,0:T(8,128)}, bf16[256,192]{1,0:T(8,128)(2,1)S(1)}, bf16[96,768]{1,0:T(8,128)(2,1)S(1)}) custom-call(s32[4]{0:T(128)S(1)} %pad_add_fusion.1.refs_6_.refs_0_, bf16[2048,384]{1,0:T(8,128)(2,1)} %get-tuple-element.99.refs_1_, bf16[2048,768]{1,0:T(8,128)(2,1)} %get-tuple-element.100.refs_2_, ...), custom_call_target="tpu_custom_call" | custom-call | flops 1000 | bytes 1000 | tf_op jit(solution)/shard_map/weights_back/pallas_call | solution.py:102
  123.8 30.5 %attention_back.1 = (bf16[240,960]{1,0:T(8,128)(2,1)S(1)}, bf16[240,960]{1,0:T(8,128)(2,1)S(1)}) custom-call(s32[4]{0:T(128)S(1)} %pad_add_fusion.1.refs_6_.refs_0_, bf16[3,2048,128]{2,1,0:T(8,128)(2,1)} %get-tuple-element.94.refs_1_, bf16[3,2048,128]{2,1,0:T(8,128)(2,1)} %get-tuple-element.95.refs_2_, bf16[3,2048,128]{2,1,0:T(8,128)(2,1)} %get-tuple-element.96.refs_3_, ...), custom_call_target="tpu_custom_call" | custom-call | flops 1000 | bytes 1000 | tf_op jit(solution)/shard_map/attention_back/pallas_call | solution.py:102
  154.3 1.0 collective-permute-start.12
  155.3 1.5 collective-permute-done.12.refs_2_
  157.0 0.7 collective-permute-start.13
  157.8 13.1 %collective-permute-done.13.refs_2_ = bf16[240,1152]{1,0:T(8,128)(2,1)S(1)} collective-permute-done((bf16[240,1152]{1,0:T(8,128)(2,1)S(1)}, bf16[240,1152]{1,0:T(8,128)(2,1)S(1)}, u32[]{:S(2)}, u32[]{:S(2)}) %collective-permute-start.13) | collective-permute-done | bytes 552992 | tf_op jit(solution)/shard_map/ppermute | solution.py:1291
  170.9 2.2 %finish.1 = (bf16[224,1536]{1,0:T(8,128)(2,1)S(1)}, f32[16,384]{1,0:T(8,128)S(1)}) custom-call(s32[2]{0:T(128)S(1)} %pad_add_fusion.refs_0_, bf16[240,1152]{1,0:T(8,128)(2,1)S(1)} %merge.1.refs_1_, bf16[240,1152]{1,0:T(8,128)(2,1)S(1)} %collective-permute-done.13.refs_2_, bf16[256,768]{1,0:T(8,128)(2,1)S(1)} %copy-done.5, f32[256,768]{1,0:T(8,128)} %copy-done.13, ...), custom_call_target="tpu_custom_call" | custom-call | flops 1000 | bytes 1000 | tf_op jit(solution)/shard_map/finish/pallas_call | solution.py:102
  173.1 1.3 collective-permute-start.14
  174.4 1.8 collective-permute-done.14.refs_2_
  176.1 1.3 join.1
  177.4 1.5 all-to-all-done.1.refs_0_
  178.9 1.8 peel.1
  180.7 1.8 collective-permute-start.15
  182.6 3.4 %unpack.1 = f32[4,96,3072]{2,1,0:T(8,128)} custom-call(bf16[8,96,1792]{2,1,0:T(8,128)(2,1)} %all-to-all-done.1.refs_0_, bf16[96,2048]{1,0:T(8,128)(2,1)} %get-tuple-element.123.refs_1_), custom_call_target="tpu_custom_call" | custom-call | flops 1000 | bytes 1000 | tf_op jit(solution)/shard_map/unpack/pallas_call | solution.py:102
  186.0 1.2 spread.1
  (50 shorter events, 1.6 us)
Async XLA Ops:
  1.8 20.2 %collective-permute-start.1 = (bf16[1,2,64,768]{3,2,1,0:T(8,128)(2,1)S(1)}, bf16[1,2,64,768]{3,2,1,0:T(8,128)(2,1)S(1)}, u32[]{:S(2)}, u32[]{:S(2)}) collective-permute-start(bf16[1,2,64,768]{3,2,1,0:T(8,128)(2,1)S(1)} %get-tuple-element.75), channel_id=1, source_target_pairs={{0,2},{1,3},{2,0},{3,1},{4,6},{5,7},{6,4},{7,5},{8,10},{9,11},{10,... | collective-permute-start | bytes 589832 | tf_op jit(solution)/shard_map/ppermute | solution.py:1288
  4.0 18.0 %collective-permute-start.2 = (bf16[1,2,64,768]{3,2,1,0:T(8,128)(2,1)S(1)}, bf16[1,2,64,768]{3,2,1,0:T(8,128)(2,1)S(1)}, u32[]{:S(2)}, u32[]{:S(2)}) collective-permute-start(bf16[1,2,64,768]{3,2,1,0:T(8,128)(2,1)S(1)} %get-tuple-element.75), channel_id=1, source_target_pairs={{0,3},{1,2},{2,1},{3,0},{4,7},{5,6},{6,5},{7,4},{8,11},{9,10},{10,... | collective-permute-start | bytes 589832 | tf_op jit(solution)/shard_map/ppermute | solution.py:1288
  5.1 16.9 %collective-permute-start.3 = (bf16[1,2,64,768]{3,2,1,0:T(8,128)(2,1)S(1)}, bf16[1,2,64,768]{3,2,1,0:T(8,128)(2,1)S(1)}, u32[]{:S(2)}, u32[]{:S(2)}) collective-permute-start(bf16[1,2,64,768]{3,2,1,0:T(8,128)(2,1)S(1)} %get-tuple-element.75), channel_id=1, source_target_pairs={{0,4},{1,5},{2,6},{3,7},{4,0},{5,1},{6,2},{7,3},{8,12},{9,13},{10,... | collective-permute-start | bytes 589832 | tf_op jit(solution)/shard_map/ppermute | solution.py:1288
  7.4 15.8 %collective-permute-start.4 = (bf16[1,2,64,768]{3,2,1,0:T(8,128)(2,1)S(1)}, bf16[1,2,64,768]{3,2,1,0:T(8,128)(2,1)S(1)}, u32[]{:S(2)}, u32[]{:S(2)}) collective-permute-start(bf16[1,2,64,768]{3,2,1,0:T(8,128)(2,1)S(1)} %get-tuple-element.75), channel_id=1, source_target_pairs={{0,6},{1,7},{2,4},{3,5},{4,2},{5,3},{6,0},{7,1},{8,14},{9,15},{10,... | collective-permute-start | bytes 589832 | tf_op jit(solution)/shard_map/ppermute | solution.py:1288
  8.5 19.7 %collective-permute-start = (bf16[2,2,64,768]{3,2,1,0:T(8,128)(2,1)S(1)}, bf16[2,2,64,768]{3,2,1,0:T(8,128)(2,1)S(1)}, u32[]{:S(2)}, u32[]{:S(2)}) collective-permute-start(bf16[2,2,64,768]{3,2,1,0:T(8,128)(2,1)S(1)} %get-tuple-element.74.refs_0_), channel_id=1, source_target_pairs={{0,1},{1,0},{2,3},{3,2},{4,5},{5,4},{6,7},{7,6},{8,9},{9,8},{10,11... | collective-permute-start | bytes 1179656 | tf_op jit(solution)/shard_map/ppermute | solution.py:1288
  9.7 1.0 copy-start.4
  10.7 1.0 copy-start.7
  11.7 0.7 copy-start.15
  12.4 14.1 %copy-start.6 = (bf16[4,96,3072]{2,1,0:T(8,128)(2,1)S(1)}, bf16[4,96,3072]{2,1,0:T(8,128)(2,1)}, u32[]{:S(2)}) copy-start(bf16[4,96,3072]{2,1,0:T(8,128)(2,1)} %refs_0_.5) | copy-start | bytes 7077892
  22.0 6.2 %copy-start.13 = (f32[256,768]{1,0:T(8,128)}, f32[256,768]{1,0:T(8,128)S(1)}, u32[]{:S(2)}) copy-start(f32[256,768]{1,0:T(8,128)S(1)} %get-tuple-element.112.refs_4_) | copy-start | bytes 2359300
  22.0 6.2 %copy-start.14 = (f32[256,768]{1,0:T(8,128)}, f32[256,768]{1,0:T(8,128)S(1)}, u32[]{:S(2)}) copy-start(f32[256,768]{1,0:T(8,128)S(1)} %get-tuple-element.113.refs_5_) | copy-start | bytes 2359300
  24.1 9.1 %collective-permute-start.5 = (bf16[2,2,64,768]{3,2,1,0:T(8,128)(2,1)S(1)}, bf16[2,2,64,768]{3,2,1,0:T(8,128)(2,1)S(1)}, u32[]{:S(2)}, u32[]{:S(2)}) collective-permute-start(bf16[2,2,64,768]{3,2,1,0:T(8,128)(2,1)S(1)} %get-tuple-element.77.refs_2_), channel_id=1, source_target_pairs={{0,16},{8,24},{16,0},{24,8},{1,17},{9,25},{17,1},{25,9},{2,18},{10... | collective-permute-start | bytes 1179656 | tf_op jit(solution)/shard_map/ppermute | solution.py:1291
  25.3 8.8 %collective-permute-start.9 = (bf16[2,2,64,768]{3,2,1,0:T(8,128)(2,1)S(1)}, bf16[2,2,64,768]{3,2,1,0:T(8,128)(2,1)}, u32[]{:S(2)}, u32[]{:S(2)}) collective-permute-start(bf16[2,2,64,768]{3,2,1,0:T(8,128)(2,1)S(1)} %get-tuple-element.77.refs_2_), channel_id=1, source_target_pairs={{0,1},{1,0},{2,3},{3,2},{4,5},{5,4},{6,7},{7,6},{8,9},{9,8},{10,11... | collective-permute-start | bytes 1179656 | tf_op jit(solution)/shard_map/ppermute | solution.py:1288
  28.2 5.9 %copy-start.8 = (bf16[2,2,64,768]{3,2,1,0:T(8,128)(2,1)}, bf16[2,2,64,768]{3,2,1,0:T(8,128)(2,1)S(1)}, u32[]{:S(2)}) copy-start(bf16[2,2,64,768]{3,2,1,0:T(8,128)(2,1)S(1)} %collective-permute-done.refs_1_.refs_3_) | copy-start | bytes 1179652
  33.2 1.0 copy-start.10
  34.1 4.7 %copy-start.9 = (bf16[2,2,64,768]{3,2,1,0:T(8,128)(2,1)S(1)}, bf16[2,2,64,768]{3,2,1,0:T(8,128)(2,1)}, u32[]{:S(2)}) copy-start(bf16[2,2,64,768]{3,2,1,0:T(8,128)(2,1)} %copy-done.8) | copy-start | bytes 1179652
  34.1 4.7 %copy-start.11 = (bf16[2,2,64,768]{3,2,1,0:T(8,128)(2,1)S(1)}, bf16[2,2,64,768]{3,2,1,0:T(8,128)(2,1)}, u32[]{:S(2)}) copy-start(bf16[2,2,64,768]{3,2,1,0:T(8,128)(2,1)} %copy-done.10) | copy-start | bytes 1179652
  34.2 61.5 %all-to-all-start = ((bf16[8,96,1536]{2,1,0:T(8,128)(2,1)}), bf16[8,96,1536]{2,1,0:T(8,128)(2,1)}, u32[]{:S(2)}, u32[]{:S(2)}) async-start(bf16[8,96,1536]{2,1,0:T(8,128)(2,1)} %tie.3), calls=%async_computation | async-start | bytes 4718592 | tf_op jit(solution)/shard_map/all_to_all | solution.py:1341
  38.9 4.8 %copy-start.16 = (bf16[3072]{0:T(1024)(128)(2,1)S(1)}, bf16[3072]{0:T(1024)(128)(2,1)}, u32[]{:S(2)}) copy-start(bf16[3072]{0:T(1024)(128)(2,1)} %refs_3_.4) | copy-start | bytes 18436
  39.0 6.2 %collective-permute-start.6 = (bf16[8,2,64,768]{3,2,1,0:T(8,128)(2,1)S(1)}, bf16[8,2,64,768]{3,2,1,0:T(8,128)(2,1)S(1)}, u32[]{:S(2)}, u32[]{:S(2)}) collective-permute-start(bf16[8,2,64,768]{3,2,1,0:T(8,128)(2,1)S(1)} %stack.46.refs_1_.refs_2_.refs_0_), channel_id=1, source_target_pairs={{0,8},{8,0},{16,24},{24,16},{1,9},{9,1},{17,25},{25,17},{2,10},{10... | collective-permute-start | bytes 4718600 | tf_op jit(solution)/shard_map/ppermute | solution.py:1291
  42.2 11.0 %collective-permute-start.7 = (bf16[2,2,64,768]{3,2,1,0:T(8,128)(2,1)}, bf16[2,2,64,768]{3,2,1,0:T(8,128)(2,1)}, u32[]{:S(2)}, u32[]{:S(2)}) collective-permute-start(bf16[2,2,64,768]{3,2,1,0:T(8,128)(2,1)} %get-tuple-element.78.refs_0_), channel_id=1, source_target_pairs={{0,16},{8,24},{16,0},{24,8},{1,17},{9,25},{17,1},{25,9},{2,18},{10... | collective-permute-start | bytes 1179656 | tf_op jit(solution)/shard_map/ppermute | solution.py:1291
  42.8 18.8 %collective-permute-start.10 = (bf16[2,2,64,768]{3,2,1,0:T(8,128)(2,1)}, bf16[2,2,64,768]{3,2,1,0:T(8,128)(2,1)}, u32[]{:S(2)}, u32[]{:S(2)}) collective-permute-start(bf16[2,2,64,768]{3,2,1,0:T(8,128)(2,1)} %collective-permute-done.9.refs_0_.refs_1_), channel_id=1, source_target_pairs={{0,16},{8,24},{16,0},{24,8},{1,17},{9,25},{17,1},{25,9},{2,18},{10... | collective-permute-start | bytes 1179656 | tf_op jit(solution)/shard_map/ppermute | solution.py:1291
  45.2 6.9 %copy-start.2 = (bf16[8,2,64,768]{3,2,1,0:T(8,128)(2,1)}, bf16[8,2,64,768]{3,2,1,0:T(8,128)(2,1)S(1)}, u32[]{:S(2)}) copy-start(bf16[8,2,64,768]{3,2,1,0:T(8,128)(2,1)S(1)} %collective-permute-done.6.refs_3_.refs_4_.refs_1_) | copy-start | bytes 4718596
  54.4 9.4 %collective-permute-start.8 = (bf16[4,2,64,768]{3,2,1,0:T(8,128)(2,1)S(1)}, bf16[4,2,64,768]{3,2,1,0:T(8,128)(2,1)}, u32[]{:S(2)}, u32[]{:S(2)}) collective-permute-start(bf16[4,2,64,768]{3,2,1,0:T(8,128)(2,1)S(1)} %stack.47.refs_2_.refs_1_), channel_id=1, source_target_pairs={{0,8},{8,0},{16,24},{24,16},{1,9},{9,1},{17,25},{25,17},{2,10},{10... | collective-permute-start | bytes 2359304 | tf_op jit(solution)/shard_map/ppermute | solution.py:1291
  62.8 1.0 copy-start
  62.8 6.1 %collective-permute-start.11 = (bf16[4,2,64,768]{3,2,1,0:T(8,128)(2,1)S(1)}, bf16[4,2,64,768]{3,2,1,0:T(8,128)(2,1)}, u32[]{:S(2)}, u32[]{:S(2)}) collective-permute-start(bf16[4,2,64,768]{3,2,1,0:T(8,128)(2,1)S(1)} %stack.48.refs_1_.refs_2_.refs_4_), channel_id=1, source_target_pairs={{0,8},{8,0},{16,24},{24,16},{1,9},{9,1},{17,25},{25,17},{2,10},{10... | collective-permute-start | bytes 2359304 | tf_op jit(solution)/shard_map/ppermute | solution.py:1291
  63.8 5.1 %copy-start.1 = (bf16[4,2,64,768]{3,2,1,0:T(8,128)(2,1)S(1)}, bf16[4,2,64,768]{3,2,1,0:T(8,128)(2,1)}, u32[]{:S(2)}) copy-start(bf16[4,2,64,768]{3,2,1,0:T(8,128)(2,1)} %copy-done) | copy-start | bytes 2359300
  68.9 5.1 %copy-start.3 = (bf16[8,2,64,768]{3,2,1,0:T(8,128)(2,1)S(1)}, bf16[8,2,64,768]{3,2,1,0:T(8,128)(2,1)}, u32[]{:S(2)}) copy-start(bf16[8,2,64,768]{3,2,1,0:T(8,128)(2,1)} %copy-done.2) | copy-start | bytes 4718596
  111.3 67.6 %all-to-all-start.1 = ((bf16[8,96,1792]{2,1,0:T(8,128)(2,1)}), bf16[8,96,1792]{2,1,0:T(8,128)(2,1)}, u32[]{:S(2)}, u32[]{:S(2)}) async-start(bf16[8,96,1792]{2,1,0:T(8,128)(2,1)} %get-tuple-element.122), calls=%async_computation.1 | async-start | bytes 5505024 | tf_op jit(solution)/shard_map/all_to_all | solution.py:1366
  123.8 47.1 %copy-start.5 = (bf16[256,768]{1,0:T(8,128)(2,1)S(1)}, bf16[256,768]{1,0:T(8,128)(2,1)}, u32[]{:S(2)}) copy-start(bf16[256,768]{1,0:T(8,128)(2,1)} %refs_3_.5) | copy-start | bytes 1179652
  154.3 2.5 %collective-permute-start.12 = (bf16[240,960]{1,0:T(8,128)(2,1)S(1)}, bf16[240,960]{1,0:T(8,128)(2,1)S(1)}, u32[]{:S(2)}, u32[]{:S(2)}) collective-permute-start(bf16[240,960]{1,0:T(8,128)(2,1)S(1)} %get-tuple-element.111), channel_id=1, source_target_pairs={{0,8},{8,0},{16,24},{24,16},{1,9},{9,1},{17,25},{25,17},{2,10},{10... | collective-permute-start | bytes 1382408 | tf_op jit(solution)/shard_map/ppermute | solution.py:1291
  157.0 13.8 %collective-permute-start.13 = (bf16[240,1152]{1,0:T(8,128)(2,1)S(1)}, bf16[240,1152]{1,0:T(8,128)(2,1)S(1)}, u32[]{:S(2)}, u32[]{:S(2)}) collective-permute-start(bf16[240,1152]{1,0:T(8,128)(2,1)S(1)} %merge.1.refs_1_), channel_id=1, source_target_pairs={{0,16},{8,24},{16,0},{24,8},{1,17},{9,25},{17,1},{25,9},{2,18},{10... | collective-permute-start | bytes 1658888 | tf_op jit(solution)/shard_map/ppermute | solution.py:1291
  173.1 3.0 %collective-permute-start.14 = (bf16[224,1536]{1,0:T(8,128)(2,1)S(1)}, bf16[224,1536]{1,0:T(8,128)(2,1)S(1)}, u32[]{:S(2)}, u32[]{:S(2)}) collective-permute-start(bf16[224,1536]{1,0:T(8,128)(2,1)S(1)} %get-tuple-element.114.refs_1_), channel_id=1, source_target_pairs={{0,8},{8,0},{16,24},{24,16},{1,9},{9,1},{17,25},{25,17},{2,10},{10... | collective-permute-start | bytes 2064392 | tf_op jit(solution)/shard_map/ppermute | solution.py:1291
  180.7 5.3 %copy-start.12 = (bf16[96,2048]{1,0:T(8,128)(2,1)S(1)}, bf16[96,2048]{1,0:T(8,128)(2,1)}, u32[]{:S(2)}) copy-start(bf16[96,2048]{1,0:T(8,128)(2,1)} %get-tuple-element.123.refs_1_) | copy-start | bytes 1179652
  180.7 5.2 %collective-permute-start.15 = (bf16[96,2048]{1,0:T(8,128)(2,1)}, bf16[96,2048]{1,0:T(8,128)(2,1)S(1)}, u32[]{:S(2)}, u32[]{:S(2)}) collective-permute-start(bf16[96,2048]{1,0:T(8,128)(2,1)} %get-tuple-element.123.refs_1_), channel_id=1, source_target_pairs={{0,8},{8,0},{16,24},{24,16},{1,9},{9,1},{17,25},{25,17},{2,10},{10... | collective-permute-start | bytes 1179656 | tf_op jit(solution)/shard_map/ppermute | solution.py:1291

commit v2 on v1

--- a/solution.py
+++ b/solution.py
@@ -331,10 +331,13 @@
     return jnp.where(place_in < ROT // 2, -low, jnp.where(place_in < ROT, high, 0.0))
 
 
-def with_column(tile, lane, column):
-    first = column.astype(BF).astype(F32)
+def with_column(tile, lane, column, parts):
     number = lanes(tile.shape[0])
-    return jnp.where(number == lane, first, jnp.where(number == lane + 1, column - first, tile))
+    for k in range(parts):
+        part = column.astype(BF).astype(F32) if k + 1 < parts else column
+        tile = jnp.where(number == lane + k, part, tile)
+        column = column - part
+    return tile
 
 
 def heads_joined(values):
@@ -397,7 +400,7 @@
         target[:, heads * pair :] = jnp.concatenate(values, axis=1).astype(target.dtype)
 
     number = lanes(block)
-    ones = (number >= HEAD_DIM + 16) & (number < HEAD_DIM + 18)
+    ones = (number >= HEAD_DIM + 16) & (number < HEAD_DIM + 19)
     coded = (number >= HEAD_DIM) & (number < HEAD_DIM + 16)
     for index in range(blocks):
         segment = jnp.broadcast_to(vectors_ref[16 + index : 17 + index, :block], (pair, block)).T
@@ -497,8 +500,8 @@
             delta = jnp.sum(attended * back, axis=-1, keepdims=True)
             log_total = top + jnp.log(total)
             query = query_s[head, start:stop, :].astype(F32)
-            query_s[head, start:stop, :] = with_column(query, HEAD_DIM + 16, -log_total).astype(BF)
-            back_s[head, start:stop, :] = with_column(back, HEAD_DIM, -delta).astype(BF)
+            query_s[head, start:stop, :] = with_column(query, HEAD_DIM + 16, -log_total, 3).astype(BF)
+            back_s[head, start:stop, :] = with_column(back, HEAD_DIM, -delta, 2).astype(BF)
         for copy in head_leaving(head):
             copy.start()
         return carry

time: 191 us -> 192 us (level)
  no operation moved by 1% of the time
where the time goes in v2:
time: 192 us; the launch traced here: 188 us
  Pallas kernels  118 us (61%)
  waiting for transfers between devices  33.4 us (17%)
  starting transfers between devices  32 us (17%)
  local copies, waits for them, and re-layouts  2.76 us (1%)
    pallas_call x20, Pallas kernels, call(): pl.pallas_call(body, in_specs=list(in_specs) + [ANY] * spare, input_outpu...  101 us
    ppermute x10, waiting for transfers between devices, swap_probe(): lax.ppermute(value, 'probe', [(i, i ^ distance) for i in range(probe_grou...  29.7 us
    pallas_call x3, Pallas kernels, hidden_units(): pl.pallas_call(body, grid_spec=pltpu.PrefetchScalarGridSpec(num_scalar_pr...  17.1 us
    ppermute x10, starting transfers between devices, swap_probe(): lax.ppermute(value, 'probe', [(i, i ^ distance) for i in range(probe_grou...  13 us
    ppermute x6, starting transfers between devices, swap(): return lax.ppermute(value, 'ex', [(i, i ^ distance) for i in range(groups)])  8.13 us
    all_to_all x1, starting transfers between devices, on_device(): lax.all_to_all(part, 'ex', 0, 0, axis_index_groups=row_groups, tiled=True)  6.12 us
    all_to_all x1, starting transfers between devices, on_device(): lax.all_to_all(dirs, 'ex', 0, 0, axis_index_groups=row_groups, tiled=True)  4.71 us
  transfers between devices with their start and end apart: 18, of which 10 were waited for; matrix products, arithmetic and copies ran while one was open for 0% of the time, Pallas kernels for 52%

profile of v2, /device:TPU:1, one launch (start us, length us, event | category | flops | bytes accessed | tf_op | source)
XLA Modules:
  0.0 188.0 jit_solution(15308501263172835153)
XLA Ops:
  0.7 1.2 slices.1
  1.8 2.2 %collective-permute-start.1 = (bf16[1,2,64,768]{3,2,1,0:T(8,128)(2,1)S(1)}, bf16[1,2,64,768]{3,2,1,0:T(8,128)(2,1)S(1)}, u32[]{:S(2)}, u32[]{:S(2)}) collective-permute-start(bf16[1,2,64,768]{3,2,1,0:T(8,128)(2,1)S(1)} %get-tuple-element.75), channel_id=1, source_target_pairs={{0,2},{1,3},{2,0},{3,1},{4,6},{5,7},{6,4},{7,5},{8,10},{9,11},{10,... | collective-permute-start | bytes 589832 | tf_op jit(solution)/shard_map/ppermute | solution.py:1291
  4.0 1.1 collective-permute-start.2
  5.1 2.3 %collective-permute-start.3 = (bf16[1,2,64,768]{3,2,1,0:T(8,128)(2,1)S(1)}, bf16[1,2,64,768]{3,2,1,0:T(8,128)(2,1)S(1)}, u32[]{:S(2)}, u32[]{:S(2)}) collective-permute-start(bf16[1,2,64,768]{3,2,1,0:T(8,128)(2,1)S(1)} %get-tuple-element.75), channel_id=1, source_target_pairs={{0,4},{1,5},{2,6},{3,7},{4,0},{5,1},{6,2},{7,3},{8,12},{9,13},{10,... | collective-permute-start | bytes 589832 | tf_op jit(solution)/shard_map/ppermute | solution.py:1291
  7.4 1.1 collective-permute-start.4
  8.8 1.0 vectors.1.refs_5_.refs_8_.refs_9_.refs_6_
  9.8 1.0 copy-done.4
  10.7 1.0 copy-done.7
  11.7 0.7 copy-done.15
  12.4 9.6 %local.1 = (f32[256,768]{1,0:T(8,128)S(1)}, f32[256,768]{1,0:T(8,128)S(1)}, f32[8,768]{1,0:T(8,128)S(1)}) custom-call(bf16[256,768]{1,0:T(8,128)(2,1)S(1)} %copy-done.4, bf16[256,768]{1,0:T(8,128)(2,1)S(1)} %copy-done.7, bf16[768,3072]{1,0:T(8,128)(2,1)} %refs_5_.7, bf16[3072]{0:T(1024)(128)(2,1)S(1)} %copy-done.15, bf16[3072,768]{1,0:T(8,128)(2,1)} %refs_7_.9, ...), custom_call_target="tpu_custom_call" | custom-call | flops 1000 | bytes 1000 | tf_op jit(solution)/shard_map/local/pallas_call | solution.py:102
  22.1 1.2 collective-permute-done.4.refs_3_
  23.3 0.8 stack.45
  24.1 1.2 collective-permute-start.5
  25.3 1.2 collective-permute-start.9
  26.5 1.7 pack.1.refs_0_
  28.2 4.9 %collective-permute-done.5.refs_3_.refs_2_ = bf16[2,2,64,768]{3,2,1,0:T(8,128)(2,1)S(1)} collective-permute-done((bf16[2,2,64,768]{3,2,1,0:T(8,128)(2,1)S(1)}, bf16[2,2,64,768]{3,2,1,0:T(8,128)(2,1)S(1)}, u32[]{:S(2)}, u32[]{:S(2)}) %collective-permute-start.5) | collective-permute-done | bytes 393248 | tf_op jit(solution)/shard_map/ppermute | solution.py:1294
  33.2 1.0 collective-permute-done.9.refs_0_.refs_1_
  34.2 4.7 %all-to-all-start = ((bf16[8,96,1536]{2,1,0:T(8,128)(2,1)}), bf16[8,96,1536]{2,1,0:T(8,128)(2,1)}, u32[]{:S(2)}, u32[]{:S(2)}) async-start(bf16[8,96,1536]{2,1,0:T(8,128)(2,1)} %tie.3), calls=%async_computation | async-start | bytes 4718592 | tf_op jit(solution)/shard_map/all_to_all | solution.py:1344
  39.0 3.2 %collective-permute-start.6 = (bf16[8,2,64,768]{3,2,1,0:T(8,128)(2,1)S(1)}, bf16[8,2,64,768]{3,2,1,0:T(8,128)(2,1)S(1)}, u32[]{:S(2)}, u32[]{:S(2)}) collective-permute-start(bf16[8,2,64,768]{3,2,1,0:T(8,128)(2,1)S(1)} %stack.46.refs_1_.refs_2_.refs_0_), channel_id=1, source_target_pairs={{0,8},{8,0},{16,24},{24,16},{1,9},{9,1},{17,25},{25,17},{2,10},{10... | collective-permute-start | bytes 4718600 | tf_op jit(solution)/shard_map/ppermute | solution.py:1294
  42.8 0.9 collective-permute-start.10
  43.8 1.4 collective-permute-done.6.refs_3_.refs_4_.refs_1_
  45.2 6.9 %hidden_units.3 = (bf16[2048,768]{1,0:T(8,128)(2,1)}, bf16[768,2048]{1,0:T(8,128)(2,1)}, f32[2048,384]{1,0:T(8,128)}, bf16[2048,384]{1,0:T(8,128)(2,1)}, bf16[20...) custom-call(s32[3]{0:T(128)S(1)} %pad_add_fusion.2.refs_0_, ...), custom_call_target="tpu_custom_call" | custom-call | flops 1000 | bytes 1000 | tf_op jit(solution)/shard_map/hidden_units/pallas_call | solution.py:809
  52.1 1.1 collective-permute-done.7.refs_1_
  53.2 1.2 stack.47.refs_2_.refs_1_
  54.4 1.4 collective-permute-start.8
  55.7 5.9 %collective-permute-done.10.refs_1_ = bf16[2,2,64,768]{3,2,1,0:T(8,128)(2,1)} collective-permute-done((bf16[2,2,64,768]{3,2,1,0:T(8,128)(2,1)}, bf16[2,2,64,768]{3,2,1,0:T(8,128)(2,1)}, u32[]{:S(2)}, u32[]{:S(2)}) %collective-permute-start.10) | collective-permute-done | bytes 393248 | tf_op jit(solution)/shard_map/ppermute | solution.py:1294
  61.6 1.2 stack.48.refs_1_.refs_2_.refs_4_
  62.8 0.9 collective-permute-start.11
  63.8 5.1 %hidden_units.4 = (bf16[2048,768]{1,0:T(8,128)(2,1)}, bf16[768,2048]{1,0:T(8,128)(2,1)}, f32[2048,384]{1,0:T(8,128)}, bf16[2048,384]{1,0:T(8,128)(2,1)}, bf16[20...) custom-call(s32[3]{0:T(128)S(1)} %pad_add_fusion.2.refs_0_, ...), custom_call_target="tpu_custom_call", output_to_operand_aliasing={{0}: (11, {}), {1}: (12, {}), {2}: (13, {}), {3}: (14, {}),... | custom-call | flops 1000 | bytes 1000 | tf_op jit(solution)/shard_map/hidden_units/pallas_call | solution.py:809
  69.0 5.1 %hidden_units.5 = (bf16[2048,768]{1,0:T(8,128)(2,1)}, bf16[768,2048]{1,0:T(8,128)(2,1)}, f32[2048,384]{1,0:T(8,128)}, bf16[2048,384]{1,0:T(8,128)(2,1)}, bf16[20...) custom-call(s32[3]{0:T(128)S(1)} %pad_add_fusion.2.refs_0_, ...), custom_call_target="tpu_custom_call", output_to_operand_aliasing={{0}: (11, {}), {1}: (12, {}), {2}: (13, {}), {3}: (14, {}),... | custom-call | flops 1000 | bytes 1000 | tf_op jit(solution)/shard_map/hidden_units/pallas_call | solution.py:809
  74.1 22.2 %attention.1 = (bf16[3,2048,128]{2,1,0:T(8,128)(2,1)}, bf16[3,2048,128]{2,1,0:T(8,128)(2,1)}, bf16[3,2048,128]{2,1,0:T(8,128)(2,1)}, bf16[3,2048,128]{2,1,0:T(8,...) custom-call(bf16[8,2,64,768]{3,2,1,0:T(8,128)(2,1)S(1)} %stack.46.refs_1_.refs_2_.ref, ...), custom_call_target="tpu_custom_call" | custom-call | flops 1000 | bytes 1000 | tf_op jit(solution)/shard_map/attention/pallas_call | solution.py:102
  96.3 15.7 %curvature.1 = (bf16[8,96,1792]{2,1,0:T(8,128)(2,1)}, f32[8,128]{1,0:T(8,128)S(1)}) custom-call(s32[1]{0:T(128)} %bitcast.refs_0_, bf16[768,1536]{1,0:T(8,128)(2,1)} %bitcast.8.refs_1_, f32[8,768]{1,0:T(8,128)S(1)} %get-tuple-element.76.refs_4_.refs_1_.refs_2_, f32[1,384]{1,0:T(1,128)S(1)} %get-tuple-element.102.refs_3_, ...), custom_call_target="tpu_custom_call" | custom-call | flops 1000 | bytes 1000 | tf_op jit(solution)/shard_map/curvature/pallas_call | solution.py:102
  112.0 6.1 %all-to-all-start.1 = ((bf16[8,96,1792]{2,1,0:T(8,128)(2,1)}), bf16[8,96,1792]{2,1,0:T(8,128)(2,1)}, u32[]{:S(2)}, u32[]{:S(2)}) async-start(bf16[8,96,1792]{2,1,0:T(8,128)(2,1)} %get-tuple-element.122), calls=%async_computation.1 | async-start | bytes 5505024 | tf_op jit(solution)/shard_map/all_to_all | solution.py:1369
  118.1 6.2 %weights_back.1 = (f32[384,768]{1,0:T(8,128)}, bf16[256,192]{1,0:T(8,128)(2,1)S(1)}, bf16[96,768]{1,0:T(8,128)(2,1)S(1)}) custom-call(s32[4]{0:T(128)S(1)} %pad_add_fusion.1.refs_6_.refs_0_, bf16[2048,384]{1,0:T(8,128)(2,1)} %get-tuple-element.99.refs_1_, bf16[2048,768]{1,0:T(8,128)(2,1)} %get-tuple-element.100.refs_2_, ...), custom_call_target="tpu_custom_call" | custom-call | flops 1000 | bytes 1000 | tf_op jit(solution)/shard_map/weights_back/pallas_call | solution.py:102
  124.3 30.5 %attention_back.1 = (bf16[240,960]{1,0:T(8,128)(2,1)S(1)}, bf16[240,960]{1,0:T(8,128)(2,1)S(1)}) custom-call(s32[4]{0:T(128)S(1)} %pad_add_fusion.1.refs_6_.refs_0_, bf16[3,2048,128]{2,1,0:T(8,128)(2,1)} %get-tuple-element.94.refs_1_, bf16[3,2048,128]{2,1,0:T(8,128)(2,1)} %get-tuple-element.95.refs_2_, bf16[3,2048,128]{2,1,0:T(8,128)(2,1)} %get-tuple-element.96.refs_3_, ...), custom_call_target="tpu_custom_call" | custom-call | flops 1000 | bytes 1000 | tf_op jit(solution)/shard_map/attention_back/pallas_call | solution.py:102
  154.8 1.1 collective-permute-start.12
  155.9 1.5 collective-permute-done.12.refs_2_
  157.6 0.7 collective-permute-start.13
  158.3 13.1 %collective-permute-done.13.refs_2_ = bf16[240,1152]{1,0:T(8,128)(2,1)S(1)} collective-permute-done((bf16[240,1152]{1,0:T(8,128)(2,1)S(1)}, bf16[240,1152]{1,0:T(8,128)(2,1)S(1)}, u32[]{:S(2)}, u32[]{:S(2)}) %collective-permute-start.13) | collective-permute-done | bytes 552992 | tf_op jit(solution)/shard_map/ppermute | solution.py:1294
  171.4 2.2 %finish.1 = (bf16[224,1536]{1,0:T(8,128)(2,1)S(1)}, f32[16,384]{1,0:T(8,128)S(1)}) custom-call(s32[2]{0:T(128)S(1)} %pad_add_fusion.refs_0_, bf16[240,1152]{1,0:T(8,128)(2,1)S(1)} %merge.1.refs_1_, bf16[240,1152]{1,0:T(8,128)(2,1)S(1)} %collective-permute-done.13.refs_2_, bf16[256,768]{1,0:T(8,128)(2,1)S(1)} %copy-done.5, f32[256,768]{1,0:T(8,128)} %copy-done.13, ...), custom_call_target="tpu_custom_call" | custom-call | flops 1000 | bytes 1000 | tf_op jit(solution)/shard_map/finish/pallas_call | solution.py:102
  173.6 1.3 collective-permute-start.14
  174.9 1.8 collective-permute-done.14.refs_2_
  176.7 1.3 join.1
  178.0 1.6 all-to-all-done.1.refs_0_
  179.6 1.8 peel.1
  181.4 1.9 collective-permute-start.15
  183.2 3.4 %unpack.1 = f32[4,96,3072]{2,1,0:T(8,128)} custom-call(bf16[8,96,1792]{2,1,0:T(8,128)(2,1)} %all-to-all-done.1.refs_0_, bf16[96,2048]{1,0:T(8,128)(2,1)} %get-tuple-element.123.refs_1_), custom_call_target="tpu_custom_call" | custom-call | flops 1000 | bytes 1000 | tf_op jit(solution)/shard_map/unpack/pallas_call | solution.py:102
  186.6 1.2 spread.1
  (50 shorter events, 1.6 us)
Async XLA Ops:
  1.8 20.2 %collective-permute-start.1 = (bf16[1,2,64,768]{3,2,1,0:T(8,128)(2,1)S(1)}, bf16[1,2,64,768]{3,2,1,0:T(8,128)(2,1)S(1)}, u32[]{:S(2)}, u32[]{:S(2)}) collective-permute-start(bf16[1,2,64,768]{3,2,1,0:T(8,128)(2,1)S(1)} %get-tuple-element.75), channel_id=1, source_target_pairs={{0,2},{1,3},{2,0},{3,1},{4,6},{5,7},{6,4},{7,5},{8,10},{9,11},{10,... | collective-permute-start | bytes 589832 | tf_op jit(solution)/shard_map/ppermute | solution.py:1291
  4.0 18.0 %collective-permute-start.2 = (bf16[1,2,64,768]{3,2,1,0:T(8,128)(2,1)S(1)}, bf16[1,2,64,768]{3,2,1,0:T(8,128)(2,1)S(1)}, u32[]{:S(2)}, u32[]{:S(2)}) collective-permute-start(bf16[1,2,64,768]{3,2,1,0:T(8,128)(2,1)S(1)} %get-tuple-element.75), channel_id=1, source_target_pairs={{0,3},{1,2},{2,1},{3,0},{4,7},{5,6},{6,5},{7,4},{8,11},{9,10},{10,... | collective-permute-start | bytes 589832 | tf_op jit(solution)/shard_map/ppermute | solution.py:1291
  5.1 16.9 %collective-permute-start.3 = (bf16[1,2,64,768]{3,2,1,0:T(8,128)(2,1)S(1)}, bf16[1,2,64,768]{3,2,1,0:T(8,128)(2,1)S(1)}, u32[]{:S(2)}, u32[]{:S(2)}) collective-permute-start(bf16[1,2,64,768]{3,2,1,0:T(8,128)(2,1)S(1)} %get-tuple-element.75), channel_id=1, source_target_pairs={{0,4},{1,5},{2,6},{3,7},{4,0},{5,1},{6,2},{7,3},{8,12},{9,13},{10,... | collective-permute-start | bytes 589832 | tf_op jit(solution)/shard_map/ppermute | solution.py:1291
  7.4 15.8 %collective-permute-start.4 = (bf16[1,2,64,768]{3,2,1,0:T(8,128)(2,1)S(1)}, bf16[1,2,64,768]{3,2,1,0:T(8,128)(2,1)S(1)}, u32[]{:S(2)}, u32[]{:S(2)}) collective-permute-start(bf16[1,2,64,768]{3,2,1,0:T(8,128)(2,1)S(1)} %get-tuple-element.75), channel_id=1, source_target_pairs={{0,6},{1,7},{2,4},{3,5},{4,2},{5,3},{6,0},{7,1},{8,14},{9,15},{10,... | collective-permute-start | bytes 589832 | tf_op jit(solution)/shard_map/ppermute | solution.py:1291
  8.5 19.7 %collective-permute-start = (bf16[2,2,64,768]{3,2,1,0:T(8,128)(2,1)S(1)}, bf16[2,2,64,768]{3,2,1,0:T(8,128)(2,1)S(1)}, u32[]{:S(2)}, u32[]{:S(2)}) collective-permute-start(bf16[2,2,64,768]{3,2,1,0:T(8,128)(2,1)S(1)} %get-tuple-element.74.refs_0_), channel_id=1, source_target_pairs={{0,1},{1,0},{2,3},{3,2},{4,5},{5,4},{6,7},{7,6},{8,9},{9,8},{10,11... | collective-permute-start | bytes 1179656 | tf_op jit(solution)/shard_map/ppermute | solution.py:1291
  9.7 1.0 copy-start.4
  10.7 1.0 copy-start.7
  11.7 0.7 copy-start.15
  12.4 14.1 %copy-start.6 = (bf16[4,96,3072]{2,1,0:T(8,128)(2,1)S(1)}, bf16[4,96,3072]{2,1,0:T(8,128)(2,1)}, u32[]{:S(2)}) copy-start(bf16[4,96,3072]{2,1,0:T(8,128)(2,1)} %refs_0_.5) | copy-start | bytes 7077892
  22.0 6.2 %copy-start.13 = (f32[256,768]{1,0:T(8,128)}, f32[256,768]{1,0:T(8,128)S(1)}, u32[]{:S(2)}) copy-start(f32[256,768]{1,0:T(8,128)S(1)} %get-tuple-element.112.refs_4_) | copy-start | bytes 2359300
  22.0 6.2 %copy-start.14 = (f32[256,768]{1,0:T(8,128)}, f32[256,768]{1,0:T(8,128)S(1)}, u32[]{:S(2)}) copy-start(f32[256,768]{1,0:T(8,128)S(1)} %get-tuple-element.113.refs_5_) | copy-start | bytes 2359300
  24.1 9.1 %collective-permute-start.5 = (bf16[2,2,64,768]{3,2,1,0:T(8,128)(2,1)S(1)}, bf16[2,2,64,768]{3,2,1,0:T(8,128)(2,1)S(1)}, u32[]{:S(2)}, u32[]{:S(2)}) collective-permute-start(bf16[2,2,64,768]{3,2,1,0:T(8,128)(2,1)S(1)} %get-tuple-element.77.refs_2_), channel_id=1, source_target_pairs={{0,16},{8,24},{16,0},{24,8},{1,17},{9,25},{17,1},{25,9},{2,18},{10... | collective-permute-start | bytes 1179656 | tf_op jit(solution)/shard_map/ppermute | solution.py:1294
  25.3 8.8 %collective-permute-start.9 = (bf16[2,2,64,768]{3,2,1,0:T(8,128)(2,1)S(1)}, bf16[2,2,64,768]{3,2,1,0:T(8,128)(2,1)}, u32[]{:S(2)}, u32[]{:S(2)}) collective-permute-start(bf16[2,2,64,768]{3,2,1,0:T(8,128)(2,1)S(1)} %get-tuple-element.77.refs_2_), channel_id=1, source_target_pairs={{0,1},{1,0},{2,3},{3,2},{4,5},{5,4},{6,7},{7,6},{8,9},{9,8},{10,11... | collective-permute-start | bytes 1179656 | tf_op jit(solution)/shard_map/ppermute | solution.py:1291
  28.2 5.9 %copy-start.8 = (bf16[2,2,64,768]{3,2,1,0:T(8,128)(2,1)}, bf16[2,2,64,768]{3,2,1,0:T(8,128)(2,1)S(1)}, u32[]{:S(2)}) copy-start(bf16[2,2,64,768]{3,2,1,0:T(8,128)(2,1)S(1)} %collective-permute-done.refs_1_.refs_3_) | copy-start | bytes 1179652
  33.2 1.0 copy-start.10
  34.1 4.7 %copy-start.9 = (bf16[2,2,64,768]{3,2,1,0:T(8,128)(2,1)S(1)}, bf16[2,2,64,768]{3,2,1,0:T(8,128)(2,1)}, u32[]{:S(2)}) copy-start(bf16[2,2,64,768]{3,2,1,0:T(8,128)(2,1)} %copy-done.8) | copy-start | bytes 1179652
  34.1 4.7 %copy-start.11 = (bf16[2,2,64,768]{3,2,1,0:T(8,128)(2,1)S(1)}, bf16[2,2,64,768]{3,2,1,0:T(8,128)(2,1)}, u32[]{:S(2)}) copy-start(bf16[2,2,64,768]{3,2,1,0:T(8,128)(2,1)} %copy-done.10) | copy-start | bytes 1179652
  34.2 62.1 %all-to-all-start = ((bf16[8,96,1536]{2,1,0:T(8,128)(2,1)}), bf16[8,96,1536]{2,1,0:T(8,128)(2,1)}, u32[]{:S(2)}, u32[]{:S(2)}) async-start(bf16[8,96,1536]{2,1,0:T(8,128)(2,1)} %tie.3), calls=%async_computation | async-start | bytes 4718592 | tf_op jit(solution)/shard_map/all_to_all | solution.py:1344
  38.9 4.8 %copy-start.16 = (bf16[3072]{0:T(1024)(128)(2,1)S(1)}, bf16[3072]{0:T(1024)(128)(2,1)}, u32[]{:S(2)}) copy-start(bf16[3072]{0:T(1024)(128)(2,1)} %refs_3_.4) | copy-start | bytes 18436
  39.0 6.2 %collective-permute-start.6 = (bf16[8,2,64,768]{3,2,1,0:T(8,128)(2,1)S(1)}, bf16[8,2,64,768]{3,2,1,0:T(8,128)(2,1)S(1)}, u32[]{:S(2)}, u32[]{:S(2)}) collective-permute-start(bf16[8,2,64,768]{3,2,1,0:T(8,128)(2,1)S(1)} %stack.46.refs_1_.refs_2_.refs_0_), channel_id=1, source_target_pairs={{0,8},{8,0},{16,24},{24,16},{1,9},{9,1},{17,25},{25,17},{2,10},{10... | collective-permute-start | bytes 4718600 | tf_op jit(solution)/shard_map/ppermute | solution.py:1294
  42.2 11.0 %collective-permute-start.7 = (bf16[2,2,64,768]{3,2,1,0:T(8,128)(2,1)}, bf16[2,2,64,768]{3,2,1,0:T(8,128)(2,1)}, u32[]{:S(2)}, u32[]{:S(2)}) collective-permute-start(bf16[2,2,64,768]{3,2,1,0:T(8,128)(2,1)} %get-tuple-element.78.refs_0_), channel_id=1, source_target_pairs={{0,16},{8,24},{16,0},{24,8},{1,17},{9,25},{17,1},{25,9},{2,18},{10... | collective-permute-start | bytes 1179656 | tf_op jit(solution)/shard_map/ppermute | solution.py:1294
  42.8 18.8 %collective-permute-start.10 = (bf16[2,2,64,768]{3,2,1,0:T(8,128)(2,1)}, bf16[2,2,64,768]{3,2,1,0:T(8,128)(2,1)}, u32[]{:S(2)}, u32[]{:S(2)}) collective-permute-start(bf16[2,2,64,768]{3,2,1,0:T(8,128)(2,1)} %collective-permute-done.9.refs_0_.refs_1_), channel_id=1, source_target_pairs={{0,16},{8,24},{16,0},{24,8},{1,17},{9,25},{17,1},{25,9},{2,18},{10... | collective-permute-start | bytes 1179656 | tf_op jit(solution)/shard_map/ppermute | solution.py:1294
  45.2 6.9 %copy-start.2 = (bf16[8,2,64,768]{3,2,1,0:T(8,128)(2,1)}, bf16[8,2,64,768]{3,2,1,0:T(8,128)(2,1)S(1)}, u32[]{:S(2)}) copy-start(bf16[8,2,64,768]{3,2,1,0:T(8,128)(2,1)S(1)} %collective-permute-done.6.refs_3_.refs_4_.refs_1_) | copy-start | bytes 4718596
  54.4 9.4 %collective-permute-start.8 = (bf16[4,2,64,768]{3,2,1,0:T(8,128)(2,1)S(1)}, bf16[4,2,64,768]{3,2,1,0:T(8,128)(2,1)}, u32[]{:S(2)}, u32[]{:S(2)}) collective-permute-start(bf16[4,2,64,768]{3,2,1,0:T(8,128)(2,1)S(1)} %stack.47.refs_2_.refs_1_), channel_id=1, source_target_pairs={{0,8},{8,0},{16,24},{24,16},{1,9},{9,1},{17,25},{25,17},{2,10},{10... | collective-permute-start | bytes 2359304 | tf_op jit(solution)/shard_map/ppermute | solution.py:1294
  62.8 1.0 copy-start
  62.8 6.1 %collective-permute-start.11 = (bf16[4,2,64,768]{3,2,1,0:T(8,128)(2,1)S(1)}, bf16[4,2,64,768]{3,2,1,0:T(8,128)(2,1)}, u32[]{:S(2)}, u32[]{:S(2)}) collective-permute-start(bf16[4,2,64,768]{3,2,1,0:T(8,128)(2,1)S(1)} %stack.48.refs_1_.refs_2_.refs_4_), channel_id=1, source_target_pairs={{0,8},{8,0},{16,24},{24,16},{1,9},{9,1},{17,25},{25,17},{2,10},{10... | collective-permute-start | bytes 2359304 | tf_op jit(solution)/shard_map/ppermute | solution.py:1294
  63.8 5.1 %copy-start.1 = (bf16[4,2,64,768]{3,2,1,0:T(8,128)(2,1)S(1)}, bf16[4,2,64,768]{3,2,1,0:T(8,128)(2,1)}, u32[]{:S(2)}) copy-start(bf16[4,2,64,768]{3,2,1,0:T(8,128)(2,1)} %copy-done) | copy-start | bytes 2359300
  68.9 5.1 %copy-start.3 = (bf16[8,2,64,768]{3,2,1,0:T(8,128)(2,1)S(1)}, bf16[8,2,64,768]{3,2,1,0:T(8,128)(2,1)}, u32[]{:S(2)}) copy-start(bf16[8,2,64,768]{3,2,1,0:T(8,128)(2,1)} %copy-done.2) | copy-start | bytes 4718596
  112.0 67.6 %all-to-all-start.1 = ((bf16[8,96,1792]{2,1,0:T(8,128)(2,1)}), bf16[8,96,1792]{2,1,0:T(8,128)(2,1)}, u32[]{:S(2)}, u32[]{:S(2)}) async-start(bf16[8,96,1792]{2,1,0:T(8,128)(2,1)} %get-tuple-element.122), calls=%async_computation.1 | async-start | bytes 5505024 | tf_op jit(solution)/shard_map/all_to_all | solution.py:1369
  124.3 47.1 %copy-start.5 = (bf16[256,768]{1,0:T(8,128)(2,1)S(1)}, bf16[256,768]{1,0:T(8,128)(2,1)}, u32[]{:S(2)}) copy-start(bf16[256,768]{1,0:T(8,128)(2,1)} %refs_3_.5) | copy-start | bytes 1179652
  154.8 2.5 %collective-permute-start.12 = (bf16[240,960]{1,0:T(8,128)(2,1)S(1)}, bf16[240,960]{1,0:T(8,128)(2,1)S(1)}, u32[]{:S(2)}, u32[]{:S(2)}) collective-permute-start(bf16[240,960]{1,0:T(8,128)(2,1)S(1)} %get-tuple-element.111), channel_id=1, source_target_pairs={{0,8},{8,0},{16,24},{24,16},{1,9},{9,1},{17,25},{25,17},{2,10},{10... | collective-permute-start | bytes 1382408 | tf_op jit(solution)/shard_map/ppermute | solution.py:1294
  157.6 13.8 %collective-permute-start.13 = (bf16[240,1152]{1,0:T(8,128)(2,1)S(1)}, bf16[240,1152]{1,0:T(8,128)(2,1)S(1)}, u32[]{:S(2)}, u32[]{:S(2)}) collective-permute-start(bf16[240,1152]{1,0:T(8,128)(2,1)S(1)} %merge.1.refs_1_), channel_id=1, source_target_pairs={{0,16},{8,24},{16,0},{24,8},{1,17},{9,25},{17,1},{25,9},{2,18},{10... | collective-permute-start | bytes 1658888 | tf_op jit(solution)/shard_map/ppermute | solution.py:1294
  173.6 3.0 %collective-permute-start.14 = (bf16[224,1536]{1,0:T(8,128)(2,1)S(1)}, bf16[224,1536]{1,0:T(8,128)(2,1)S(1)}, u32[]{:S(2)}, u32[]{:S(2)}) collective-permute-start(bf16[224,1536]{1,0:T(8,128)(2,1)S(1)} %get-tuple-element.114.refs_1_), channel_id=1, source_target_pairs={{0,8},{8,0},{16,24},{24,16},{1,9},{9,1},{17,25},{25,17},{2,10},{10... | collective-permute-start | bytes 2064392 | tf_op jit(solution)/shard_map/ppermute | solution.py:1294
  181.4 5.3 %copy-start.12 = (bf16[96,2048]{1,0:T(8,128)(2,1)S(1)}, bf16[96,2048]{1,0:T(8,128)(2,1)}, u32[]{:S(2)}) copy-start(bf16[96,2048]{1,0:T(8,128)(2,1)} %get-tuple-element.123.refs_1_) | copy-start | bytes 1179652
  181.4 5.3 %collective-permute-start.15 = (bf16[96,2048]{1,0:T(8,128)(2,1)}, bf16[96,2048]{1,0:T(8,128)(2,1)S(1)}, u32[]{:S(2)}, u32[]{:S(2)}) collective-permute-start(bf16[96,2048]{1,0:T(8,128)(2,1)} %get-tuple-element.123.refs_1_), channel_id=1, source_target_pairs={{0,8},{8,0},{16,24},{24,16},{1,9},{9,1},{17,25},{25,17},{2,10},{10... | collective-permute-start | bytes 1179656 | tf_op jit(solution)/shard_map/ppermute | solution.py:1294

commit v3 on v2

--- a/solution.py
+++ b/solution.py
@@ -883,12 +883,6 @@
     last.wait()
     shape = curvature_ref.shape[:2]
     leaving = []
-    for k in range(0, probes, 2):
-        columns = slice(k * part_width, (k + 2) * part_width)
-        total = dot(turned_ref[...], weighted_s[:, columns])
-        curvature_ref[:, :, columns] = total.astype(BF).reshape(shape + (2 * part_width,))
-        leaving.append((curvature_ref.at[:, :, columns], curvature_out.at[:, :, columns]))
-        pltpu.make_async_copy(*leaving[-1], sems.at[3 * steps + 1 + len(leaving)]).start()
     final = dot(turned_ref[...], weighted_s[:, width:]).astype(BF)
     own = jnp.where(place_ref[0] == 1, final[:, half:], final[:, :half])
     scores = jnp.sum(score_s[...], axis=1, keepdims=True)
@@ -913,6 +907,12 @@
     curvature_ref[:, :, width + LANES :] = tail
     leaving.append((curvature_ref.at[:, :, width:], curvature_out.at[:, :, width:]))
     pltpu.make_async_copy(*leaving[-1], sems.at[3 * steps + 1 + len(leaving)]).start()
+    for k in range(0, probes, 2):
+        columns = slice(k * part_width, (k + 2) * part_width)
+        total = dot(turned_ref[...], weighted_s[:, columns])
+        curvature_ref[:, :, columns] = total.astype(BF).reshape(shape + (2 * part_width,))
+        leaving.append((curvature_ref.at[:, :, columns], curvature_out.at[:, :, columns]))
+        pltpu.make_async_copy(*leaving[-1], sems.at[3 * steps + 1 + len(leaving)]).start()
     for number, move in enumerate(leaving):
         pltpu.make_async_copy(*move, sems.at[3 * steps + 2 + number]).wait()
 

time: 192 us -> 192 us (level)
  no operation moved by 1% of the time
where the time goes in v3:
time: 192 us; the launch traced here: 188 us
  Pallas kernels  119 us (62%)
  waiting for transfers between devices  33.3 us (17%)
  starting transfers between devices  32 us (17%)
  local copies, waits for them, and re-layouts  2.76 us (1%)
    pallas_call x20, Pallas kernels, call(): pl.pallas_call(body, in_specs=list(in_specs) + [ANY] * spare, input_outpu...  102 us
    ppermute x10, waiting for transfers between devices, swap_probe(): lax.ppermute(value, 'probe', [(i, i ^ distance) for i in range(probe_grou...  29.7 us
    pallas_call x3, Pallas kernels, hidden_units(): pl.pallas_call(body, grid_spec=pltpu.PrefetchScalarGridSpec(num_scalar_pr...  17.1 us
    ppermute x10, starting transfers between devices, swap_probe(): lax.ppermute(value, 'probe', [(i, i ^ distance) for i in range(probe_grou...  13 us
    ppermute x6, starting transfers between devices, swap(): return lax.ppermute(value, 'ex', [(i, i ^ distance) for i in range(groups)])  8.13 us
    all_to_all x1, starting transfers between devices, on_device(): lax.all_to_all(part, 'ex', 0, 0, axis_index_groups=row_groups, tiled=True)  6.17 us
    all_to_all x1, starting transfers between devices, on_device(): lax.all_to_all(dirs, 'ex', 0, 0, axis_index_groups=row_groups, tiled=True)  4.71 us
  transfers between devices with their start and end apart: 18, of which 10 were waited for; matrix products, arithmetic and copies ran while one was open for 0% of the time, Pallas kernels for 52%

profile of v3, /device:TPU:1, one launch (start us, length us, event | category | flops | bytes accessed | tf_op | source)
XLA Modules:
  0.0 188.1 jit_solution(10208938784950272567)
XLA Ops:
  0.7 1.2 slices.1
  1.8 2.2 %collective-permute-start.1 = (bf16[1,2,64,768]{3,2,1,0:T(8,128)(2,1)S(1)}, bf16[1,2,64,768]{3,2,1,0:T(8,128)(2,1)S(1)}, u32[]{:S(2)}, u32[]{:S(2)}) collective-permute-start(bf16[1,2,64,768]{3,2,1,0:T(8,128)(2,1)S(1)} %get-tuple-element.75), channel_id=1, source_target_pairs={{0,2},{1,3},{2,0},{3,1},{4,6},{5,7},{6,4},{7,5},{8,10},{9,11},{10,... | collective-permute-start | bytes 589832 | tf_op jit(solution)/shard_map/ppermute | solution.py:1291
  4.0 1.1 collective-permute-start.2
  5.1 2.3 %collective-permute-start.3 = (bf16[1,2,64,768]{3,2,1,0:T(8,128)(2,1)S(1)}, bf16[1,2,64,768]{3,2,1,0:T(8,128)(2,1)S(1)}, u32[]{:S(2)}, u32[]{:S(2)}) collective-permute-start(bf16[1,2,64,768]{3,2,1,0:T(8,128)(2,1)S(1)} %get-tuple-element.75), channel_id=1, source_target_pairs={{0,4},{1,5},{2,6},{3,7},{4,0},{5,1},{6,2},{7,3},{8,12},{9,13},{10,... | collective-permute-start | bytes 589832 | tf_op jit(solution)/shard_map/ppermute | solution.py:1291
  7.4 1.1 collective-permute-start.4
  8.8 1.0 vectors.1.refs_5_.refs_8_.refs_9_.refs_6_
  9.8 1.0 copy-done.4
  10.7 1.0 copy-done.7
  11.7 0.7 copy-done.15
  12.4 9.6 %local.1 = (f32[256,768]{1,0:T(8,128)S(1)}, f32[256,768]{1,0:T(8,128)S(1)}, f32[8,768]{1,0:T(8,128)S(1)}) custom-call(bf16[256,768]{1,0:T(8,128)(2,1)S(1)} %copy-done.4, bf16[256,768]{1,0:T(8,128)(2,1)S(1)} %copy-done.7, bf16[768,3072]{1,0:T(8,128)(2,1)} %refs_5_.7, bf16[3072]{0:T(1024)(128)(2,1)S(1)} %copy-done.15, bf16[3072,768]{1,0:T(8,128)(2,1)} %refs_7_.9, ...), custom_call_target="tpu_custom_call" | custom-call | flops 1000 | bytes 1000 | tf_op jit(solution)/shard_map/local/pallas_call | solution.py:102
  22.1 1.2 collective-permute-done.4.refs_3_
  23.3 0.8 stack.45
  24.1 1.2 collective-permute-start.5
  25.3 1.2 collective-permute-start.9
  26.5 1.7 pack.1.refs_0_
  28.2 4.9 %collective-permute-done.5.refs_3_.refs_2_ = bf16[2,2,64,768]{3,2,1,0:T(8,128)(2,1)S(1)} collective-permute-done((bf16[2,2,64,768]{3,2,1,0:T(8,128)(2,1)S(1)}, bf16[2,2,64,768]{3,2,1,0:T(8,128)(2,1)S(1)}, u32[]{:S(2)}, u32[]{:S(2)}) %collective-permute-start.5) | collective-permute-done | bytes 393248 | tf_op jit(solution)/shard_map/ppermute | solution.py:1294
  33.2 1.0 collective-permute-done.9.refs_0_.refs_1_
  34.2 4.7 %all-to-all-start = ((bf16[8,96,1536]{2,1,0:T(8,128)(2,1)}), bf16[8,96,1536]{2,1,0:T(8,128)(2,1)}, u32[]{:S(2)}, u32[]{:S(2)}) async-start(bf16[8,96,1536]{2,1,0:T(8,128)(2,1)} %tie.3), calls=%async_computation | async-start | bytes 4718592 | tf_op jit(solution)/shard_map/all_to_all | solution.py:1344
  39.0 3.2 %collective-permute-start.6 = (bf16[8,2,64,768]{3,2,1,0:T(8,128)(2,1)S(1)}, bf16[8,2,64,768]{3,2,1,0:T(8,128)(2,1)S(1)}, u32[]{:S(2)}, u32[]{:S(2)}) collective-permute-start(bf16[8,2,64,768]{3,2,1,0:T(8,128)(2,1)S(1)} %stack.46.refs_1_.refs_2_.refs_0_), channel_id=1, source_target_pairs={{0,8},{8,0},{16,24},{24,16},{1,9},{9,1},{17,25},{25,17},{2,10},{10... | collective-permute-start | bytes 4718600 | tf_op jit(solution)/shard_map/ppermute | solution.py:1294
  42.8 0.9 collective-permute-start.10
  43.8 1.4 collective-permute-done.6.refs_3_.refs_4_.refs_1_
  45.2 6.9 %hidden_units.3 = (bf16[2048,768]{1,0:T(8,128)(2,1)}, bf16[768,2048]{1,0:T(8,128)(2,1)}, f32[2048,384]{1,0:T(8,128)}, bf16[2048,384]{1,0:T(8,128)(2,1)}, bf16[20...) custom-call(s32[3]{0:T(128)S(1)} %pad_add_fusion.2.refs_0_, ...), custom_call_target="tpu_custom_call" | custom-call | flops 1000 | bytes 1000 | tf_op jit(solution)/shard_map/hidden_units/pallas_call | solution.py:809
  52.1 1.1 collective-permute-done.7.refs_1_
  53.2 1.2 stack.47.refs_2_.refs_1_
  54.4 1.4 collective-permute-start.8
  55.7 5.9 %collective-permute-done.10.refs_1_ = bf16[2,2,64,768]{3,2,1,0:T(8,128)(2,1)} collective-permute-done((bf16[2,2,64,768]{3,2,1,0:T(8,128)(2,1)}, bf16[2,2,64,768]{3,2,1,0:T(8,128)(2,1)}, u32[]{:S(2)}, u32[]{:S(2)}) %collective-permute-start.10) | collective-permute-done | bytes 393248 | tf_op jit(solution)/shard_map/ppermute | solution.py:1294
  61.6 1.2 stack.48.refs_1_.refs_2_.refs_4_
  62.8 0.9 collective-permute-start.11
  63.8 5.1 %hidden_units.4 = (bf16[2048,768]{1,0:T(8,128)(2,1)}, bf16[768,2048]{1,0:T(8,128)(2,1)}, f32[2048,384]{1,0:T(8,128)}, bf16[2048,384]{1,0:T(8,128)(2,1)}, bf16[20...) custom-call(s32[3]{0:T(128)S(1)} %pad_add_fusion.2.refs_0_, ...), custom_call_target="tpu_custom_call", output_to_operand_aliasing={{0}: (11, {}), {1}: (12, {}), {2}: (13, {}), {3}: (14, {}),... | custom-call | flops 1000 | bytes 1000 | tf_op jit(solution)/shard_map/hidden_units/pallas_call | solution.py:809
  69.0 5.1 %hidden_units.5 = (bf16[2048,768]{1,0:T(8,128)(2,1)}, bf16[768,2048]{1,0:T(8,128)(2,1)}, f32[2048,384]{1,0:T(8,128)}, bf16[2048,384]{1,0:T(8,128)(2,1)}, bf16[20...) custom-call(s32[3]{0:T(128)S(1)} %pad_add_fusion.2.refs_0_, ...), custom_call_target="tpu_custom_call", output_to_operand_aliasing={{0}: (11, {}), {1}: (12, {}), {2}: (13, {}), {3}: (14, {}),... | custom-call | flops 1000 | bytes 1000 | tf_op jit(solution)/shard_map/hidden_units/pallas_call | solution.py:809
  74.1 22.2 %attention.1 = (bf16[3,2048,128]{2,1,0:T(8,128)(2,1)}, bf16[3,2048,128]{2,1,0:T(8,128)(2,1)}, bf16[3,2048,128]{2,1,0:T(8,128)(2,1)}, bf16[3,2048,128]{2,1,0:T(8,...) custom-call(bf16[8,2,64,768]{3,2,1,0:T(8,128)(2,1)S(1)} %stack.46.refs_1_.refs_2_.ref, ...), custom_call_target="tpu_custom_call" | custom-call | flops 1000 | bytes 1000 | tf_op jit(solution)/shard_map/attention/pallas_call | solution.py:102
  96.3 15.8 %curvature.1 = (bf16[8,96,1792]{2,1,0:T(8,128)(2,1)}, f32[8,128]{1,0:T(8,128)S(1)}) custom-call(s32[1]{0:T(128)} %bitcast.refs_0_, bf16[768,1536]{1,0:T(8,128)(2,1)} %bitcast.8.refs_1_, f32[8,768]{1,0:T(8,128)S(1)} %get-tuple-element.76.refs_4_.refs_1_.refs_2_, f32[1,384]{1,0:T(1,128)S(1)} %get-tuple-element.102.refs_3_, ...), custom_call_target="tpu_custom_call" | custom-call | flops 1000 | bytes 1000 | tf_op jit(solution)/shard_map/curvature/pallas_call | solution.py:102
  112.1 6.2 %all-to-all-start.1 = ((bf16[8,96,1792]{2,1,0:T(8,128)(2,1)}), bf16[8,96,1792]{2,1,0:T(8,128)(2,1)}, u32[]{:S(2)}, u32[]{:S(2)}) async-start(bf16[8,96,1792]{2,1,0:T(8,128)(2,1)} %get-tuple-element.122), calls=%async_computation.1 | async-start | bytes 5505024 | tf_op jit(solution)/shard_map/all_to_all | solution.py:1369
  118.3 6.2 %weights_back.1 = (f32[384,768]{1,0:T(8,128)}, bf16[256,192]{1,0:T(8,128)(2,1)S(1)}, bf16[96,768]{1,0:T(8,128)(2,1)S(1)}) custom-call(s32[4]{0:T(128)S(1)} %pad_add_fusion.1.refs_6_.refs_0_, bf16[2048,384]{1,0:T(8,128)(2,1)} %get-tuple-element.99.refs_1_, bf16[2048,768]{1,0:T(8,128)(2,1)} %get-tuple-element.100.refs_2_, ...), custom_call_target="tpu_custom_call" | custom-call | flops 1000 | bytes 1000 | tf_op jit(solution)/shard_map/weights_back/pallas_call | solution.py:102
  124.5 30.5 %attention_back.1 = (bf16[240,960]{1,0:T(8,128)(2,1)S(1)}, bf16[240,960]{1,0:T(8,128)(2,1)S(1)}) custom-call(s32[4]{0:T(128)S(1)} %pad_add_fusion.1.refs_6_.refs_0_, bf16[3,2048,128]{2,1,0:T(8,128)(2,1)} %get-tuple-element.94.refs_1_, bf16[3,2048,128]{2,1,0:T(8,128)(2,1)} %get-tuple-element.95.refs_2_, bf16[3,2048,128]{2,1,0:T(8,128)(2,1)} %get-tuple-element.96.refs_3_, ...), custom_call_target="tpu_custom_call" | custom-call | flops 1000 | bytes 1000 | tf_op jit(solution)/shard_map/attention_back/pallas_call | solution.py:102
  155.0 1.1 collective-permute-start.12
  156.1 1.5 collective-permute-done.12.refs_2_
  157.8 0.7 collective-permute-start.13
  158.5 13.1 %collective-permute-done.13.refs_2_ = bf16[240,1152]{1,0:T(8,128)(2,1)S(1)} collective-permute-done((bf16[240,1152]{1,0:T(8,128)(2,1)S(1)}, bf16[240,1152]{1,0:T(8,128)(2,1)S(1)}, u32[]{:S(2)}, u32[]{:S(2)}) %collective-permute-start.13) | collective-permute-done | bytes 552992 | tf_op jit(solution)/shard_map/ppermute | solution.py:1294
  171.6 2.2 %finish.1 = (bf16[224,1536]{1,0:T(8,128)(2,1)S(1)}, f32[16,384]{1,0:T(8,128)S(1)}) custom-call(s32[2]{0:T(128)S(1)} %pad_add_fusion.refs_0_, bf16[240,1152]{1,0:T(8,128)(2,1)S(1)} %merge.1.refs_1_, bf16[240,1152]{1,0:T(8,128)(2,1)S(1)} %collective-permute-done.13.refs_2_, bf16[256,768]{1,0:T(8,128)(2,1)S(1)} %copy-done.5, f32[256,768]{1,0:T(8,128)} %copy-done.13, ...), custom_call_target="tpu_custom_call" | custom-call | flops 1000 | bytes 1000 | tf_op jit(solution)/shard_map/finish/pallas_call | solution.py:102
  173.8 1.3 collective-permute-start.14
  175.1 1.8 collective-permute-done.14.refs_2_
  176.9 1.3 join.1
  178.2 1.5 all-to-all-done.1.refs_0_
  179.7 1.8 peel.1
  181.5 1.8 collective-permute-start.15
  183.3 3.4 %unpack.1 = f32[4,96,3072]{2,1,0:T(8,128)} custom-call(bf16[8,96,1792]{2,1,0:T(8,128)(2,1)} %all-to-all-done.1.refs_0_, bf16[96,2048]{1,0:T(8,128)(2,1)} %get-tuple-element.123.refs_1_), custom_call_target="tpu_custom_call" | custom-call | flops 1000 | bytes 1000 | tf_op jit(solution)/shard_map/unpack/pallas_call | solution.py:102
  186.7 1.2 spread.1
  (50 shorter events, 1.6 us)
Async XLA Ops:
  1.8 20.2 %collective-permute-start.1 = (bf16[1,2,64,768]{3,2,1,0:T(8,128)(2,1)S(1)}, bf16[1,2,64,768]{3,2,1,0:T(8,128)(2,1)S(1)}, u32[]{:S(2)}, u32[]{:S(2)}) collective-permute-start(bf16[1,2,64,768]{3,2,1,0:T(8,128)(2,1)S(1)} %get-tuple-element.75), channel_id=1, source_target_pairs={{0,2},{1,3},{2,0},{3,1},{4,6},{5,7},{6,4},{7,5},{8,10},{9,11},{10,... | collective-permute-start | bytes 589832 | tf_op jit(solution)/shard_map/ppermute | solution.py:1291
  4.0 18.0 %collective-permute-start.2 = (bf16[1,2,64,768]{3,2,1,0:T(8,128)(2,1)S(1)}, bf16[1,2,64,768]{3,2,1,0:T(8,128)(2,1)S(1)}, u32[]{:S(2)}, u32[]{:S(2)}) collective-permute-start(bf16[1,2,64,768]{3,2,1,0:T(8,128)(2,1)S(1)} %get-tuple-element.75), channel_id=1, source_target_pairs={{0,3},{1,2},{2,1},{3,0},{4,7},{5,6},{6,5},{7,4},{8,11},{9,10},{10,... | collective-permute-start | bytes 589832 | tf_op jit(solution)/shard_map/ppermute | solution.py:1291
  5.1 16.9 %collective-permute-start.3 = (bf16[1,2,64,768]{3,2,1,0:T(8,128)(2,1)S(1)}, bf16[1,2,64,768]{3,2,1,0:T(8,128)(2,1)S(1)}, u32[]{:S(2)}, u32[]{:S(2)}) collective-permute-start(bf16[1,2,64,768]{3,2,1,0:T(8,128)(2,1)S(1)} %get-tuple-element.75), channel_id=1, source_target_pairs={{0,4},{1,5},{2,6},{3,7},{4,0},{5,1},{6,2},{7,3},{8,12},{9,13},{10,... | collective-permute-start | bytes 589832 | tf_op jit(solution)/shard_map/ppermute | solution.py:1291
  7.4 15.8 %collective-permute-start.4 = (bf16[1,2,64,768]{3,2,1,0:T(8,128)(2,1)S(1)}, bf16[1,2,64,768]{3,2,1,0:T(8,128)(2,1)S(1)}, u32[]{:S(2)}, u32[]{:S(2)}) collective-permute-start(bf16[1,2,64,768]{3,2,1,0:T(8,128)(2,1)S(1)} %get-tuple-element.75), channel_id=1, source_target_pairs={{0,6},{1,7},{2,4},{3,5},{4,2},{5,3},{6,0},{7,1},{8,14},{9,15},{10,... | collective-permute-start | bytes 589832 | tf_op jit(solution)/shard_map/ppermute | solution.py:1291
  8.5 19.7 %collective-permute-start = (bf16[2,2,64,768]{3,2,1,0:T(8,128)(2,1)S(1)}, bf16[2,2,64,768]{3,2,1,0:T(8,128)(2,1)S(1)}, u32[]{:S(2)}, u32[]{:S(2)}) collective-permute-start(bf16[2,2,64,768]{3,2,1,0:T(8,128)(2,1)S(1)} %get-tuple-element.74.refs_0_), channel_id=1, source_target_pairs={{0,1},{1,0},{2,3},{3,2},{4,5},{5,4},{6,7},{7,6},{8,9},{9,8},{10,11... | collective-permute-start | bytes 1179656 | tf_op jit(solution)/shard_map/ppermute | solution.py:1291
  9.7 1.0 copy-start.4
  10.7 1.0 copy-start.7
  11.7 0.7 copy-start.15
  12.4 14.1 %copy-start.6 = (bf16[4,96,3072]{2,1,0:T(8,128)(2,1)S(1)}, bf16[4,96,3072]{2,1,0:T(8,128)(2,1)}, u32[]{:S(2)}) copy-start(bf16[4,96,3072]{2,1,0:T(8,128)(2,1)} %refs_0_.5) | copy-start | bytes 7077892
  22.0 6.2 %copy-start.13 = (f32[256,768]{1,0:T(8,128)}, f32[256,768]{1,0:T(8,128)S(1)}, u32[]{:S(2)}) copy-start(f32[256,768]{1,0:T(8,128)S(1)} %get-tuple-element.112.refs_4_) | copy-start | bytes 2359300
  22.0 6.2 %copy-start.14 = (f32[256,768]{1,0:T(8,128)}, f32[256,768]{1,0:T(8,128)S(1)}, u32[]{:S(2)}) copy-start(f32[256,768]{1,0:T(8,128)S(1)} %get-tuple-element.113.refs_5_) | copy-start | bytes 2359300
  24.1 9.1 %collective-permute-start.5 = (bf16[2,2,64,768]{3,2,1,0:T(8,128)(2,1)S(1)}, bf16[2,2,64,768]{3,2,1,0:T(8,128)(2,1)S(1)}, u32[]{:S(2)}, u32[]{:S(2)}) collective-permute-start(bf16[2,2,64,768]{3,2,1,0:T(8,128)(2,1)S(1)} %get-tuple-element.77.refs_2_), channel_id=1, source_target_pairs={{0,16},{8,24},{16,0},{24,8},{1,17},{9,25},{17,1},{25,9},{2,18},{10... | collective-permute-start | bytes 1179656 | tf_op jit(solution)/shard_map/ppermute | solution.py:1294
  25.3 8.8 %collective-permute-start.9 = (bf16[2,2,64,768]{3,2,1,0:T(8,128)(2,1)S(1)}, bf16[2,2,64,768]{3,2,1,0:T(8,128)(2,1)}, u32[]{:S(2)}, u32[]{:S(2)}) collective-permute-start(bf16[2,2,64,768]{3,2,1,0:T(8,128)(2,1)S(1)} %get-tuple-element.77.refs_2_), channel_id=1, source_target_pairs={{0,1},{1,0},{2,3},{3,2},{4,5},{5,4},{6,7},{7,6},{8,9},{9,8},{10,11... | collective-permute-start | bytes 1179656 | tf_op jit(solution)/shard_map/ppermute | solution.py:1291
  28.2 5.9 %copy-start.8 = (bf16[2,2,64,768]{3,2,1,0:T(8,128)(2,1)}, bf16[2,2,64,768]{3,2,1,0:T(8,128)(2,1)S(1)}, u32[]{:S(2)}) copy-start(bf16[2,2,64,768]{3,2,1,0:T(8,128)(2,1)S(1)} %collective-permute-done.refs_1_.refs_3_) | copy-start | bytes 1179652
  33.2 1.0 copy-start.10
  34.1 4.7 %copy-start.9 = (bf16[2,2,64,768]{3,2,1,0:T(8,128)(2,1)S(1)}, bf16[2,2,64,768]{3,2,1,0:T(8,128)(2,1)}, u32[]{:S(2)}) copy-start(bf16[2,2,64,768]{3,2,1,0:T(8,128)(2,1)} %copy-done.8) | copy-start | bytes 1179652
  34.1 4.7 %copy-start.11 = (bf16[2,2,64,768]{3,2,1,0:T(8,128)(2,1)S(1)}, bf16[2,2,64,768]{3,2,1,0:T(8,128)(2,1)}, u32[]{:S(2)}) copy-start(bf16[2,2,64,768]{3,2,1,0:T(8,128)(2,1)} %copy-done.10) | copy-start | bytes 1179652
  34.2 62.1 %all-to-all-start = ((bf16[8,96,1536]{2,1,0:T(8,128)(2,1)}), bf16[8,96,1536]{2,1,0:T(8,128)(2,1)}, u32[]{:S(2)}, u32[]{:S(2)}) async-start(bf16[8,96,1536]{2,1,0:T(8,128)(2,1)} %tie.3), calls=%async_computation | async-start | bytes 4718592 | tf_op jit(solution)/shard_map/all_to_all | solution.py:1344
  38.9 4.8 %copy-start.16 = (bf16[3072]{0:T(1024)(128)(2,1)S(1)}, bf16[3072]{0:T(1024)(128)(2,1)}, u32[]{:S(2)}) copy-start(bf16[3072]{0:T(1024)(128)(2,1)} %refs_3_.4) | copy-start | bytes 18436
  39.0 6.2 %collective-permute-start.6 = (bf16[8,2,64,768]{3,2,1,0:T(8,128)(2,1)S(1)}, bf16[8,2,64,768]{3,2,1,0:T(8,128)(2,1)S(1)}, u32[]{:S(2)}, u32[]{:S(2)}) collective-permute-start(bf16[8,2,64,768]{3,2,1,0:T(8,128)(2,1)S(1)} %stack.46.refs_1_.refs_2_.refs_0_), channel_id=1, source_target_pairs={{0,8},{8,0},{16,24},{24,16},{1,9},{9,1},{17,25},{25,17},{2,10},{10... | collective-permute-start | bytes 4718600 | tf_op jit(solution)/shard_map/ppermute | solution.py:1294
  42.2 11.0 %collective-permute-start.7 = (bf16[2,2,64,768]{3,2,1,0:T(8,128)(2,1)}, bf16[2,2,64,768]{3,2,1,0:T(8,128)(2,1)}, u32[]{:S(2)}, u32[]{:S(2)}) collective-permute-start(bf16[2,2,64,768]{3,2,1,0:T(8,128)(2,1)} %get-tuple-element.78.refs_0_), channel_id=1, source_target_pairs={{0,16},{8,24},{16,0},{24,8},{1,17},{9,25},{17,1},{25,9},{2,18},{10... | collective-permute-start | bytes 1179656 | tf_op jit(solution)/shard_map/ppermute | solution.py:1294
  42.8 18.8 %collective-permute-start.10 = (bf16[2,2,64,768]{3,2,1,0:T(8,128)(2,1)}, bf16[2,2,64,768]{3,2,1,0:T(8,128)(2,1)}, u32[]{:S(2)}, u32[]{:S(2)}) collective-permute-start(bf16[2,2,64,768]{3,2,1,0:T(8,128)(2,1)} %collective-permute-done.9.refs_0_.refs_1_), channel_id=1, source_target_pairs={{0,16},{8,24},{16,0},{24,8},{1,17},{9,25},{17,1},{25,9},{2,18},{10... | collective-permute-start | bytes 1179656 | tf_op jit(solution)/shard_map/ppermute | solution.py:1294
  45.2 6.9 %copy-start.2 = (bf16[8,2,64,768]{3,2,1,0:T(8,128)(2,1)}, bf16[8,2,64,768]{3,2,1,0:T(8,128)(2,1)S(1)}, u32[]{:S(2)}) copy-start(bf16[8,2,64,768]{3,2,1,0:T(8,128)(2,1)S(1)} %collective-permute-done.6.refs_3_.refs_4_.refs_1_) | copy-start | bytes 4718596
  54.4 9.4 %collective-permute-start.8 = (bf16[4,2,64,768]{3,2,1,0:T(8,128)(2,1)S(1)}, bf16[4,2,64,768]{3,2,1,0:T(8,128)(2,1)}, u32[]{:S(2)}, u32[]{:S(2)}) collective-permute-start(bf16[4,2,64,768]{3,2,1,0:T(8,128)(2,1)S(1)} %stack.47.refs_2_.refs_1_), channel_id=1, source_target_pairs={{0,8},{8,0},{16,24},{24,16},{1,9},{9,1},{17,25},{25,17},{2,10},{10... | collective-permute-start | bytes 2359304 | tf_op jit(solution)/shard_map/ppermute | solution.py:1294
  62.8 1.0 copy-start
  62.8 6.1 %collective-permute-start.11 = (bf16[4,2,64,768]{3,2,1,0:T(8,128)(2,1)S(1)}, bf16[4,2,64,768]{3,2,1,0:T(8,128)(2,1)}, u32[]{:S(2)}, u32[]{:S(2)}) collective-permute-start(bf16[4,2,64,768]{3,2,1,0:T(8,128)(2,1)S(1)} %stack.48.refs_1_.refs_2_.refs_4_), channel_id=1, source_target_pairs={{0,8},{8,0},{16,24},{24,16},{1,9},{9,1},{17,25},{25,17},{2,10},{10... | collective-permute-start | bytes 2359304 | tf_op jit(solution)/shard_map/ppermute | solution.py:1294
  63.8 5.1 %copy-start.1 = (bf16[4,2,64,768]{3,2,1,0:T(8,128)(2,1)S(1)}, bf16[4,2,64,768]{3,2,1,0:T(8,128)(2,1)}, u32[]{:S(2)}) copy-start(bf16[4,2,64,768]{3,2,1,0:T(8,128)(2,1)} %copy-done) | copy-start | bytes 2359300
  68.9 5.1 %copy-start.3 = (bf16[8,2,64,768]{3,2,1,0:T(8,128)(2,1)S(1)}, bf16[8,2,64,768]{3,2,1,0:T(8,128)(2,1)}, u32[]{:S(2)}) copy-start(bf16[8,2,64,768]{3,2,1,0:T(8,128)(2,1)} %copy-done.2) | copy-start | bytes 4718596
  112.1 67.6 %all-to-all-start.1 = ((bf16[8,96,1792]{2,1,0:T(8,128)(2,1)}), bf16[8,96,1792]{2,1,0:T(8,128)(2,1)}, u32[]{:S(2)}, u32[]{:S(2)}) async-start(bf16[8,96,1792]{2,1,0:T(8,128)(2,1)} %get-tuple-element.122), calls=%async_computation.1 | async-start | bytes 5505024 | tf_op jit(solution)/shard_map/all_to_all | solution.py:1369
  124.5 47.1 %copy-start.5 = (bf16[256,768]{1,0:T(8,128)(2,1)S(1)}, bf16[256,768]{1,0:T(8,128)(2,1)}, u32[]{:S(2)}) copy-start(bf16[256,768]{1,0:T(8,128)(2,1)} %refs_3_.5) | copy-start | bytes 1179652
  155.0 2.5 %collective-permute-start.12 = (bf16[240,960]{1,0:T(8,128)(2,1)S(1)}, bf16[240,960]{1,0:T(8,128)(2,1)S(1)}, u32[]{:S(2)}, u32[]{:S(2)}) collective-permute-start(bf16[240,960]{1,0:T(8,128)(2,1)S(1)} %get-tuple-element.111), channel_id=1, source_target_pairs={{0,8},{8,0},{16,24},{24,16},{1,9},{9,1},{17,25},{25,17},{2,10},{10... | collective-permute-start | bytes 1382408 | tf_op jit(solution)/shard_map/ppermute | solution.py:1294
  157.8 13.8 %collective-permute-start.13 = (bf16[240,1152]{1,0:T(8,128)(2,1)S(1)}, bf16[240,1152]{1,0:T(8,128)(2,1)S(1)}, u32[]{:S(2)}, u32[]{:S(2)}) collective-permute-start(bf16[240,1152]{1,0:T(8,128)(2,1)S(1)} %merge.1.refs_1_), channel_id=1, source_target_pairs={{0,16},{8,24},{16,0},{24,8},{1,17},{9,25},{17,1},{25,9},{2,18},{10... | collective-permute-start | bytes 1658888 | tf_op jit(solution)/shard_map/ppermute | solution.py:1294
  173.8 3.0 %collective-permute-start.14 = (bf16[224,1536]{1,0:T(8,128)(2,1)S(1)}, bf16[224,1536]{1,0:T(8,128)(2,1)S(1)}, u32[]{:S(2)}, u32[]{:S(2)}) collective-permute-start(bf16[224,1536]{1,0:T(8,128)(2,1)S(1)} %get-tuple-element.114.refs_1_), channel_id=1, source_target_pairs={{0,8},{8,0},{16,24},{24,16},{1,9},{9,1},{17,25},{25,17},{2,10},{10... | collective-permute-start | bytes 2064392 | tf_op jit(solution)/shard_map/ppermute | solution.py:1294
  181.5 5.3 %copy-start.12 = (bf16[96,2048]{1,0:T(8,128)(2,1)S(1)}, bf16[96,2048]{1,0:T(8,128)(2,1)}, u32[]{:S(2)}) copy-start(bf16[96,2048]{1,0:T(8,128)(2,1)} %get-tuple-element.123.refs_1_) | copy-start | bytes 1179652
  181.5 5.2 %collective-permute-start.15 = (bf16[96,2048]{1,0:T(8,128)(2,1)}, bf16[96,2048]{1,0:T(8,128)(2,1)S(1)}, u32[]{:S(2)}, u32[]{:S(2)}) collective-permute-start(bf16[96,2048]{1,0:T(8,128)(2,1)} %get-tuple-element.123.refs_1_), channel_id=1, source_target_pairs={{0,8},{8,0},{16,24},{24,16},{1,9},{9,1},{17,25},{25,17},{2,10},{10... | collective-permute-start | bytes 1179656 | tf_op jit(solution)/shard_map/ppermute | solution.py:1294
